TPU v7x, 512 devices: a whole 4x4x16 slice. The times are simulated.
512 devices in a mesh: layer: 8 (over z_lo, core), feat: 64 (over y, x, z_hi).
Axes of the slice: x: 4, y: 4, z: 16 (z_hi: 4, z_lo: 4; z = z_hi * 4 + z_lo), core: 2. Of those that a mesh axis runs over, the one named last changes fastest.
Arguments:
- acts: bfloat16 [960, 3584], P('feat', 'layer'), may hold values from -48 to 48, as said below
- enc_weight: bfloat16 [3584, 32768], P('layer', 'feat'), may hold values from -0.09375 to 0.09375
- enc_bias: float32 [32768], P('feat'), may hold values from -3 to 3
- dec_weight: bfloat16 [32768, 3584], P('feat', 'layer'), as said below
- dec_bias: float32 [3584], P('layer'), may hold values from -3 to 3
- enc_moment: float32 [3584, 32768], P('layer', 'feat'), may hold values from -0.06 to 0.06
- enc_second: float32 [3584, 32768], P('layer', 'feat'), may hold values from 1e-05 to 0.001
Outputs:
- enc_new: bfloat16 [3584, 32768], P('layer', 'feat')
- moment_new: float32 [3584, 32768], P('layer', 'feat')
- second_new: float32 [3584, 32768], P('layer', 'feat')
- total_loss: float32 [], replicated
Inputs may be any that keep to these rules, and one draw needn't show every extreme that they name: `acts`: activations with token scales and channel scales that vary. `dec_weight`: decoder rows with scales that vary over latents and layers.
All inputs are finite; a program needn't handle non-finite values.
Results may differ from a plain program's by a relative error of at most 0.0051.
Values may be sent and summed in bfloat16 or wider, within the bound.
No kernel may reach another device: no remote copies, remote signals or barrier semaphores. Data moves between devices by JAX's collectives and lax.ppermute only.
A program may use at most 64 MiB of HBM per device.

v0:
```python
import jax
import jax.numpy as jnp
from jax import lax
from jax.sharding import PartitionSpec as P

D = 1792
LAYERS = 2


sparsity = 0.5
beta_one = 0.9
beta_two = 0.999
first_fix = 0.9999734386011124
second_fix = 0.0952078528862911
learn_rate = 0.002
adam_eps = 1e-08
sharpness = 4.0


def transposed(left, right):
    return lax.dot_general(
        left, right, (((1,), (1,)), ((), ())), preferred_element_type=jnp.float32
    )


def body(acts, enc_weight, enc_bias, dec_weight, dec_bias, enc_moment, enc_second):
    local_rows, chan_count = acts.shape
    feat_count = lax.axis_size("feat")
    layer_count = lax.axis_size("layer")
    batch_rows = local_rows * feat_count
    inv_batch = 1.0 / batch_rows
    column_ids = lax.axis_index("layer") * chan_count + jnp.arange(chan_count, dtype=jnp.int32)
    owner_layer = column_ids // D
    selector = (owner_layer[:, None] == jnp.arange(LAYERS, dtype=jnp.int32)[None, :]).astype(
        jnp.float32
    )
    square_part = jnp.dot(
        jnp.square(dec_weight.astype(jnp.float32)), selector, precision=lax.Precision.HIGHEST
    )
    gathered = lax.all_gather(acts, "feat", axis=0, tiled=True)
    partial_value = jnp.dot(gathered, enc_weight, preferred_element_type=jnp.float32)
    summed, squares = lax.psum((partial_value, square_part), "layer")
    preact = summed + enc_bias
    codes = (jax.nn.softplus(sharpness * preact) / sharpness).astype(jnp.bfloat16)
    slopes = jax.nn.sigmoid(sharpness * preact)
    code_sums = jnp.sum(codes.astype(jnp.float32), axis=0)
    bias_row = dec_bias.reshape(1, chan_count)
    rebuilt = lax.psum_scatter(
        jnp.dot(codes, dec_weight, preferred_element_type=jnp.float32),
        "feat",
        scatter_dimension=0,
        tiled=True,
    )
    error = rebuilt + bias_row - acts.astype(jnp.float32)
    error_piece = jnp.sum(error * error)
    grad_rebuilt = (error * (2.0 * inv_batch)).astype(jnp.bfloat16)
    code_part = transposed(lax.all_gather(grad_rebuilt, "feat", axis=0, tiled=True), dec_weight)
    code_sum = lax.psum(code_part, "layer")
    dec_norms = jnp.sum(jnp.sqrt(squares), axis=1)
    code_grad = code_sum + sparsity * inv_batch * dec_norms
    pre_grad = (code_grad * slopes).astype(jnp.bfloat16)
    gradient = lax.dot_general(
        gathered, pre_grad, (((0,), (0,)), ((), ())), preferred_element_type=jnp.float32
    )
    sparse_piece = jnp.sum(code_sums * dec_norms) / layer_count
    total_loss = lax.psum(inv_batch * (error_piece + sparsity * sparse_piece), ("layer", "feat"))
    moment_new = beta_one * enc_moment + (1.0 - beta_one) * gradient
    second_new = beta_two * enc_second + (1.0 - beta_two) * gradient * gradient
    update = moment_new / first_fix / (jnp.sqrt(second_new / second_fix) + adam_eps)
    enc_new = (enc_weight.astype(jnp.float32) - learn_rate * update).astype(jnp.bfloat16)
    return (enc_new, moment_new, second_new, total_loss)


def solution(mesh):
    return jax.shard_map(
        body,
        mesh=mesh,
        in_specs=(
            P("feat", "layer"),
            P("layer", "feat"),
            P("feat"),
            P("feat", "layer"),
            P("layer"),
            P("layer", "feat"),
            P("layer", "feat"),
        ),
        out_specs=(P("layer", "feat"), P("layer", "feat"), P("layer", "feat"), P()),
        check_vma=False,
    )
```

profile of v0, /device:TPU:1, one launch (start us, length us, event | category | flops | bytes accessed | tf_op | source)
XLA Modules:
  0.0 940.2 jit_solution(12819282306030912859)
XLA Ops:
  7.2 0.0 all-reduce.5.cloned.1.call-start
  7.2 207.6 %all-gather = bf16[64,15,448]{2,1,0:T(8,128)(2,1)S(1)} all-gather(bf16[1,15,448]{2,1,0:T(8,128)(2,1)} %bitcast.15), channel_id=1, replica_groups=mesh['layer'=8,'feat'=64] {'feat'}, dimensions={0}, use_global_device_ids=true | all-gather | bytes 873600 | tf_op jit(solution)/shard_map/all_gather | solution.py:40
  214.8 0.5 reshape.27
  215.3 2.0 fusion.15
  217.3 0.0 all-reduce.7.cloned.1.call-start
  217.4 103.2 %all-reduce.5.cloned.1.call-done = f32[960,512]{1,0:T(8,128)} async-done(((f32[960,512]{1,0:T(8,128)}), f32[960,512]{1,0:T(8,128)}) %all-reduce.5.cloned.1.call-update) | async-done | bytes 1966096 | tf_op jit(solution)/shard_map/psum | solution.py:42
  320.6 3.0 convert_reduce_fusion
  323.6 0.7 fusion.16
  324.3 217.5 %fusion = f32[16,448]{1,0:T(8,128)S(1)} fusion(f32[960,448]{1,0:T(8,128)S(1)} %fusion.16), kind=kCustom, calls=%all-reduce-scatter | all-reduce-scatter fusion | flops 458753 | bytes 1751040
  541.8 1.3 collective-permute-start.2
  543.1 3.9 collective-permute-start.1
  547.0 3.4 collective-permute-start
  550.4 1.3 collective-permute-start.3
  551.7 1.3 dynamic-slice.4
  553.7 0.5 concatenate
  554.2 0.6 multiply_reduce_fusion
  554.8 197.6 %all-gather.1 = bf16[64,15,448]{2,1,0:T(8,128)(2,1)S(1)} all-gather(bf16[1,15,448]{2,1,0:T(8,128)(2,1)S(1)} %get-tuple-element.10), channel_id=1, replica_groups=mesh['layer'=8,'feat'=64] {'feat'}, dimensions={0}, use_global_device_ids=true | all-gather | bytes 873600 | tf_op jit(solution)/shard_map/all_gather | solution.py:57
  752.4 0.5 reshape.29
  752.9 2.0 fusion.17
  754.9 0.5 fusion.4
  755.4 72.2 %psum.30 = f32[512,2]{0,1:T(2,128)S(1)} all-reduce(f32[512,2]{0,1:T(2,128)S(1)} %fusion.4), channel_id=1, replica_groups=mesh['layer'=8,'feat'=64] {'layer'}, use_global_device_ids=true, to_apply=%region_3.4 | all-reduce | flops 1024 | bytes 8192 | tf_op jit(solution)/shard_map/psum | solution.py:42
  827.6 0.6 multiply_reduce_fusion.1
  829.5 98.7 %psum.31 = f32[]{:T(128)} all-reduce(f32[]{:T(128)S(6)} %mul_shard_map.7), channel_id=1, replica_groups=mesh['layer'=8,'feat'=64] {'layer','feat'}, use_global_device_ids=true, to_apply=%region_8.9 | all-reduce | flops 1 | bytes 8 | tf_op jit(solution)/shard_map/psum | solution.py:66
  928.2 5.1 subtract_convert_fusion
  (22 shorter events, 0.1 us)
Async XLA Ops:
  7.2 208.2 %copy-start.2 = (bf16[448,512]{1,0:T(8,128)(2,1)S(1)}, bf16[448,512]{1,0:T(8,128)(2,1)}, u32[]{:S(2)}) copy-start(bf16[448,512]{1,0:T(8,128)(2,1)} %param.8) | copy-start | bytes 1376260
  7.2 313.4 %all-reduce.5.cloned.1.call-start = ((), (), s32[]{:S(2)}) async-start(), calls=%async_computation | async-start | bytes 3932160 | tf_op jit(solution)/shard_map/psum | solution.py:42
  215.3 105.3 %copy-start.5 = (f32[512]{0:T(512)S(1)}, f32[512]{0:T(512)}, u32[]{:S(2)}) copy-start(f32[512]{0:T(512)} %param.9) | copy-start | bytes 6148
  217.3 106.3 %copy-start.1 = (bf16[512,448]{0,1:T(8,128)(2,1)S(1)}, bf16[512,448]{0,1:T(8,128)(2,1)}, u32[]{:S(2)}) copy-start(bf16[512,448]{0,1:T(8,128)(2,1)} %param.10) | copy-start | bytes 1376260
  217.3 710.9 %all-reduce.7.cloned.1.call-start = ((), (), s32[]{:S(2)}) async-start(), calls=%async_computation.1 | async-start | bytes 3932160 | tf_op jit(solution)/shard_map/psum | solution.py:58
  324.3 229.9 %copy-start.3 = (bf16[15,448]{1,0:T(8,128)(2,1)S(1)}, bf16[15,448]{1,0:T(8,128)(2,1)}, u32[]{:S(2)}) copy-start(bf16[15,448]{1,0:T(8,128)(2,1)} %param.7) | copy-start | bytes 40324
  324.3 229.9 %copy-start.4 = (f32[448]{0:T(512)S(1)}, f32[448]{0:T(512)}, u32[]{:S(2)}) copy-start(f32[448]{0:T(512)} %param.11) | copy-start | bytes 5380
  541.8 11.8 %collective-permute-start.2 = (f32[16,448]{1,0:T(8,128)S(1)}, f32[16,448]{1,0:T(8,128)S(1)}, u32[]{:S(2)}, u32[]{:S(2)}) collective-permute-start(f32[16,448]{1,0:T(8,128)S(1)} %fusion), channel_id=1, source_target_pairs={{0,3},{1,4},{2,5},{3,6},{4,7},{5,8},{6,9},{7,10},{8,11},{9,12},{10... | collective-permute-start | bytes 86024
  543.1 10.6 %collective-permute-start.1 = (f32[16,448]{1,0:T(8,128)S(1)}, f32[16,448]{1,0:T(8,128)S(1)}, u32[]{:S(2)}, u32[]{:S(2)}) collective-permute-start(f32[16,448]{1,0:T(8,128)S(1)} %fusion), channel_id=1, source_target_pairs={{0,2},{1,3},{2,4},{3,5},{4,6},{5,7},{6,8},{7,9},{8,10},{9,11},{10,... | collective-permute-start | bytes 86024
  547.0 6.7 collective-permute-start
  550.4 3.2 collective-permute-start.3
  754.9 173.3 %copy-start = (f32[960,512]{1,0:T(8,128)S(1)}, f32[960,512]{1,0:T(8,128)}, u32[]{:S(2)}) copy-start(f32[960,512]{1,0:T(8,128)} %all-reduce.5.cloned.1.call-done) | copy-start | bytes 5898244
Sparse Core Ops, SparseCore 0:
  217.4 103.1 all-reduce.4
  755.0 135.5 all-reduce.6
where the time goes:
time: 941 us; the launch traced here: 940 us
  blocking collectives  793 us (84%)
  waiting for transfers between devices  103 us (11%)
  between operations  16.2 us (2%)
  matrix products  10.2 us (1%)
  starting transfers between devices  9.94 us (1%)
    unnamed x1, blocking collectives  217 us
    all_gather x1, blocking collectives, body(): gathered = lax.all_gather(acts, 'feat', axis=0, tiled=True)  208 us
    all_gather x1, blocking collectives, body(): lax.all_gather(grad_rebuilt, 'feat', axis=0, tiled=True)  198 us
    psum x1, waiting for transfers between devices, body(): summed, squares = lax.psum((partial_value, square_part), 'layer')  103 us
    psum x1, blocking collectives, body(): lax.psum(inv_batch * (error_piece + sparsity * sparse_piece), ('layer', '...  98.7 us
    psum x1, blocking collectives, body(): summed, squares = lax.psum((partial_value, square_part), 'layer')  72.2 us
  transfers between devices with their start and end apart: 6, of which 1 were waited for; matrix products, arithmetic and copies ran while one was open for 0% of the time, Pallas kernels for 0%

commit v1 on v0

v1 whole, which is shorter than its diff:
```python
import jax
import jax.numpy as jnp
from jax import lax
from jax.sharding import Mesh, PartitionSpec as P

D = 1792
LAYERS = 2

sparsity = 0.5
beta_one = 0.9
beta_two = 0.999
first_fix = 0.9999734386011124
second_fix = 0.0952078528862911
learn_rate = 0.002
adam_eps = 1e-08
sharpness = 4.0

SIZES = (4, 2, 4, 4, 4)
NAMES = ("zl", "core", "y", "x", "zh")
LAYER = ("zl", "core")
FEAT = ("y", "x", "zh")
PLANE = ("y", "x")
PARTS = 8
BLOCKS = 16
HIGH = 4
BF = jnp.bfloat16
F32 = jnp.float32


def pieces(value):
    top = value.astype(BF)
    rest = value - top.astype(F32)
    mid = rest.astype(BF)
    low = (rest - mid.astype(F32)).astype(BF)
    return top, mid, low


def body(acts, enc_weight, enc_bias, dec_weight, dec_bias, enc_moment, enc_second):
    rows, chans = acts.shape
    latents = enc_weight.shape[1]
    inv_batch = 1.0 / (rows * BLOCKS * HIGH)
    wide = PARTS * chans
    part = lax.axis_index(LAYER)
    padded = rows + 1
    share = padded // PARTS

    enc_all = lax.all_gather(enc_weight, LAYER, axis=0, tiled=True)
    dec_all = lax.all_gather(dec_weight, LAYER, axis=0)

    bias_rows = jnp.stack(pieces(dec_bias))
    packed = jnp.concatenate([acts, jnp.zeros((1, chans), BF), bias_rows], axis=0)
    column = lax.all_gather(packed, ("zh",) + LAYER, axis=0)
    column = column.reshape(HIGH, PARTS, padded + 3, chans)
    bias_full = column[0, :, padded:].astype(F32).sum(axis=1).reshape(1, wide)
    mine = lax.dynamic_slice_in_dim(column[:, :, :padded], part * share, share, axis=2)
    mine = mine.transpose(0, 2, 1, 3).reshape(HIGH * share, wide)
    own = lax.dynamic_slice_in_dim(column[:, :, :padded], part, 1, axis=1)
    own = own.reshape(HIGH, PARTS, share, chans).transpose(1, 0, 2, 3)
    own = own.reshape(PARTS * HIGH * share, chans)

    small = HIGH * share
    tokens = BLOCKS * small
    acts_part = lax.all_gather(mine, PLANE, axis=0, tiled=True)

    preact = jnp.dot(acts_part, enc_all, preferred_element_type=F32) + enc_bias
    codes = (jax.nn.softplus(sharpness * preact) / sharpness).astype(BF)
    slopes = jax.nn.sigmoid(sharpness * preact)

    squares = jnp.sum(jnp.square(dec_all.astype(F32)), axis=2)
    per_layer = squares.reshape(LAYERS, PARTS // LAYERS, latents).sum(axis=1)
    dec_norms = jnp.sum(jnp.sqrt(per_layer), axis=0)

    sparse = jnp.sum(codes.astype(F32) * dec_norms, axis=1, keepdims=True)
    partial_value = jnp.einsum("bf,lfc->blc", codes, dec_all, preferred_element_type=F32)
    tail = jnp.zeros((tokens, 125), BF)
    sending = jnp.concatenate(
        [partial_value.reshape(tokens, wide).astype(BF), *pieces(sparse), tail], axis=1
    )
    got = lax.all_to_all(
        sending.reshape(BLOCKS, small, wide + 128), PLANE, 0, 0, tiled=True
    )
    summed = jnp.sum(got.astype(F32), axis=0)
    top = summed.astype(BF)
    again = lax.all_gather(top, "zh", axis=0)
    total = jnp.sum(again.astype(F32), axis=0)

    slots = part * share + jnp.arange(small, dtype=jnp.int32) % share
    real = (slots < rows).astype(F32)[:, None]
    error = total[:, :wide] + bias_full - mine.astype(F32)
    sparse_sum = jnp.sum(total[:, wide:], axis=1, keepdims=True)
    token_loss = real * inv_batch * (
        jnp.sum(error * error, axis=1, keepdims=True) + sparsity * sparse_sum
    )
    grad = (error * (2.0 * inv_batch)).astype(BF)
    grad_send = jnp.concatenate([grad, *pieces(token_loss), jnp.zeros((small, 125), BF)], axis=1)
    grad_got = lax.all_gather(grad_send, PLANE, axis=0, tiled=True)
    part_loss = jnp.sum(grad_got[:, wide:].astype(F32))
    grad_all = grad_got[:, :wide].reshape(tokens, PARTS, chans)
    code_grad = jnp.einsum("blc,lfc->bf", grad_all, dec_all, preferred_element_type=F32)
    code_grad = code_grad + sparsity * inv_batch * dec_norms
    pre_grad = (code_grad * slopes).astype(BF)

    loss_rows = jnp.broadcast_to(jnp.stack(pieces(part_loss))[:, None], (3, latents))
    last = jnp.concatenate([pre_grad, loss_rows, jnp.zeros((5, latents), BF)], axis=0)
    last_got = lax.all_gather(last, LAYER, axis=0)
    total_loss = jnp.sum(last_got[:, tokens : tokens + 3, 0].astype(F32))
    pre_all = last_got[:, :tokens]

    own_all = lax.all_gather(own, PLANE, axis=0)
    own_all = own_all.reshape(BLOCKS, PARTS, small, chans).transpose(1, 0, 2, 3)
    gradient = jnp.einsum(
        "lbc,lbf->cf",
        own_all.reshape(PARTS, tokens, chans),
        pre_all,
        preferred_element_type=F32,
    )
    moment_new = beta_one * enc_moment + (1.0 - beta_one) * gradient
    second_new = beta_two * enc_second + (1.0 - beta_two) * gradient * gradient
    update = moment_new / first_fix / (jnp.sqrt(second_new / second_fix) + adam_eps)
    enc_new = (enc_weight.astype(F32) - learn_rate * update).astype(BF)
    return (enc_new, moment_new, second_new, total_loss)


def solution(mesh):
    fine = Mesh(mesh.devices.reshape(SIZES), NAMES)
    return jax.shard_map(
        body,
        mesh=fine,
        in_specs=(
            P(FEAT, LAYER),
            P(LAYER, FEAT),
            P(FEAT),
            P(FEAT, LAYER),
            P(LAYER),
            P(LAYER, FEAT),
            P(LAYER, FEAT),
        ),
        out_specs=(P(LAYER, FEAT), P(LAYER, FEAT), P(LAYER, FEAT), P()),
        check_vma=False,
    )
```

time: 941 us -> 259 us (0.28)
  blocking collectives: 793 us -> 125 us
  waiting for transfers between devices: 103 us -> 82.9 us
    all_gather x2 -> x5, blocking collectives: 405 us -> 125 us  [the longest x1 40.4 us: body(): column = lax.all_gather(packed, ('zh',) + LAYER, axis=0)]
    unnamed x1 -> x0, blocking collectives: 217 us -> none
    psum x2 -> x0, blocking collectives: 171 us -> none  [the longest x1 98.7 us: body(): lax.psum(inv_batch * (error_piece + sparsity * sparse_piece), ('layer', '...]
    psum x2 -> x0, waiting for transfers between devices: 103 us -> none  [the longest x1 103 us: body(): summed, squares = lax.psum((partial_value, square_part), 'layer')]
    all_gather x0 -> x3, waiting for transfers between devices: none -> 68.7 us  [the longest x1 46.8 us: body(): enc_all = lax.all_gather(enc_weight, LAYER, axis=0, tiled=True)]
    all_to_all x0 -> x1, waiting for transfers between devices: none -> 12.7 us  [body(): lax.all_to_all(sending.reshape(BLOCKS, small, wide + 128), PLANE, 0, 0, t...]
    unnamed x4 -> x0, starting transfers between devices: 9.86 us -> none
  transfers between devices with their start and end apart: 6 -> 4, of which waited for: 1 -> 3; matrix products, arithmetic and copies ran while one was open for 0% -> 3% of each run, Pallas kernels for 0% -> 0%
where the time goes in v1:
time: 259 us; the launch traced here: 257 us
  blocking collectives  125 us (48%)
  waiting for transfers between devices  82.9 us (32%)
  between operations  15.3 us (6%)
  matrix products  12 us (5%)
  local copies, waits for them, and re-layouts  10.2 us (4%)
  starting transfers between devices  6.64 us (3%)
  other arithmetic  5.17 us (2%)
    all_gather x1, waiting for transfers between devices, body(): enc_all = lax.all_gather(enc_weight, LAYER, axis=0, tiled=True)  46.8 us
    all_gather x1, blocking collectives, body(): column = lax.all_gather(packed, ('zh',) + LAYER, axis=0)  40.4 us
    all_gather x1, blocking collectives, body(): again = lax.all_gather(top, 'zh', axis=0)  23.4 us
    all_gather x1, blocking collectives, body(): acts_part = lax.all_gather(mine, PLANE, axis=0, tiled=True)  22.2 us
    all_gather x1, waiting for transfers between devices, body(): last_got = lax.all_gather(last, LAYER, axis=0)  21.9 us
    all_gather x1, blocking collectives, body(): own_all = lax.all_gather(own, PLANE, axis=0)  20.1 us
    all_gather x1, blocking collectives, body(): grad_got = lax.all_gather(grad_send, PLANE, axis=0, tiled=True)  19 us
    all_to_all x1, waiting for transfers between devices, body(): lax.all_to_all(sending.reshape(BLOCKS, small, wide + 128), PLANE, 0, 0, t...  12.7 us
  transfers between devices with their start and end apart: 4, of which 3 were waited for; matrix products, arithmetic and copies ran while one was open for 3% of the time, Pallas kernels for 0%

profile of v1, /device:TPU:1, one launch (start us, length us, event | category | flops | bytes accessed | tf_op | source)
XLA Modules:
  0.0 257.3 jit_solution(15311085068732921085)
XLA Ops:
  7.2 0.7 all-gather.11.cloned.1.call-update
  7.9 0.7 all-gather.9.cloned.1.call-update
  8.7 0.8 subtract_convert_fusion.3
  9.5 0.8 concatenate.13
  10.2 40.4 %all-gather.4 = bf16[32,19,448]{2,1,0:T(8,128)(2,1)S(1)} all-gather(bf16[1,19,448]{2,1,0:T(8,128)(2,1)S(1)} %bitcast.76), channel_id=2, replica_groups=mesh['zl'=4,'core'=2,'y'=4,'x'=4,'zh'=4] {'zh','zl','core'}, dimensions={0}, use_global_device_ids=true | all-gather | bytes 561792 | tf_op jit(solution)/shard_map/all_gather | solution.py:52
  51.0 22.2 %all_gather.39 = bf16[128,3584]{1,0:T(8,128)(2,1)S(1)} all-gather(bf16[8,3584]{1,0:T(8,128)(2,1)S(1)} %reshape.208), channel_id=1, replica_groups=mesh['zl'=4,'core'=2,'y'=4,'x'=4,'zh'=4] {'y','x'}, dimensions={0}, use_global_device_ids=true | all-gather | bytes 974848 | tf_op jit(solution)/shard_map/all_gather | solution.py:63
  73.2 4.0 %copy.79 = bf16[56,8,8,512]{3,2,1,0:T(8,128)(2,1)S(1)} copy(bf16[56,8,8,512]{3,1,2,0:T(8,128)(2,1)} %bitcast.68) | data formatting | bytes 7340032
  77.2 1.1 multiply_reduce_fusion
  78.3 46.8 %all-gather.9.cloned.1.call-done = bf16[3584,512]{1,0:T(8,128)(2,1)} async-done(((bf16[448,512]{1,0:T(8,128)(2,1)}), bf16[3584,512]{1,0:T(8,128)(2,1)}) %all-gather.9.cloned.1.call-update) | async-done | bytes 3670032 | tf_op jit(solution)/shard_map/all_gather | solution.py:47
  125.2 3.7 %multiply_reduce_fusion.1 = (f32[128]{0:T(128)S(1)}, bf16[128,512]{1,0:T(8,128)(2,1)S(1)}, f32[128,512]{1,0:T(8,128)}) fusion(f32[512]{0:T(512)S(1)} %sqrt_reduce_fusion, f32[512]{0:T(512)S(1)} %copy-done.3, bf16[128,3584]{1,0:T(8,128)(2,1)S(1)} %all_gather.39, bf16[3584,512]{1,0:T(8,128)(2,1)} %all-gather.9.cloned.1.call-done), kind=kOutput, calls=%fused_computation.26 | convolution fusion | flops 470613888 | bytes 4985344 | tf_op jit(solution)/shard_map/dot_general | solution.py:65
  128.9 1.1 fusion.6
  130.0 1.0 copy.63
  131.1 1.2 convert_element_type.240
  132.9 1.1 concatenate.14
  134.0 6.5 %all-to-all-start = ((bf16[16,8,3712]{2,1,0:T(8,128)(2,1)}), bf16[16,8,3712]{2,1,0:T(8,128)(2,1)S(1)}, u32[]{:S(2)}, u32[]{:S(2)}) async-start(bf16[16,8,3712]{2,1,0:T(8,128)(2,1)} %concatenate.14), calls=%async_computation | async-start | bytes 1900544 | tf_op jit(solution)/shard_map/all_to_all | solution.py:79
  140.8 12.7 %all-to-all-done = bf16[16,8,3712]{2,1,0:T(8,128)(2,1)S(1)} async-done(((bf16[16,8,3712]{2,1,0:T(8,128)(2,1)}), bf16[16,8,3712]{2,1,0:T(8,128)(2,1)S(1)}, u32[]{:S(2)}, u32[]{:S(2)}) %all-to-all-start) | async-done | bytes 950304 | tf_op jit(solution)/shard_map/all_to_all | solution.py:79
  153.7 23.4 %all-gather.2 = bf16[32,3712]{1,0:T(8,128)(2,1)S(1)} all-gather(bf16[8,3712]{1,0:T(8,128)(2,1)S(1)} %reduce_sum.109), channel_id=4, replica_groups=mesh['zl'=4,'core'=2,'y'=4,'x'=4,'zh'=4] {'zh'}, dimensions={0}, use_global_device_ids=true | all-gather | bytes 296960 | tf_op jit(solution)/shard_map/all_gather | solution.py:84
  177.6 19.0 %all_gather.45 = bf16[128,3712]{1,0:T(8,128)(2,1)S(1)} all-gather(bf16[8,3712]{1,0:T(8,128)(2,1)S(1)} %concatenate.15), channel_id=1, replica_groups=mesh['zl'=4,'core'=2,'y'=4,'x'=4,'zh'=4] {'y','x'}, dimensions={0}, use_global_device_ids=true | all-gather | bytes 1009664 | tf_op jit(solution)/shard_map/all_gather | solution.py:96
  199.3 2.8 %fusion.19 = bf16[128,512]{1,0:T(8,128)(2,1)S(1)} fusion(bf16[128,8,448]{0,2,1:T(8,128)(2,1)S(1)} %bitcast.73, bf16[56,8,8,512]{3,2,1,0:T(8,128)(2,1)} %bitcast.69, f32[128,512]{1,0:T(8,128)S(1)} %copy-done.2, f32[512]{0:T(512)S(1)} %broadcast_multiply_fusion), kind=kOutput, calls=%fused_computation.15 | convolution fusion | flops 470155264 | bytes 4982784 | tf_op jit(solution)/shard_map/blc,lfc->bf/dot_general | solution.py:99
  202.1 0.8 maximum_maximum_fusion
  203.1 20.1 %all_gather.38 = bf16[16,64,448]{2,1,0:T(8,128)(2,1)S(1)} all-gather(bf16[1,64,448]{2,1,0:T(8,128)(2,1)S(1)} %all_gather_reshape.3), channel_id=1, replica_groups=mesh['zl'=4,'core'=2,'y'=4,'x'=4,'zh'=4] {'y','x'}, dimensions={0}, use_global_device_ids=true | all-gather | bytes 974848 | tf_op jit(solution)/shard_map/all_gather | solution.py:109
  223.2 21.9 %all-gather.13.cloned.1.call-done = bf16[1088,512]{1,0:T(8,128)(2,1)} async-done(((bf16[136,512]{1,0:T(8,128)(2,1)}), bf16[1088,512]{1,0:T(8,128)(2,1)}) %all-gather.13.cloned.1.call-update) | async-done | bytes 1114128 | tf_op jit(solution)/shard_map/all_gather | solution.py:105
  245.1 1.3 convert_reduce_fusion.3
  246.4 4.4 %subtract_convert_fusion = (bf16[448,512]{1,0:T(8,128)(2,1)}, f32[448,512]{1,0:T(8,128)}, f32[448,512]{1,0:T(8,128)}) fusion(bf16[448,512]{1,0:T(8,128)(2,1)S(1)} %copy-done.1, f32[448,512]{1,0:T(8,128)} %param.12, f32[448,512]{1,0:T(8,128)} %param.13, bf16[8,136,512]{2,1,0:T(8,128)(2,1)} %bitcast.78, bf16[16,64,448]{2,1,0:T(8,128)(2,1)S(1)} %all_gather.38), kind=kOutput, calls=%fused_computation.20 | convolution fusion | flops 473202688 | bytes 6553600 | tf_op jit(solution)/shard_map/lbc,lbf->cf/dot_general | solution.py:111
  (53 shorter events, 3.5 us)
Async XLA Ops:
  7.2 66.0 %all-gather.11.cloned.1.call-start = ((), (), s32[]{:S(2)}) async-start(), calls=%async_computation.2 | async-start | bytes 4128768 | tf_op jit(solution)/shard_map/all_gather | solution.py:48
  7.9 117.3 %all-gather.9.cloned.1.call-start = ((), (), s32[]{:S(2)}) async-start(), calls=%async_computation.1 | async-start | bytes 4128768 | tf_op jit(solution)/shard_map/all_gather | solution.py:47
  77.2 48.0 %copy-start.3 = (f32[512]{0:T(512)S(1)}, f32[512]{0:T(512)}, u32[]{:S(2)}) copy-start(f32[512]{0:T(512)} %param.9) | copy-start | bytes 6148
  125.2 3.7 %copy-start = (bf16[4096,448]{0,1:T(8,128)(2,1)S(1)}, bf16[4096,448]{0,1:T(8,128)(2,1)}, u32[]{:S(2)}) copy-start(bf16[4096,448]{0,1:T(8,128)(2,1)} %all-gather.11.cloned.1.call-done) | copy-start | bytes 11010052
  134.0 19.6 %all-to-all-start = ((bf16[16,8,3712]{2,1,0:T(8,128)(2,1)}), bf16[16,8,3712]{2,1,0:T(8,128)(2,1)S(1)}, u32[]{:S(2)}, u32[]{:S(2)}) async-start(bf16[16,8,3712]{2,1,0:T(8,128)(2,1)} %concatenate.14), calls=%async_computation | async-start | bytes 1900544 | tf_op jit(solution)/shard_map/all_to_all | solution.py:79
  140.5 58.8 %copy-start.2 = (f32[128,512]{1,0:T(8,128)S(1)}, f32[128,512]{1,0:T(8,128)}, u32[]{:S(2)}) copy-start(f32[128,512]{1,0:T(8,128)} %get-tuple-element.20) | copy-start | bytes 786436
  140.5 104.5 %all-gather.13.cloned.1.call-start = ((), (), s32[]{:S(2)}) async-start(), calls=%async_computation.3 | async-start | bytes 1253376 | tf_op jit(solution)/shard_map/all_gather | solution.py:105
  199.3 47.1 %copy-start.1 = (bf16[448,512]{1,0:T(8,128)(2,1)S(1)}, bf16[448,512]{1,0:T(8,128)(2,1)}, u32[]{:S(2)}) copy-start(bf16[448,512]{1,0:T(8,128)(2,1)} %param.8) | copy-start | bytes 1376260
Sparse Core Ops, SparseCore 0:
  10.1 59.4 all-gather.10
  71.7 53.4 all-gather.8
  203.0 42.0 all-gather.12

commit v2 on v1

v2 whole, which is shorter than its diff:
```python
import jax
import jax.numpy as jnp
from jax import lax
from jax.sharding import Mesh, PartitionSpec as P

D = 1792
LAYERS = 2

sparsity = 0.5
beta_one = 0.9
beta_two = 0.999
first_fix = 0.9999734386011124
second_fix = 0.0952078528862911
learn_rate = 0.002
adam_eps = 1e-08
sharpness = 4.0

SIZES = (4, 2, 4, 4, 4)
NAMES = ("zl", "core", "y", "x", "zh")
LAYER = ("zl", "core")
FEAT = ("y", "x", "zh")
PLANE = ("y", "x")
CORES = 2
CHIPS = 4
PARTS = 8
BLOCKS = 16
HIGH = 4
LANES = 128
BF = jnp.bfloat16
F32 = jnp.float32


def pieces(value):
    top = value.astype(BF)
    rest = value - top.astype(F32)
    mid = rest.astype(BF)
    low = (rest - mid.astype(F32)).astype(BF)
    return top, mid, low


def spread(value, axes, count):
    copies = jnp.broadcast_to(value[None], (count,) + value.shape)
    return lax.all_to_all(copies, axes, 0, 0, tiled=True)


def swap(value):
    return lax.ppermute(value, "core", [(0, 1), (1, 0)])


def beside(value, number):
    rows = value.shape[0]
    lane = lax.broadcasted_iota(jnp.int32, (rows, LANES), 1)
    row = lax.broadcasted_iota(jnp.int32, (rows, LANES), 0)
    top, mid, low = pieces(number)
    zero = jnp.zeros((), BF)
    block = jnp.where(lane == 0, top, jnp.where(lane == 1, mid, jnp.where(lane == 2, low, zero)))
    return jnp.concatenate([value, jnp.where(row == 0, block, zero)], axis=1)


def body(acts, enc_weight, enc_bias, dec_weight, dec_bias, enc_moment, enc_second):
    rows, chans = acts.shape
    latents = enc_weight.shape[1]
    inv_batch = 1.0 / (rows * BLOCKS * HIGH)
    wide = PARTS * chans
    core = lax.axis_index("core")
    part = lax.axis_index(LAYER)
    padded = rows + 1
    share = padded // PARTS
    small = HIGH * share
    tokens = BLOCKS * small

    dec_all = lax.all_gather(dec_weight.T, LAYER, axis=0, tiled=True)

    packed = jnp.concatenate([acts, jnp.zeros((1, chans), BF)], axis=0)
    column = spread(packed, "zh", HIGH)
    column = column.reshape(HIGH, CHIPS, CORES, share, chans).transpose(2, 1, 0, 3, 4)
    column = column.reshape(PARTS, small, chans)
    gathered = spread(column, PLANE, BLOCKS).transpose(1, 0, 2, 3)
    gathered = gathered.reshape(CORES, CHIPS * tokens, chans)
    acts_here = lax.dynamic_index_in_dim(gathered, core, 0, keepdims=False)
    acts_there = lax.dynamic_index_in_dim(gathered, 1 - core, 0, keepdims=False)

    bias_rows = jnp.concatenate(
        [jnp.stack(pieces(dec_bias)), jnp.zeros((small - 3, chans), BF)], axis=0
    )
    by_part = column.reshape(CORES, CHIPS, small, chans).transpose(1, 0, 2, 3)
    by_part = by_part.reshape(PARTS, small, chans)
    small_send = jnp.concatenate(
        [by_part, jnp.broadcast_to(bias_rows[None], by_part.shape)], axis=1
    )
    small_got = lax.all_to_all(small_send, LAYER, 0, 0, tiled=True)
    mine = small_got[:, :small].transpose(1, 0, 2).reshape(small, wide).astype(F32)
    bias_full = small_got[:, small:].astype(F32).sum(axis=1).reshape(1, wide)

    sent = swap(jnp.dot(acts_there, enc_weight, preferred_element_type=F32))
    pair = jnp.dot(acts_here, enc_weight, preferred_element_type=F32) + sent
    quarter = lax.all_to_all(
        pair.astype(BF).reshape(CHIPS, tokens, latents), "zl", 0, 0, tiled=True
    )
    preact = jnp.sum(quarter.astype(F32), axis=0) + enc_bias
    codes = (jax.nn.softplus(sharpness * preact) / sharpness).astype(BF)
    slopes = jax.nn.sigmoid(sharpness * preact)

    squares = jnp.square(dec_all.astype(F32)).reshape(LAYERS, wide // LAYERS, latents)
    dec_norms = jnp.sum(jnp.sqrt(jnp.sum(squares, axis=1)), axis=0)

    def real(count):
        place = lax.broadcasted_iota(jnp.int32, (count, 1), 0) % share
        return (part * share + place < rows).astype(F32)

    sparse = jnp.sum(real(tokens) * codes.astype(F32) * dec_norms)
    partial_value = lax.dot_general(
        codes, dec_all, (((1,), (1,)), ((), ())), preferred_element_type=F32
    )
    got = lax.all_to_all(
        partial_value.astype(BF).reshape(BLOCKS, small, wide), PLANE, 0, 0, tiled=True
    )
    summed = jnp.sum(got.astype(F32), axis=0).astype(BF)
    total = jnp.sum(spread(beside(summed, sparse), "zh", HIGH).astype(F32), axis=0)

    error = total[:, :wide] + bias_full - mine
    piece = jnp.sum(real(small) * error * error) + sparsity * jnp.sum(total[:, wide:])
    grad = (error * (2.0 * inv_batch)).astype(BF)
    grad_got = spread(beside(grad, inv_batch * piece), PLANE, BLOCKS)
    grad_got = grad_got.reshape(tokens, wide + LANES)
    part_loss = jnp.sum(grad_got[:, wide:].astype(F32))
    code_grad = jnp.dot(grad_got[:, :wide], dec_all, preferred_element_type=F32)
    code_grad = code_grad + sparsity * inv_batch * dec_norms
    pre_grad = (code_grad * slopes).astype(BF)

    loss_rows = jnp.broadcast_to(jnp.stack(pieces(part_loss))[:, None], (3, latents))
    last = jnp.concatenate([pre_grad, loss_rows, jnp.zeros((5, latents), BF)], axis=0)
    pre_here = lax.all_gather(last, "zl", axis=0)
    pre_there = swap(pre_here)

    def part_of(acts_half, pre_half):
        return lax.dot_general(
            acts_half,
            pre_half[:, :tokens].reshape(CHIPS * tokens, latents),
            (((0,), (0,)), ((), ())),
            preferred_element_type=F32,
        )

    near, far = pre_here[:, tokens:, 0].astype(F32), pre_there[:, tokens:, 0].astype(F32)
    first, second = jnp.where(core == 0, near, far), jnp.where(core == 0, far, near)
    total_loss = jnp.sum(jnp.concatenate([first, second]))
    gradient = part_of(acts_here, pre_here) + part_of(acts_there, pre_there)
    moment_new = beta_one * enc_moment + (1.0 - beta_one) * gradient
    second_new = beta_two * enc_second + (1.0 - beta_two) * gradient * gradient
    update = moment_new / first_fix / (jnp.sqrt(second_new / second_fix) + adam_eps)
    enc_new = (enc_weight.astype(F32) - learn_rate * update).astype(BF)
    return (enc_new, moment_new, second_new, total_loss)


def solution(mesh):
    fine = Mesh(mesh.devices.reshape(SIZES), NAMES)
    return jax.shard_map(
        body,
        mesh=fine,
        in_specs=(
            P(FEAT, LAYER),
            P(LAYER, FEAT),
            P(FEAT),
            P(FEAT, LAYER),
            P(LAYER),
            P(LAYER, FEAT),
            P(LAYER, FEAT),
        ),
        out_specs=(P(LAYER, FEAT), P(LAYER, FEAT), P(LAYER, FEAT), P()),
        check_vma=False,
    )
```

time: 259 us -> 219 us (0.85)
  blocking collectives: 125 us -> 42.3 us
  starting transfers between devices: 6.64 us -> 42.8 us
  other arithmetic: 5.17 us -> 15.1 us
  between operations: 15.3 us -> 20.7 us
  waiting for transfers between devices: 82.9 us -> 78.1 us
  local copies, waits for them, and re-layouts: 10.2 us -> 5.43 us
    all_gather x5 -> x1, blocking collectives: 125 us -> 14.3 us  [body(): pre_here = lax.all_gather(last, 'zl', axis=0)]
    all_gather x3 -> x1, waiting for transfers between devices: 68.7 us -> 0.02 us  [body(): dec_all = lax.all_gather(dec_weight.T, LAYER, axis=0, tiled=True)]
    all_to_all x1 -> x6, waiting for transfers between devices: 12.7 us -> 73.7 us  [the longest x3 41.9 us: spread(): return lax.all_to_all(copies, axes, 0, 0, tiled=True)]
    all_to_all x0 -> x1, blocking collectives: none -> 27.9 us  [spread(): return lax.all_to_all(copies, axes, 0, 0, tiled=True)]
    all_to_all x1 -> x6, starting transfers between devices: 6.52 us -> 29.2 us  [the longest x3 16.2 us: spread(): return lax.all_to_all(copies, axes, 0, 0, tiled=True)]
    ppermute x0 -> x2, starting transfers between devices: none -> 13.6 us  [swap(): return lax.ppermute(value, 'core', [(0, 1), (1, 0)])]
    square x0 -> x1, other arithmetic: none -> 6.06 us  [body(): jnp.square(dec_all.astype(F32)).reshape(LAYERS, wide // LAYERS, latents)]
    unnamed x10 -> x6, local copies, waits for them, and re-layouts: 4.01 us -> 0.01 us
  transfers between devices with their start and end apart: 4 -> 9, of which waited for: 3 -> 8; matrix products, arithmetic and copies ran while one was open for 3% -> 3% of each run, Pallas kernels for 0% -> 0%
where the time goes in v2:
time: 219 us; the launch traced here: 218 us
  waiting for transfers between devices  78.1 us (36%)
  starting transfers between devices  42.8 us (20%)
  blocking collectives  42.3 us (19%)
  between operations  20.7 us (9%)
  other arithmetic  15.1 us (7%)
  matrix products  13.9 us (6%)
  local copies, waits for them, and re-layouts  5.43 us (2%)
    all_to_all x3, waiting for transfers between devices, spread(): return lax.all_to_all(copies, axes, 0, 0, tiled=True)  41.9 us
    all_to_all x1, blocking collectives, spread(): return lax.all_to_all(copies, axes, 0, 0, tiled=True)  27.9 us
    all_to_all x3, starting transfers between devices, spread(): return lax.all_to_all(copies, axes, 0, 0, tiled=True)  16.2 us
    all_gather x1, blocking collectives, body(): pre_here = lax.all_gather(last, 'zl', axis=0)  14.3 us
    all_to_all x1, waiting for transfers between devices, body(): lax.all_to_all(pair.astype(BF).reshape(CHIPS, tokens, latents), 'zl', 0,...  14 us
    ppermute x2, starting transfers between devices, swap(): return lax.ppermute(value, 'core', [(0, 1), (1, 0)])  13.6 us
    all_to_all x1, waiting for transfers between devices, body(): lax.all_to_all(partial_value.astype(BF).reshape(BLOCKS, small, wide), PLA...  12 us
    square x1, other arithmetic, body(): jnp.square(dec_all.astype(F32)).reshape(LAYERS, wide // LAYERS, latents)  6.06 us
  transfers between devices with their start and end apart: 9, of which 8 were waited for; matrix products, arithmetic and copies ran while one was open for 3% of the time, Pallas kernels for 0%

profile of v2, /device:TPU:1, one launch (start us, length us, event | category | flops | bytes accessed | tf_op | source)
XLA Modules:
  0.0 218.3 jit_solution(1201408039253913878)
XLA Ops:
  8.6 27.9 %all_to_all.35 = bf16[4,16,448]{2,1,0:T(8,128)(2,1)S(1)} all-to-all(bf16[4,16,448]{2,1,0:T(8,128)(2,1)S(1)} %broadcast_in_dim.77), channel_id=1, replica_groups=mesh['zl'=4,'core'=2,'y'=4,'x'=4,'zh'=4] {'zh'}, dimensions={0} | all-to-all | bytes 114688 | tf_op jit(solution)/shard_map/all_to_all | solution.py:43
  37.9 6.8 %all-to-all-start.1 = ((bf16[16,8,8,448]{3,2,1,0:T(8,128)(2,1)}), bf16[16,8,8,448]{3,2,1,0:T(8,128)(2,1)S(1)}, u32[]{:S(2)}, u32[]{:S(2)}) async-start(bf16[16,8,8,448]{3,2,1,0:T(8,128)(2,1)} %broadcast_in_dim.79), calls=%async_computation.1 | async-start | bytes 2097152 | tf_op jit(solution)/shard_map/all_to_all | solution.py:43
  44.6 15.1 %all-to-all-done.1 = bf16[16,8,8,448]{3,2,1,0:T(8,128)(2,1)S(1)} async-done(((bf16[16,8,8,448]{3,2,1,0:T(8,128)(2,1)}), bf16[16,8,8,448]{3,2,1,0:T(8,128)(2,1)S(1)}, u32[]{:S(2)}, u32[]{:S(2)}) %all-to-all-start.1) | async-done | bytes 917536 | tf_op jit(solution)/shard_map/all_to_all | solution.py:43
  59.8 1.4 fusion.7
  61.3 5.2 %collective-permute-start = (f32[512,512]{1,0:T(8,128)}, f32[512,512]{1,0:T(8,128)S(1)}, u32[]{:S(2)}, u32[]{:S(2)}) collective-permute-start(f32[512,512]{1,0:T(8,128)} %fusion.7), channel_id=1, source_target_pairs={{0,64},{64,0},{1,65},{65,1},{2,66},{66,2},{3,67},{67,3},{4,68},{68... | collective-permute-start | bytes 3145736 | tf_op jit(solution)/shard_map/ppermute | solution.py:47
  66.4 2.5 %collective-permute-done = f32[512,512]{1,0:T(8,128)S(1)} collective-permute-done((f32[512,512]{1,0:T(8,128)}, f32[512,512]{1,0:T(8,128)S(1)}, u32[]{:S(2)}, u32[]{:S(2)}) %collective-permute-start) | collective-permute-done | bytes 1048608 | tf_op jit(solution)/shard_map/ppermute | solution.py:47
  70.1 3.5 %all-to-all-start.2 = ((bf16[4,128,512]{2,1,0:T(8,128)(2,1)}), bf16[4,128,512]{2,1,0:T(8,128)(2,1)S(1)}, u32[]{:S(2)}, u32[]{:S(2)}) async-start(bf16[4,128,512]{2,1,0:T(8,128)(2,1)} %bitcast.6), calls=%async_computation.2 | async-start | bytes 1048576 | tf_op jit(solution)/shard_map/all_to_all | solution.py:97
  73.8 14.0 %all-to-all-done.2 = bf16[4,128,512]{2,1,0:T(8,128)(2,1)S(1)} async-done(((bf16[4,128,512]{2,1,0:T(8,128)(2,1)}), bf16[4,128,512]{2,1,0:T(8,128)(2,1)S(1)}, u32[]{:S(2)}, u32[]{:S(2)}) %all-to-all-start.2) | async-done | bytes 524320 | tf_op jit(solution)/shard_map/all_to_all | solution.py:97
  87.9 6.1 %convert_multiply_fusion = f32[3584,512]{1,0:T(8,128)} fusion(bf16[3584,512]{1,0:T(8,128)(2,1)} %all-gather.3.cloned.1.call-done), kind=kLoop, calls=%fused_computation | loop fusion | flops 3670016 | bytes 11010048 | tf_op jit(solution)/shard_map/square | solution.py:104
  94.0 3.5 %reduce_sum.112 = f32[2,512]{1,0:T(2,128)S(1)} reduce(f32[2,1792,512]{2,1,0:T(8,128)} %bitcast.42, f32[]{:T(128)} %constant.43.clone.1), dimensions={1}, to_apply=%region_2.3 | reduce | flops 1833984 | bytes 7344132 | tf_op jit(solution)/shard_map/reduce_sum | solution.py:105
  98.4 4.3 %fusion = bf16[16,8,3584]{2,1,0:T(8,128)(2,1)} fusion(bf16[128,512]{1,0:T(8,128)(2,1)S(1)} %get-tuple-element.10, bf16[3584,512]{1,0:T(8,128)(2,1)} %all-gather.3.cloned.1.call-done), kind=kOutput, calls=%fused_computation.2 | convolution fusion | flops 470220800 | bytes 4718592 | tf_op jit(solution)/shard_map/dot_general | solution.py:112
  102.7 3.6 %all-to-all-start.3 = ((bf16[16,8,3584]{2,1,0:T(8,128)(2,1)}), bf16[16,8,3584]{2,1,0:T(8,128)(2,1)S(1)}, u32[]{:S(2)}, u32[]{:S(2)}) async-start(bf16[16,8,3584]{2,1,0:T(8,128)(2,1)} %fusion), calls=%async_computation.3 | async-start | bytes 1835008 | tf_op jit(solution)/shard_map/all_to_all | solution.py:115
  108.6 12.0 %all-to-all-done.3 = bf16[16,8,3584]{2,1,0:T(8,128)(2,1)S(1)} async-done(((bf16[16,8,3584]{2,1,0:T(8,128)(2,1)}), bf16[16,8,3584]{2,1,0:T(8,128)(2,1)S(1)}, u32[]{:S(2)}, u32[]{:S(2)}) %all-to-all-start.3) | async-done | bytes 917536 | tf_op jit(solution)/shard_map/all_to_all | solution.py:115
  120.6 5.9 %all-to-all-start.5 = ((bf16[8,16,448]{2,1,0:T(8,128)(2,1)}), bf16[8,16,448]{2,1,0:T(8,128)(2,1)S(1)}, u32[]{:S(2)}, u32[]{:S(2)}) async-start(bf16[8,16,448]{2,1,0:T(8,128)(2,1)} %pad_maximum_fusion), calls=%async_computation.5 | async-start | bytes 262144 | tf_op jit(solution)/shard_map/all_to_all | solution.py:91
  126.7 5.7 %all-to-all-done.5 = bf16[8,16,448]{2,1,0:T(8,128)(2,1)S(1)} async-done(((bf16[8,16,448]{2,1,0:T(8,128)(2,1)}), bf16[8,16,448]{2,1,0:T(8,128)(2,1)S(1)}, u32[]{:S(2)}, u32[]{:S(2)}) %all-to-all-start.5) | async-done | bytes 114720 | tf_op jit(solution)/shard_map/all_to_all | solution.py:91
  133.1 5.8 %all-to-all-start.4 = ((bf16[4,8,3712]{2,1,0:T(8,128)(2,1)}), bf16[4,8,3712]{2,1,0:T(8,128)(2,1)S(1)}, u32[]{:S(2)}, u32[]{:S(2)}) async-start(bf16[4,8,3712]{2,1,0:T(8,128)(2,1)} %broadcast_in_dim.85), calls=%async_computation.4 | async-start | bytes 475136 | tf_op jit(solution)/shard_map/all_to_all | solution.py:43
  139.2 14.2 %all-to-all-done.4 = bf16[4,8,3712]{2,1,0:T(8,128)(2,1)S(1)} async-done(((bf16[4,8,3712]{2,1,0:T(8,128)(2,1)}), bf16[4,8,3712]{2,1,0:T(8,128)(2,1)S(1)}, u32[]{:S(2)}, u32[]{:S(2)}) %all-to-all-start.4) | async-done | bytes 237600 | tf_op jit(solution)/shard_map/all_to_all | solution.py:43
  157.2 3.6 %all-to-all-start.6 = ((bf16[16,8,3712]{2,1,0:T(8,128)(2,1)}), bf16[16,8,3712]{2,1,0:T(8,128)(2,1)S(1)}, u32[]{:S(2)}, u32[]{:S(2)}) async-start(bf16[16,8,3712]{2,1,0:T(8,128)(2,1)} %broadcast_in_dim.91), calls=%async_computation.6 | async-start | bytes 1900544 | tf_op jit(solution)/shard_map/all_to_all | solution.py:43
  160.9 12.6 %all-to-all-done.6 = bf16[16,8,3712]{2,1,0:T(8,128)(2,1)S(1)} async-done(((bf16[16,8,3712]{2,1,0:T(8,128)(2,1)}), bf16[16,8,3712]{2,1,0:T(8,128)(2,1)S(1)}, u32[]{:S(2)}, u32[]{:S(2)}) %all-to-all-start.6) | async-done | bytes 950304 | tf_op jit(solution)/shard_map/all_to_all | solution.py:43
  175.5 2.7 %fusion.3 = bf16[128,512]{1,0:T(8,128)(2,1)S(1)} fusion(bf16[3584,512]{1,0:T(8,128)(2,1)} %all-gather.3.cloned.1.call-done, bf16[128,3712]{1,0:T(8,128)(2,1)S(1)} %bitcast.53, f32[128,512]{1,0:T(8,128)S(1)} %convert_reduce_fusion, f32[512]{0:T(512)S(1)} %broadcast_multiply_fusion, f32[512]{0:T(512)S(1)} %copy-done.1), kind=kOutput, calls=%fused_computation.9 | convolution fusion | flops 470286336 | bytes 4984832 | tf_op jit(solution)/shard_map/dot_general | solution.py:127
  178.3 14.3 %all-gather = bf16[544,512]{1,0:T(8,128)(2,1)S(1)} all-gather(bf16[136,512]{1,0:T(8,128)(2,1)S(1)} %maximum_maximum_fusion), channel_id=2, replica_groups=mesh['zl'=4,'core'=2,'y'=4,'x'=4,'zh'=4] {'zl'}, dimensions={0}, use_global_device_ids=true | all-gather | bytes 696320 | tf_op jit(solution)/shard_map/all_gather | solution.py:133
  192.6 8.5 %collective-permute-start.1 = (bf16[4,136,512]{2,1,0:T(8,128)(2,1)S(1)}, bf16[4,136,512]{2,1,0:T(8,128)(2,1)}, u32[]{:S(2)}, u32[]{:S(2)}) collective-permute-start(bf16[4,136,512]{2,1,0:T(8,128)(2,1)S(1)} %bitcast.48), channel_id=1, source_target_pairs={{0,64},{64,0},{1,65},{65,1},{2,66},{66,2},{3,67},{67,3},{4,68},{68... | collective-permute-start | bytes 1671176 | tf_op jit(solution)/shard_map/ppermute | solution.py:47
  202.8 1.3 fusion.21
  206.5 3.9 %subtract_convert_fusion = (bf16[448,512]{1,0:T(8,128)(2,1)}, f32[448,512]{1,0:T(8,128)}, f32[448,512]{1,0:T(8,128)}) fusion(bf16[448,512]{1,0:T(8,128)(2,1)S(1)} %copy-done, f32[448,512]{1,0:T(8,128)} %param.12, f32[448,512]{1,0:T(8,128)} %param.13, f32[448,512]{1,0:T(8,128)S(1)} %fusion.9, bf16[512,512]{1,0:T(8,128)(2,1)S(1)} %bitcast.56, ...), kind=kOutput, calls=%fused_computation.13 | convolution fusion | flops 238551040 | bytes 6553604 | tf_op jit(solution)/shard_map/dot_general | solution.py:137
  (61 shorter events, 13.2 us)
Async XLA Ops:
  7.2 52.7 %copy-start = (bf16[448,512]{1,0:T(8,128)(2,1)S(1)}, bf16[448,512]{1,0:T(8,128)(2,1)}, u32[]{:S(2)}) copy-start(bf16[448,512]{1,0:T(8,128)(2,1)} %param.8) | copy-start | bytes 1376260
  7.2 80.7 %all-gather.3.cloned.1.call-start = ((), (), s32[]{:S(2)}) async-start(), calls=%async_computation.7 | async-start | bytes 4128768 | tf_op jit(solution)/shard_map/all_gather | solution.py:72
  37.9 21.9 %all-to-all-start.1 = ((bf16[16,8,8,448]{3,2,1,0:T(8,128)(2,1)}), bf16[16,8,8,448]{3,2,1,0:T(8,128)(2,1)S(1)}, u32[]{:S(2)}, u32[]{:S(2)}) async-start(bf16[16,8,8,448]{3,2,1,0:T(8,128)(2,1)} %broadcast_in_dim.79), calls=%async_computation.1 | async-start | bytes 2097152 | tf_op jit(solution)/shard_map/all_to_all | solution.py:43
  59.7 13.9 %copy-start.2 = (f32[448]{0:T(512)S(1)}, f32[448]{0:T(512)}, u32[]{:S(2)}) copy-start(f32[448]{0:T(512)} %param.11) | copy-start | bytes 5380
  61.3 7.6 %collective-permute-start = (f32[512,512]{1,0:T(8,128)}, f32[512,512]{1,0:T(8,128)S(1)}, u32[]{:S(2)}, u32[]{:S(2)}) collective-permute-start(f32[512,512]{1,0:T(8,128)} %fusion.7), channel_id=1, source_target_pairs={{0,64},{64,0},{1,65},{65,1},{2,66},{66,2},{3,67},{67,3},{4,68},{68... | collective-permute-start | bytes 3145736 | tf_op jit(solution)/shard_map/ppermute | solution.py:47
  70.1 17.7 %all-to-all-start.2 = ((bf16[4,128,512]{2,1,0:T(8,128)(2,1)}), bf16[4,128,512]{2,1,0:T(8,128)(2,1)S(1)}, u32[]{:S(2)}, u32[]{:S(2)}) async-start(bf16[4,128,512]{2,1,0:T(8,128)(2,1)} %bitcast.6), calls=%async_computation.2 | async-start | bytes 1048576 | tf_op jit(solution)/shard_map/all_to_all | solution.py:97
  94.0 3.6 %copy-start.1 = (f32[512]{0:T(512)S(1)}, f32[512]{0:T(512)}, u32[]{:S(2)}) copy-start(f32[512]{0:T(512)} %param.9) | copy-start | bytes 6148
  102.7 17.9 %all-to-all-start.3 = ((bf16[16,8,3584]{2,1,0:T(8,128)(2,1)}), bf16[16,8,3584]{2,1,0:T(8,128)(2,1)S(1)}, u32[]{:S(2)}, u32[]{:S(2)}) async-start(bf16[16,8,3584]{2,1,0:T(8,128)(2,1)} %fusion), calls=%async_computation.3 | async-start | bytes 1835008 | tf_op jit(solution)/shard_map/all_to_all | solution.py:115
  120.6 11.7 %all-to-all-start.5 = ((bf16[8,16,448]{2,1,0:T(8,128)(2,1)}), bf16[8,16,448]{2,1,0:T(8,128)(2,1)S(1)}, u32[]{:S(2)}, u32[]{:S(2)}) async-start(bf16[8,16,448]{2,1,0:T(8,128)(2,1)} %pad_maximum_fusion), calls=%async_computation.5 | async-start | bytes 262144 | tf_op jit(solution)/shard_map/all_to_all | solution.py:91
  133.1 20.3 %all-to-all-start.4 = ((bf16[4,8,3712]{2,1,0:T(8,128)(2,1)}), bf16[4,8,3712]{2,1,0:T(8,128)(2,1)S(1)}, u32[]{:S(2)}, u32[]{:S(2)}) async-start(bf16[4,8,3712]{2,1,0:T(8,128)(2,1)} %broadcast_in_dim.85), calls=%async_computation.4 | async-start | bytes 475136 | tf_op jit(solution)/shard_map/all_to_all | solution.py:43
  157.2 16.3 %all-to-all-start.6 = ((bf16[16,8,3712]{2,1,0:T(8,128)(2,1)}), bf16[16,8,3712]{2,1,0:T(8,128)(2,1)S(1)}, u32[]{:S(2)}, u32[]{:S(2)}) async-start(bf16[16,8,3712]{2,1,0:T(8,128)(2,1)} %broadcast_in_dim.91), calls=%async_computation.6 | async-start | bytes 1900544 | tf_op jit(solution)/shard_map/all_to_all | solution.py:43
  192.6 10.2 %collective-permute-start.1 = (bf16[4,136,512]{2,1,0:T(8,128)(2,1)S(1)}, bf16[4,136,512]{2,1,0:T(8,128)(2,1)}, u32[]{:S(2)}, u32[]{:S(2)}) collective-permute-start(bf16[4,136,512]{2,1,0:T(8,128)(2,1)S(1)} %bitcast.48), channel_id=1, source_target_pairs={{0,64},{64,0},{1,65},{65,1},{2,66},{66,2},{3,67},{67,3},{4,68},{68... | collective-permute-start | bytes 1671176 | tf_op jit(solution)/shard_map/ppermute | solution.py:47
Sparse Core Ops, SparseCore 0:
  10.1 57.4 all-gather.2

commit v3 on v2

--- a/solution.py
+++ b/solution.py
@@ -63,62 +63,82 @@
     inv_batch = 1.0 / (rows * BLOCKS * HIGH)
     wide = PARTS * chans
     core = lax.axis_index("core")
-    part = lax.axis_index(LAYER)
-    padded = rows + 1
-    share = padded // PARTS
+    chip = lax.axis_index("zl")
+    share = (rows + 1) // PARTS
+    half = CHIPS * share
     small = HIGH * share
     tokens = BLOCKS * small
 
     dec_all = lax.all_gather(dec_weight.T, LAYER, axis=0, tiled=True)
+    enc_there = swap(enc_weight)
 
-    packed = jnp.concatenate([acts, jnp.zeros((1, chans), BF)], axis=0)
-    column = spread(packed, "zh", HIGH)
-    column = column.reshape(HIGH, CHIPS, CORES, share, chans).transpose(2, 1, 0, 3, 4)
-    column = column.reshape(PARTS, small, chans)
+    padded = jnp.concatenate([acts, jnp.zeros((1, chans), BF)], axis=0)
+    bias_rows = jnp.stack(pieces(dec_bias))
+    fill = jnp.zeros((half - 3, chans), BF)
+    low, high = padded[:half], padded[half:]
+    give = jnp.concatenate([jnp.where(core == 0, high, low), bias_rows, fill], axis=0)
+    taken = swap(give)
+    pair = jnp.concatenate([jnp.where(core == 0, low, high), taken[:half]], axis=1)
+    column = spread(pair, "zh", HIGH).reshape(HIGH, CHIPS, share, 2 * chans)
+    column = column.transpose(1, 0, 2, 3).reshape(CHIPS, small, 2 * chans)
     gathered = spread(column, PLANE, BLOCKS).transpose(1, 0, 2, 3)
-    gathered = gathered.reshape(CORES, CHIPS * tokens, chans)
-    acts_here = lax.dynamic_index_in_dim(gathered, core, 0, keepdims=False)
-    acts_there = lax.dynamic_index_in_dim(gathered, 1 - core, 0, keepdims=False)
+    gathered = gathered.reshape(CHIPS * tokens, 2 * chans)
+    acts_here = gathered[:, :chans]
+    acts_there = swap(gathered[:, chans:])
 
-    bias_rows = jnp.concatenate(
-        [jnp.stack(pieces(dec_bias)), jnp.zeros((small - 3, chans), BF)], axis=0
+    enc_pair = jnp.concatenate([enc_weight, enc_there], axis=0)
+    sums = jnp.dot(gathered, enc_pair, preferred_element_type=F32).astype(BF)
+
+    extra = jnp.concatenate(
+        [
+            column[:, :, :chans],
+            column[:, :, chans:],
+            jnp.broadcast_to(bias_rows[None], (CHIPS, 3, chans)),
+            jnp.broadcast_to(taken[None, half : half + 3], (CHIPS, 3, chans)),
+            jnp.zeros((CHIPS, 2, chans), BF),
+        ],
+        axis=1,
     )
-    by_part = column.reshape(CORES, CHIPS, small, chans).transpose(1, 0, 2, 3)
-    by_part = by_part.reshape(PARTS, small, chans)
-    small_send = jnp.concatenate(
-        [by_part, jnp.broadcast_to(bias_rows[None], by_part.shape)], axis=1
-    )
-    small_got = lax.all_to_all(small_send, LAYER, 0, 0, tiled=True)
-    mine = small_got[:, :small].transpose(1, 0, 2).reshape(small, wide).astype(F32)
-    bias_full = small_got[:, small:].astype(F32).sum(axis=1).reshape(1, wide)
-
-    sent = swap(jnp.dot(acts_there, enc_weight, preferred_element_type=F32))
-    pair = jnp.dot(acts_here, enc_weight, preferred_element_type=F32) + sent
-    quarter = lax.all_to_all(
-        pair.astype(BF).reshape(CHIPS, tokens, latents), "zl", 0, 0, tiled=True
-    )
-    preact = jnp.sum(quarter.astype(F32), axis=0) + enc_bias
+    extra = jnp.pad(extra, ((0, 0), (0, 0), (0, latents - chans)))
+    sending = jnp.concatenate([sums.reshape(CHIPS, tokens, latents), extra], axis=1)
+    quarter = lax.all_to_all(sending, "zl", 0, 0, tiled=True)
+    preact = jnp.sum(quarter[:, :tokens].astype(F32), axis=0) + enc_bias
     codes = (jax.nn.softplus(sharpness * preact) / sharpness).astype(BF)
+    codes, acts_there = lax.optimization_barrier((codes, acts_there))
     slopes = jax.nn.sigmoid(sharpness * preact)
 
-    squares = jnp.square(dec_all.astype(F32)).reshape(LAYERS, wide // LAYERS, latents)
-    dec_norms = jnp.sum(jnp.sqrt(jnp.sum(squares, axis=1)), axis=0)
+    def ordered(near, far):
+        first, second = jnp.where(core == 0, near, far), jnp.where(core == 0, far, near)
+        both = jnp.stack([first, second], axis=1)
+        return both.transpose(2, 0, 1, 3).reshape(both.shape[2], wide)
+
+    beyond = quarter[:, tokens:, :chans].astype(F32)
+    mine = ordered(beyond[:, :small], beyond[:, small : 2 * small])
+    end = 2 * small
+    bias_near = beyond[:, end : end + 3].sum(axis=1, keepdims=True)
+    bias_far = beyond[:, end + 3 : end + 6].sum(axis=1, keepdims=True)
+    target = mine - ordered(bias_near, bias_far)
+
+    partial_value = lax.dot_general(
+        codes, dec_all, (((1,), (1,)), ((), ())), preferred_element_type=F32
+    )
+    dec_norms = jnp.zeros((latents,), F32)
+    for layer in range(LAYERS):
+        block = dec_all[layer * (wide // LAYERS) : (layer + 1) * (wide // LAYERS)].astype(F32)
+        dec_norms = dec_norms + jnp.sqrt(jnp.sum(block * block, axis=0))
 
     def real(count):
         place = lax.broadcasted_iota(jnp.int32, (count, 1), 0) % share
-        return (part * share + place < rows).astype(F32)
+        return (core * half + chip * share + place < rows).astype(F32)
 
     sparse = jnp.sum(real(tokens) * codes.astype(F32) * dec_norms)
-    partial_value = lax.dot_general(
-        codes, dec_all, (((1,), (1,)), ((), ())), preferred_element_type=F32
-    )
     got = lax.all_to_all(
         partial_value.astype(BF).reshape(BLOCKS, small, wide), PLANE, 0, 0, tiled=True
     )
     summed = jnp.sum(got.astype(F32), axis=0).astype(BF)
     total = jnp.sum(spread(beside(summed, sparse), "zh", HIGH).astype(F32), axis=0)
 
-    error = total[:, :wide] + bias_full - mine
+    error = total[:, :wide] - target
     piece = jnp.sum(real(small) * error * error) + sparsity * jnp.sum(total[:, wide:])
     grad = (error * (2.0 * inv_batch)).astype(BF)
     grad_got = spread(beside(grad, inv_batch * piece), PLANE, BLOCKS)
@@ -134,9 +154,10 @@
     pre_there = swap(pre_here)
 
     def part_of(acts_half, pre_half):
+        longer = jnp.pad(acts_half.reshape(CHIPS, tokens, chans), ((0, 0), (0, 8), (0, 0)))
         return lax.dot_general(
-            acts_half,
-            pre_half[:, :tokens].reshape(CHIPS * tokens, latents),
+            longer.reshape(-1, chans),
+            pre_half.reshape(-1, latents),
             (((0,), (0,)), ((), ())),
             preferred_element_type=F32,
         )

time: 219 us -> 201 us (0.918)
  blocking collectives: 42.3 us -> 17.4 us
  starting transfers between devices: 42.8 us -> 63.9 us
  waiting for transfers between devices: 78.1 us -> 70.3 us
  other arithmetic: 15.1 us -> 9.51 us
    all_to_all x1 -> x0, blocking collectives: 27.9 us -> none  [spread(): return lax.all_to_all(copies, axes, 0, 0, tiled=True)]
    all_to_all x3 -> x4, starting transfers between devices: 16.2 us -> 29.1 us  [spread(): return lax.all_to_all(copies, axes, 0, 0, tiled=True)]
    all_to_all x2 -> x1, waiting for transfers between devices: 19.7 us -> 9.62 us  [body(): quarter = lax.all_to_all(sending, 'zl', 0, 0, tiled=True)]
    ppermute x2 -> x4, starting transfers between devices: 13.6 us -> 23.7 us  [swap(): return lax.ppermute(value, 'core', [(0, 1), (1, 0)])]
    all_to_all x3 -> x4, waiting for transfers between devices: 41.9 us -> 49.8 us  [spread(): return lax.all_to_all(copies, axes, 0, 0, tiled=True)]
    square x1 -> x0, other arithmetic: 6.06 us -> none  [body(): jnp.square(dec_all.astype(F32)).reshape(LAYERS, wide // LAYERS, latents)]
    all_to_all x2 -> x1, starting transfers between devices: 9.37 us -> 3.48 us  [body(): quarter = lax.all_to_all(sending, 'zl', 0, 0, tiled=True)]
    all_to_all x1, starting transfers between devices: 3.63 us -> 7.57 us  [body(): lax.all_to_all(partial_value.astype(BF).reshape(BLOCKS, small, wide), PLA...]
  transfers between devices with their start and end apart: 9 -> 11, of which waited for: 8 -> 8; matrix products, arithmetic and copies ran while one was open for 3% -> 6% of each run, Pallas kernels for 0% -> 0%
where the time goes in v3:
time: 201 us; the launch traced here: 200 us
  waiting for transfers between devices  70.3 us (35%)
  starting transfers between devices  63.9 us (32%)
  between operations  20.9 us (10%)
  blocking collectives  17.4 us (9%)
  matrix products  13.3 us (7%)
  other arithmetic  9.51 us (5%)
  local copies, waits for them, and re-layouts  4.46 us (2%)
    all_to_all x4, waiting for transfers between devices, spread(): return lax.all_to_all(copies, axes, 0, 0, tiled=True)  49.8 us
    all_to_all x4, starting transfers between devices, spread(): return lax.all_to_all(copies, axes, 0, 0, tiled=True)  29.1 us
    ppermute x4, starting transfers between devices, swap(): return lax.ppermute(value, 'core', [(0, 1), (1, 0)])  23.7 us
    all_gather x1, blocking collectives, body(): pre_here = lax.all_gather(last, 'zl', axis=0)  17.4 us
    all_to_all x1, waiting for transfers between devices, body(): quarter = lax.all_to_all(sending, 'zl', 0, 0, tiled=True)  9.62 us
    all_to_all x1, waiting for transfers between devices, body(): lax.all_to_all(partial_value.astype(BF).reshape(BLOCKS, small, wide), PLA...  9.33 us
    all_to_all x1, starting transfers between devices, body(): lax.all_to_all(partial_value.astype(BF).reshape(BLOCKS, small, wide), PLA...  7.57 us
    dot_general x2, matrix products, part_of(): lax.dot_general(longer.reshape(-1, chans), pre_half.reshape(-1, latents),...  5.37 us
  transfers between devices with their start and end apart: 11, of which 8 were waited for; matrix products, arithmetic and copies ran while one was open for 6% of the time, Pallas kernels for 0%

profile of v3, /device:TPU:1, one launch (start us, length us, event | category | flops | bytes accessed | tf_op | source)
XLA Modules:
  0.0 199.7 jit_solution(3639100323461119613)
XLA Ops:
  9.5 8.8 %collective-permute-start = (bf16[16,448]{1,0:T(8,128)(2,1)S(1)}, bf16[16,448]{1,0:T(8,128)(2,1)S(1)}, u32[]{:S(2)}, u32[]{:S(2)}) collective-permute-start(bf16[16,448]{1,0:T(8,128)(2,1)S(1)} %concatenate.30), channel_id=1, source_target_pairs={{0,64},{64,0},{1,65},{65,1},{2,66},{66,2},{3,67},{67,3},{4,68},{68... | collective-permute-start | bytes 43016 | tf_op jit(solution)/shard_map/ppermute | solution.py:47
  19.9 9.4 %all-to-all-start = ((bf16[4,8,896]{2,1,0:T(8,128)(2,1)}), bf16[4,8,896]{2,1,0:T(8,128)(2,1)S(1)}, u32[]{:S(2)}, u32[]{:S(2)}) async-start(bf16[4,8,896]{2,1,0:T(8,128)(2,1)} %broadcast_in_dim.89), calls=%async_computation | async-start | bytes 114688 | tf_op jit(solution)/shard_map/all_to_all | solution.py:43
  29.3 2.5 %collective-permute-start.1 = (bf16[448,512]{1,0:T(8,128)(2,1)}, bf16[448,512]{1,0:T(8,128)(2,1)S(1)}, u32[]{:S(2)}, u32[]{:S(2)}) collective-permute-start(bf16[448,512]{1,0:T(8,128)(2,1)} %param.8), channel_id=1, source_target_pairs={{0,64},{64,0},{1,65},{65,1},{2,66},{66,2},{3,67},{67,3},{4,68},{68... | collective-permute-start | bytes 1376264 | tf_op jit(solution)/shard_map/ppermute | solution.py:47
  31.8 9.3 %all-to-all-done = bf16[4,8,896]{2,1,0:T(8,128)(2,1)S(1)} async-done(((bf16[4,8,896]{2,1,0:T(8,128)(2,1)}), bf16[4,8,896]{2,1,0:T(8,128)(2,1)S(1)}, u32[]{:S(2)}, u32[]{:S(2)}) %all-to-all-start) | async-done | bytes 57376 | tf_op jit(solution)/shard_map/all_to_all | solution.py:43
  41.3 1.0 broadcast_in_dim.91
  42.3 6.8 %all-to-all-start.1 = ((bf16[16,4,8,896]{3,2,1,0:T(8,128)(2,1)}), bf16[16,4,8,896]{3,2,1,0:T(8,128)(2,1)S(1)}, u32[]{:S(2)}, u32[]{:S(2)}) async-start(bf16[16,4,8,896]{3,2,1,0:T(8,128)(2,1)} %broadcast_in_dim.91), calls=%async_computation.1 | async-start | bytes 1835008 | tf_op jit(solution)/shard_map/all_to_all | solution.py:43
  49.2 13.5 %all-to-all-done.1 = bf16[16,4,8,896]{3,2,1,0:T(8,128)(2,1)S(1)} async-done(((bf16[16,4,8,896]{3,2,1,0:T(8,128)(2,1)}), bf16[16,4,8,896]{3,2,1,0:T(8,128)(2,1)S(1)}, u32[]{:S(2)}, u32[]{:S(2)}) %all-to-all-start.1) | async-done | bytes 917536 | tf_op jit(solution)/shard_map/all_to_all | solution.py:43
  64.5 3.5 %all-to-all-start.2 = ((bf16[4,152,512]{2,1,0:T(8,128)(2,1)}), bf16[4,152,512]{2,1,0:T(8,128)(2,1)S(1)}, u32[]{:S(2)}, u32[]{:S(2)}) async-start(bf16[4,152,512]{2,1,0:T(8,128)(2,1)} %fusion.10), calls=%async_computation.2 | async-start | bytes 1245184 | tf_op jit(solution)/shard_map/all_to_all | solution.py:104
  68.3 5.1 %collective-permute-start.2 = (bf16[512,448]{1,0:T(8,128)(2,1)S(1)}, bf16[512,448]{1,0:T(8,128)(2,1)S(1)}, u32[]{:S(2)}, u32[]{:S(2)}) collective-permute-start(bf16[512,448]{1,0:T(8,128)(2,1)S(1)} %get-tuple-element.20), channel_id=1, source_target_pairs={{0,64},{64,0},{1,65},{65,1},{2,66},{66,2},{3,67},{67,3},{4,68},{68... | collective-permute-start | bytes 1376264 | tf_op jit(solution)/shard_map/ppermute | solution.py:47
  73.4 9.6 %all-to-all-done.2 = bf16[4,152,512]{2,1,0:T(8,128)(2,1)S(1)} async-done(((bf16[4,152,512]{2,1,0:T(8,128)(2,1)}), bf16[4,152,512]{2,1,0:T(8,128)(2,1)S(1)}, u32[]{:S(2)}, u32[]{:S(2)}) %all-to-all-start.2) | async-done | bytes 622624 | tf_op jit(solution)/shard_map/all_to_all | solution.py:104
  83.4 4.4 %fusion = bf16[16,8,3584]{2,1,0:T(8,128)(2,1)} fusion(bf16[128,512]{1,0:T(8,128)(2,1)S(1)} %fusion.14, bf16[3584,512]{1,0:T(8,128)(2,1)} %all-gather.3.cloned.1.call-done), kind=kOutput, calls=%fused_computation.1 | convolution fusion | flops 470220800 | bytes 4718592 | tf_op jit(solution)/shard_map/dot_general | solution.py:122
  87.8 7.6 %all-to-all-start.3 = ((bf16[16,8,3584]{2,1,0:T(8,128)(2,1)}), bf16[16,8,3584]{2,1,0:T(8,128)(2,1)S(1)}, u32[]{:S(2)}, u32[]{:S(2)}) async-start(bf16[16,8,3584]{2,1,0:T(8,128)(2,1)} %fusion), calls=%async_computation.3 | async-start | bytes 1835008 | tf_op jit(solution)/shard_map/all_to_all | solution.py:135
  95.4 2.8 %multiply_reduce_fusion.1 = (f32[512]{0:T(512)S(1)}, f32[512]{0:T(512)S(1)}) fusion(bf16[3584,512]{1,0:T(8,128)(2,1)} %all-gather.3.cloned.1.call-done), kind=kLoop, calls=%fused_computation.3 | loop fusion | flops 5504000 | bytes 3674112 | tf_op jit(solution)/shard_map/reduce_sum | solution.py:128
  100.4 9.3 %all-to-all-done.3 = bf16[16,8,3584]{2,1,0:T(8,128)(2,1)S(1)} async-done(((bf16[16,8,3584]{2,1,0:T(8,128)(2,1)}), bf16[16,8,3584]{2,1,0:T(8,128)(2,1)S(1)}, u32[]{:S(2)}, u32[]{:S(2)}) %all-to-all-start.3) | async-done | bytes 917536 | tf_op jit(solution)/shard_map/all_to_all | solution.py:135
  110.5 8.6 %all-to-all-start.4 = ((bf16[4,8,3712]{2,1,0:T(8,128)(2,1)}), bf16[4,8,3712]{2,1,0:T(8,128)(2,1)S(1)}, u32[]{:S(2)}, u32[]{:S(2)}) async-start(bf16[4,8,3712]{2,1,0:T(8,128)(2,1)} %broadcast_in_dim.100), calls=%async_computation.4 | async-start | bytes 475136 | tf_op jit(solution)/shard_map/all_to_all | solution.py:43
  119.7 14.0 %all-to-all-done.4 = bf16[4,8,3712]{2,1,0:T(8,128)(2,1)S(1)} async-done(((bf16[4,8,3712]{2,1,0:T(8,128)(2,1)}), bf16[4,8,3712]{2,1,0:T(8,128)(2,1)S(1)}, u32[]{:S(2)}, u32[]{:S(2)}) %all-to-all-start.4) | async-done | bytes 237600 | tf_op jit(solution)/shard_map/all_to_all | solution.py:43
  136.5 1.0 broadcast_in_dim.104
  137.5 4.3 %all-to-all-start.5 = ((bf16[16,8,3712]{2,1,0:T(8,128)(2,1)}), bf16[16,8,3712]{2,1,0:T(8,128)(2,1)S(1)}, u32[]{:S(2)}, u32[]{:S(2)}) async-start(bf16[16,8,3712]{2,1,0:T(8,128)(2,1)} %broadcast_in_dim.104), calls=%async_computation.5 | async-start | bytes 1900544 | tf_op jit(solution)/shard_map/all_to_all | solution.py:43
  141.8 12.9 %all-to-all-done.5 = bf16[16,8,3712]{2,1,0:T(8,128)(2,1)S(1)} async-done(((bf16[16,8,3712]{2,1,0:T(8,128)(2,1)}), bf16[16,8,3712]{2,1,0:T(8,128)(2,1)S(1)}, u32[]{:S(2)}, u32[]{:S(2)}) %all-to-all-start.5) | async-done | bytes 950304 | tf_op jit(solution)/shard_map/all_to_all | solution.py:43
  156.8 2.8 %fusion.4 = bf16[128,512]{1,0:T(8,128)(2,1)S(1)} fusion(bf16[3584,512]{1,0:T(8,128)(2,1)} %all-gather.3.cloned.1.call-done, bf16[128,3712]{1,0:T(8,128)(2,1)S(1)} %bitcast.43, f32[128,512]{1,0:T(8,128)S(1)} %convert_reduce_fusion, f32[512]{0:T(512)S(1)} %get-tuple-element.17, f32[512]{0:T(512)S(1)} %copy-done), kind=kOutput, calls=%fused_computation.13 | convolution fusion | flops 470286336 | bytes 4984832 | tf_op jit(solution)/shard_map/dot_general | solution.py:147
  159.7 17.4 %all-gather = bf16[544,512]{1,0:T(8,128)(2,1)S(1)} all-gather(bf16[136,512]{1,0:T(8,128)(2,1)S(1)} %maximum_maximum_fusion), channel_id=2, replica_groups=mesh['zl'=4,'core'=2,'y'=4,'x'=4,'zh'=4] {'zl'}, dimensions={0}, use_global_device_ids=true | all-gather | bytes 696320 | tf_op jit(solution)/shard_map/all_gather | solution.py:153
  177.0 7.3 %collective-permute-start.3 = (bf16[4,136,512]{2,1,0:T(8,128)(2,1)S(1)}, bf16[4,136,512]{2,1,0:T(8,128)(2,1)S(1)}, u32[]{:S(2)}, u32[]{:S(2)}) collective-permute-start(bf16[4,136,512]{2,1,0:T(8,128)(2,1)S(1)} %bitcast.44), channel_id=1, source_target_pairs={{0,64},{64,0},{1,65},{65,1},{2,66},{66,2},{3,67},{67,3},{4,68},{68... | collective-permute-start | bytes 1671176 | tf_op jit(solution)/shard_map/ppermute | solution.py:47
  184.4 1.5 convolution_bitcast_fusion.1
  187.9 3.9 %subtract_convert_fusion = (bf16[448,512]{1,0:T(8,128)(2,1)}, f32[448,512]{1,0:T(8,128)}, f32[448,512]{1,0:T(8,128)}) fusion(bf16[448,512]{1,0:T(8,128)(2,1)} %param.8, f32[448,512]{1,0:T(8,128)S(1)} %copy-done.1, f32[448,512]{1,0:T(8,128)S(1)} %copy-done.2, f32[448,512]{1,0:T(8,128)} %convolution_bitcast_fusion.1, ...), kind=kOutput, calls=%fused_computation.20 | convolution fusion | flops 253231104 | bytes 6520832 | tf_op jit(solution)/shard_map/dot_general | solution.py:158
  (80 shorter events, 11.5 us)
Async XLA Ops:
  7.2 55.7 %copy-start.5 = (bf16[448,512]{1,0:T(8,128)(2,1)S(1)}, bf16[448,512]{1,0:T(8,128)(2,1)}, u32[]{:S(2)}) copy-start(bf16[448,512]{1,0:T(8,128)(2,1)} %param.8) | copy-start | bytes 1376260
  7.2 76.2 %all-gather.3.cloned.1.call-start = ((), (), s32[]{:S(2)}) async-start(), calls=%async_computation.6 | async-start | bytes 4128768 | tf_op jit(solution)/shard_map/all_gather | solution.py:72
  9.5 9.6 %collective-permute-start = (bf16[16,448]{1,0:T(8,128)(2,1)S(1)}, bf16[16,448]{1,0:T(8,128)(2,1)S(1)}, u32[]{:S(2)}, u32[]{:S(2)}) collective-permute-start(bf16[16,448]{1,0:T(8,128)(2,1)S(1)} %concatenate.30), channel_id=1, source_target_pairs={{0,64},{64,0},{1,65},{65,1},{2,66},{66,2},{3,67},{67,3},{4,68},{68... | collective-permute-start | bytes 43016 | tf_op jit(solution)/shard_map/ppermute | solution.py:47
  19.9 21.3 %all-to-all-start = ((bf16[4,8,896]{2,1,0:T(8,128)(2,1)}), bf16[4,8,896]{2,1,0:T(8,128)(2,1)S(1)}, u32[]{:S(2)}, u32[]{:S(2)}) async-start(bf16[4,8,896]{2,1,0:T(8,128)(2,1)} %broadcast_in_dim.89), calls=%async_computation | async-start | bytes 114688 | tf_op jit(solution)/shard_map/all_to_all | solution.py:43
  29.3 33.5 %collective-permute-start.1 = (bf16[448,512]{1,0:T(8,128)(2,1)}, bf16[448,512]{1,0:T(8,128)(2,1)S(1)}, u32[]{:S(2)}, u32[]{:S(2)}) collective-permute-start(bf16[448,512]{1,0:T(8,128)(2,1)} %param.8), channel_id=1, source_target_pairs={{0,64},{64,0},{1,65},{65,1},{2,66},{66,2},{3,67},{67,3},{4,68},{68... | collective-permute-start | bytes 1376264 | tf_op jit(solution)/shard_map/ppermute | solution.py:47
  42.3 20.5 %all-to-all-start.1 = ((bf16[16,4,8,896]{3,2,1,0:T(8,128)(2,1)}), bf16[16,4,8,896]{3,2,1,0:T(8,128)(2,1)S(1)}, u32[]{:S(2)}, u32[]{:S(2)}) async-start(bf16[16,4,8,896]{3,2,1,0:T(8,128)(2,1)} %broadcast_in_dim.91), calls=%async_computation.1 | async-start | bytes 1835008 | tf_op jit(solution)/shard_map/all_to_all | solution.py:43
  62.9 20.3 %copy-start = (f32[512]{0:T(512)S(1)}, f32[512]{0:T(512)}, u32[]{:S(2)}) copy-start(f32[512]{0:T(512)} %param.9) | copy-start | bytes 6148
  64.5 18.6 %all-to-all-start.2 = ((bf16[4,152,512]{2,1,0:T(8,128)(2,1)}), bf16[4,152,512]{2,1,0:T(8,128)(2,1)S(1)}, u32[]{:S(2)}, u32[]{:S(2)}) async-start(bf16[4,152,512]{2,1,0:T(8,128)(2,1)} %fusion.10), calls=%async_computation.2 | async-start | bytes 1245184 | tf_op jit(solution)/shard_map/all_to_all | solution.py:104
  68.3 15.0 %collective-permute-start.2 = (bf16[512,448]{1,0:T(8,128)(2,1)S(1)}, bf16[512,448]{1,0:T(8,128)(2,1)S(1)}, u32[]{:S(2)}, u32[]{:S(2)}) collective-permute-start(bf16[512,448]{1,0:T(8,128)(2,1)S(1)} %get-tuple-element.20), channel_id=1, source_target_pairs={{0,64},{64,0},{1,65},{65,1},{2,66},{66,2},{3,67},{67,3},{4,68},{68... | collective-permute-start | bytes 1376264 | tf_op jit(solution)/shard_map/ppermute | solution.py:47
  83.3 4.5 %copy-start.3 = (bf16[512,448]{1,0:T(8,128)(2,1)}, bf16[512,448]{1,0:T(8,128)(2,1)S(1)}, u32[]{:S(2)}) copy-start(bf16[512,448]{1,0:T(8,128)(2,1)S(1)} %collective-permute-done.2) | copy-start | bytes 1376260
  87.8 21.9 %all-to-all-start.3 = ((bf16[16,8,3584]{2,1,0:T(8,128)(2,1)}), bf16[16,8,3584]{2,1,0:T(8,128)(2,1)S(1)}, u32[]{:S(2)}, u32[]{:S(2)}) async-start(bf16[16,8,3584]{2,1,0:T(8,128)(2,1)} %fusion), calls=%async_computation.3 | async-start | bytes 1835008 | tf_op jit(solution)/shard_map/all_to_all | solution.py:135
  110.5 23.2 %all-to-all-start.4 = ((bf16[4,8,3712]{2,1,0:T(8,128)(2,1)}), bf16[4,8,3712]{2,1,0:T(8,128)(2,1)S(1)}, u32[]{:S(2)}, u32[]{:S(2)}) async-start(bf16[4,8,3712]{2,1,0:T(8,128)(2,1)} %broadcast_in_dim.100), calls=%async_computation.4 | async-start | bytes 475136 | tf_op jit(solution)/shard_map/all_to_all | solution.py:43
  137.5 17.3 %all-to-all-start.5 = ((bf16[16,8,3712]{2,1,0:T(8,128)(2,1)}), bf16[16,8,3712]{2,1,0:T(8,128)(2,1)S(1)}, u32[]{:S(2)}, u32[]{:S(2)}) async-start(bf16[16,8,3712]{2,1,0:T(8,128)(2,1)} %broadcast_in_dim.104), calls=%async_computation.5 | async-start | bytes 1900544 | tf_op jit(solution)/shard_map/all_to_all | solution.py:43
  156.8 31.1 %copy-start.2 = (f32[448,512]{1,0:T(8,128)S(1)}, f32[448,512]{1,0:T(8,128)}, u32[]{:S(2)}) copy-start(f32[448,512]{1,0:T(8,128)} %param.13) | copy-start | bytes 2752516
  156.8 31.1 %copy-start.4 = (bf16[512,448]{1,0:T(8,128)(2,1)S(1)}, bf16[512,448]{1,0:T(8,128)(2,1)}, u32[]{:S(2)}) copy-start(bf16[512,448]{1,0:T(8,128)(2,1)} %copy-done.3) | copy-start | bytes 1376260
  159.6 28.3 %copy-start.1 = (f32[448,512]{1,0:T(8,128)S(1)}, f32[448,512]{1,0:T(8,128)}, u32[]{:S(2)}) copy-start(f32[448,512]{1,0:T(8,128)} %param.12) | copy-start | bytes 2752516
  177.0 8.9 %collective-permute-start.3 = (bf16[4,136,512]{2,1,0:T(8,128)(2,1)S(1)}, bf16[4,136,512]{2,1,0:T(8,128)(2,1)S(1)}, u32[]{:S(2)}, u32[]{:S(2)}) collective-permute-start(bf16[4,136,512]{2,1,0:T(8,128)(2,1)S(1)} %bitcast.44), channel_id=1, source_target_pairs={{0,64},{64,0},{1,65},{65,1},{2,66},{66,2},{3,67},{67,3},{4,68},{68... | collective-permute-start | bytes 1671176 | tf_op jit(solution)/shard_map/ppermute | solution.py:47
Sparse Core Ops, SparseCore 0:
  10.1 58.9 all-gather.2

commit v4 on v3

v4 whole, which is shorter than its diff:
```python
import functools

import jax
import jax.numpy as jnp
from jax import lax
from jax.experimental import pallas as pl
from jax.experimental.pallas import tpu as pltpu
from jax.sharding import Mesh, PartitionSpec as P

D = 1792
LAYERS = 2

sparsity = 0.5
beta_one = 0.9
beta_two = 0.999
first_fix = 0.9999734386011124
second_fix = 0.0952078528862911
learn_rate = 0.002
adam_eps = 1e-08
sharpness = 4.0

SIZES = (4, 2, 4, 4, 4)
NAMES = ("zl", "core", "y", "x", "zh")
LAYER = ("zl", "core")
FEAT = ("y", "x", "zh")
PLANE = ("y", "x")
CORES = 2
CHIPS = 4
PARTS = 8
BLOCKS = 16
HIGH = 4
LANES = 128
BF = jnp.bfloat16
F32 = jnp.float32


def pieces(value, count):
    found = []
    for _ in range(count):
        top = value.astype(BF)
        found.append(top)
        value = value - top.astype(F32)
    return found


def spread(value, axes, count):
    copies = jnp.broadcast_to(value[None], (count,) + value.shape)
    return lax.all_to_all(copies, axes, 0, 0, tiled=True)


def swap(value):
    return lax.ppermute(value, "core", [(0, 1), (1, 0)])


def params(mebibytes):
    return pltpu.CompilerParams(vmem_limit_bytes=mebibytes * 1024 * 1024)


def start_blocks(source, held, sems, count):
    step = source.shape[0] // count
    found = []
    for k in range(count):
        rows = pl.ds(k * step, step)
        found.append(pltpu.make_async_copy(source.at[rows], held.at[rows], sems.at[k]))
    for copy in found:
        copy.start()
    return found


def decode_kernel(quarter_ref, bias_ref, dec_ref, out_ref, codes_ref, slopes_ref, held, sems):
    tokens = codes_ref.shape[0]
    step = held.shape[0] // CHIPS
    blocks = start_blocks(dec_ref, held, sems, CHIPS)
    sums = jnp.sum(quarter_ref[...].astype(F32), axis=0)[:tokens]
    scaled = sharpness * (sums + bias_ref[...])
    small = jnp.exp(-jnp.abs(scaled))
    soft = jnp.maximum(scaled, 0.0) + jnp.log1p(small)
    codes_ref[...] = (soft / sharpness).astype(BF)
    slopes_ref[...] = jnp.where(scaled >= 0.0, 1.0, small) / (1.0 + small)
    for k in range(CHIPS):
        blocks[k].wait()
        out_ref[:, k * step : (k + 1) * step] = lax.dot_general(
            codes_ref[...],
            held[k * step : (k + 1) * step],
            (((1,), (1,)), ((), ())),
            preferred_element_type=F32,
        ).astype(BF)


def whole():
    return pl.BlockSpec(memory_space=pltpu.VMEM)


def decode(quarter, enc_bias, dec_all, tokens):
    wide, latents = dec_all.shape
    return pl.pallas_call(
        decode_kernel,
        in_specs=[whole(), whole(), pl.BlockSpec(memory_space=pltpu.HBM)],
        out_specs=[whole(), whole(), whole()],
        out_shape=[
            jax.ShapeDtypeStruct((tokens, wide), BF),
            jax.ShapeDtypeStruct((tokens, latents), BF),
            jax.ShapeDtypeStruct((tokens, latents), F32),
        ],
        scratch_shapes=[pltpu.VMEM((wide, latents), BF), pltpu.SemaphoreType.DMA((CHIPS,))],
        compiler_params=params(50),
        cost_estimate=pl.CostEstimate(
            flops=2 * tokens * latents * wide,
            bytes_accessed=2 * wide * (latents + tokens),
            transcendentals=3 * tokens * latents,
        ),
        name="decode",
    )(quarter, enc_bias.reshape(1, latents), dec_all)


def row_sum(rows, first, last):
    row = lax.broadcasted_iota(jnp.int32, rows.shape, 0)
    return jnp.sum(jnp.where((row >= first) & (row < last), rows, 0.0), axis=0, keepdims=True)


def error_kernel(scale, got_ref, quarter_ref, mask_ref, out_ref):
    small, longer = got_ref.shape[1:]
    wide = longer - 2 * LANES
    left = wide // CHIPS - quarter_ref.shape[2]
    extra = quarter_ref[...][:, -3 * small :].astype(F32)
    target = []
    for chip in range(CHIPS):
        biases = extra[chip, 2 * small :]
        target.append(extra[chip, :small] - row_sum(biases, 0, 3))
        target.append((extra[chip, small : 2 * small] - row_sum(biases, 3, 6))[:, :left])
    total = jnp.sum(got_ref[...].astype(F32), axis=0)
    error = total[:, :wide] - jnp.concatenate(target, axis=1)
    squares = jnp.zeros((small, LANES), F32)
    for start in range(0, wide, LANES):
        part = error[:, start : start + LANES]
        squares = squares + part * part
    sparse = total[:, wide : wide + LANES] + total[:, wide + LANES :]
    lanes = scale * (mask_ref[...] * squares + sparsity * sparse)
    row = jnp.concatenate([(error * (2.0 * scale)).astype(BF), *pieces(lanes, 2)], axis=1)
    out_ref[...] = jnp.broadcast_to(row[None], out_ref.shape)


def error_copies(got, quarter, mask, scale):
    rows, longer = got.shape[1:]
    return pl.pallas_call(
        functools.partial(error_kernel, scale),
        out_shape=jax.ShapeDtypeStruct((BLOCKS, rows, longer), BF),
        compiler_params=params(16),
        cost_estimate=pl.CostEstimate(
            flops=10 * rows * longer, bytes_accessed=60 * rows * longer, transcendentals=0
        ),
        name="error",
    )(got, quarter, mask)


def back_kernel(scale, grad_ref, dec_ref, slopes_ref, norms_ref, out_ref, held, sems):
    wide, latents = held.shape
    step = wide // CHIPS
    blocks = start_blocks(dec_ref, held, sems, CHIPS)
    sums = jnp.sum(grad_ref[:, wide:].astype(F32), axis=0, keepdims=True)
    high, low = pieces(sums[:, :LANES] + sums[:, LANES:], 2)
    row = lax.broadcasted_iota(jnp.int32, (8, LANES), 0)
    both = jnp.where(row == 0, high.astype(F32), jnp.where(row == 1, low.astype(F32), 0.0))
    block = jnp.concatenate([both, jnp.zeros((8, latents - LANES), F32)], axis=1)
    code_grad = sparsity * scale * norms_ref[...]
    for k in range(CHIPS):
        blocks[k].wait()
        code_grad = code_grad + jnp.dot(
            grad_ref[:, k * step : (k + 1) * step],
            held[k * step : (k + 1) * step],
            preferred_element_type=F32,
        )
    out_ref[...] = jnp.concatenate([code_grad * slopes_ref[...], block], axis=0).astype(BF)


def back(grads, dec_all, slopes, norms, scale):
    tokens = grads.shape[0]
    wide, latents = dec_all.shape
    return pl.pallas_call(
        functools.partial(back_kernel, scale),
        in_specs=[whole(), pl.BlockSpec(memory_space=pltpu.HBM), whole(), whole()],
        out_specs=whole(),
        out_shape=jax.ShapeDtypeStruct((tokens + 8, latents), BF),
        scratch_shapes=[pltpu.VMEM((wide, latents), BF), pltpu.SemaphoreType.DMA((CHIPS,))],
        compiler_params=params(50),
        cost_estimate=pl.CostEstimate(
            flops=2 * tokens * latents * wide,
            bytes_accessed=2 * wide * (latents + tokens),
            transcendentals=0,
        ),
        name="back",
    )(grads, dec_all, slopes, norms.reshape(1, latents))


def body(acts, enc_weight, enc_bias, dec_weight, dec_bias, enc_moment, enc_second):
    rows, chans = acts.shape
    latents = enc_weight.shape[1]
    inv_batch = 1.0 / (rows * BLOCKS * HIGH)
    wide = PARTS * chans
    core = lax.axis_index("core")
    chip = lax.axis_index("zl")
    share = (rows + 1) // PARTS
    half = CHIPS * share
    small = HIGH * share
    tokens = BLOCKS * small

    dec_all = lax.all_gather(dec_weight.T, LAYER, axis=0, tiled=True)
    enc_there = swap(enc_weight)
    bias_there = swap(dec_bias)

    def ordered(near, far, axis):
        first, second = jnp.where(core == 0, near, far), jnp.where(core == 0, far, near)
        return jnp.concatenate([first, second], axis=axis)

    padded = jnp.concatenate([acts, jnp.zeros((1, chans), BF)], axis=0)
    low, high = padded[:half], padded[half:]
    taken = swap(jnp.where(core == 0, high, low))
    pair = ordered(jnp.where(core == 0, low, high), taken, 1)
    column = spread(pair, "zh", HIGH).reshape(HIGH, CHIPS, share, 2 * chans)
    column = column.transpose(1, 0, 2, 3).reshape(CHIPS, small, 2 * chans)
    gathered = spread(column, PLANE, BLOCKS).transpose(1, 0, 2, 3)
    gathered = gathered.reshape(CHIPS * tokens, 2 * chans)
    first_half, second_half = gathered[:, :chans], gathered[:, chans:]
    acts_here = jnp.where(core == 0, first_half, second_half)
    acts_there = swap(jnp.where(core == 0, second_half, first_half))

    enc_pair = ordered(enc_weight, enc_there, 0)
    sums = jnp.dot(gathered, enc_pair, preferred_element_type=F32).astype(BF)

    def folded(rows_of):
        fill = [(0, 0)] * (rows_of.ndim - 1) + [(0, 2 * latents - 2 * chans)]
        rest = jnp.pad(rows_of[..., latents:], fill)
        return jnp.concatenate([rows_of[..., :latents], rest], axis=-2)

    bias_rows = folded(jnp.stack(pieces(ordered(dec_bias, bias_there, 0), 3)))
    bias_rows = jnp.pad(bias_rows, ((0, small - 6), (0, 0)))
    bias_rows = jnp.broadcast_to(bias_rows[None], (CHIPS, small, latents))
    extra = jnp.concatenate([folded(column), bias_rows], axis=1)
    sending = jnp.concatenate([sums.reshape(CHIPS, tokens, latents), extra], axis=1)
    quarter = lax.all_to_all(sending, "zl", 0, 0, tiled=True)
    partial_value, codes, slopes = decode(quarter, enc_bias, dec_all, tokens)

    dec_norms = jnp.zeros((latents,), F32)
    for layer in range(LAYERS):
        block = dec_all[layer * (wide // LAYERS) : (layer + 1) * (wide // LAYERS)].astype(F32)
        dec_norms = dec_norms + jnp.sqrt(jnp.sum(block * block, axis=0))

    place = lax.broadcasted_iota(jnp.int32, (small, LANES), 0) % share
    real = (core * half + chip * share + place < rows).astype(F32)
    weighed = jnp.sum((codes.astype(F32) * dec_norms).reshape(BLOCKS, small, latents), axis=0)
    sparse = real * sum(weighed[:, k : k + LANES] for k in range(0, latents, LANES))

    got = lax.all_to_all(
        partial_value.reshape(BLOCKS, small, wide), PLANE, 0, 0, tiled=True
    )
    summed = jnp.sum(got.astype(F32), axis=0).astype(BF)
    again = spread(jnp.concatenate([summed, *pieces(sparse, 2)], axis=1), "zh", HIGH)
    again, acts_there = lax.optimization_barrier((again, acts_there))
    copies = error_copies(again, quarter, real, inv_batch)
    grads = lax.all_to_all(copies, PLANE, 0, 0, tiled=True)
    last = back(grads.reshape(tokens, wide + 2 * LANES), dec_all, slopes, dec_norms, inv_batch)
    pre_here = lax.all_gather(last, "zl", axis=0)
    pre_there = swap(pre_here)

    def part_of(acts_half, pre_half):
        longer = jnp.pad(acts_half.reshape(CHIPS, tokens, chans), ((0, 0), (0, 8), (0, 0)))
        return lax.dot_general(
            longer.reshape(-1, chans),
            pre_half.reshape(-1, latents),
            (((0,), (0,)), ((), ())),
            preferred_element_type=F32,
        )

    near = pre_here[:, tokens : tokens + 2, :LANES].astype(F32)
    far = pre_there[:, tokens : tokens + 2, :LANES].astype(F32)
    first, second = jnp.where(core == 0, near, far), jnp.where(core == 0, far, near)
    total_loss = jnp.sum(first + second)
    gradient = part_of(acts_here, pre_here) + part_of(acts_there, pre_there)
    moment_new = beta_one * enc_moment + (1.0 - beta_one) * gradient
    second_new = beta_two * enc_second + (1.0 - beta_two) * gradient * gradient
    update = moment_new / first_fix / (jnp.sqrt(second_new / second_fix) + adam_eps)
    enc_new = (enc_weight.astype(F32) - learn_rate * update).astype(BF)
    return (enc_new, moment_new, second_new, total_loss)


def solution(mesh):
    fine = Mesh(mesh.devices.reshape(SIZES), NAMES)
    return jax.shard_map(
        body,
        mesh=fine,
        in_specs=(
            P(FEAT, LAYER),
            P(LAYER, FEAT),
            P(FEAT),
            P(FEAT, LAYER),
            P(LAYER),
            P(LAYER, FEAT),
            P(LAYER, FEAT),
        ),
        out_specs=(P(LAYER, FEAT), P(LAYER, FEAT), P(LAYER, FEAT), P()),
        check_vma=False,
    )
```

time: 201 us -> 189 us (0.940)
  blocking collectives: 17.4 us -> 32 us
  waiting for transfers between devices: 70.3 us -> 60.3 us
  matrix products: 13.3 us -> 3.8 us
  between operations: 20.9 us -> 14.4 us
  Pallas kernels: 0 us -> 6.41 us
  other arithmetic: 9.51 us -> 6.81 us
    all_to_all x4 -> x3, waiting for transfers between devices: 49.8 us -> 29.9 us  [spread(): return lax.all_to_all(copies, axes, 0, 0, tiled=True)]
    all_to_all x0 -> x1, blocking collectives: none -> 15.4 us  [body(): grads = lax.all_to_all(copies, PLANE, 0, 0, tiled=True)]
    dot_general x2 -> x0, matrix products: 7.21 us -> none  [the longest x1 4.42 us: body(): lax.dot_general(codes, dec_all, (((1,), (1,)), ((), ())), preferred_eleme...]
    pallas_call x0 -> x3, Pallas kernels: none -> 6.41 us  [the longest x1 3.96 us: decode(): pl.pallas_call(decode_kernel, in_specs=[whole(), whole(), pl.BlockSpec(me...]
    all_to_all x1, waiting for transfers between devices: 9.62 us -> 15.1 us  [body(): quarter = lax.all_to_all(sending, 'zl', 0, 0, tiled=True)]
    all_to_all x4 -> x3, starting transfers between devices: 29.1 us -> 25.5 us  [spread(): return lax.all_to_all(copies, axes, 0, 0, tiled=True)]
    ppermute x4 -> x5, waiting for transfers between devices: 0.88 us -> 3.25 us  [swap(): return lax.ppermute(value, 'core', [(0, 1), (1, 0)])]
    dot_general x2, matrix products: 5.37 us -> 3.1 us  [part_of(): lax.dot_general(longer.reshape(-1, chans), pre_half.reshape(-1, latents),...]
  transfers between devices with their start and end apart: 11 -> 11, of which waited for: 8 -> 8; matrix products, arithmetic and copies ran while one was open for 6% -> 5% of each run, Pallas kernels for 0% -> 0%
where the time goes in v4:
time: 189 us
  starting transfers between devices  62.4 us (33%)
  waiting for transfers between devices  60.3 us (32%)
  blocking collectives  32 us (17%)
  between operations  14.4 us (8%)
  other arithmetic  6.81 us (4%)
  Pallas kernels  6.41 us (3%)
  matrix products  3.8 us (2%)
  local copies, waits for them, and re-layouts  2.58 us (1%)
    all_to_all x3, waiting for transfers between devices, spread(): return lax.all_to_all(copies, axes, 0, 0, tiled=True)  29.9 us
    ppermute x5, starting transfers between devices, swap(): return lax.ppermute(value, 'core', [(0, 1), (1, 0)])  25.8 us
    all_to_all x3, starting transfers between devices, spread(): return lax.all_to_all(copies, axes, 0, 0, tiled=True)  25.5 us
    all_gather x1, blocking collectives, body(): pre_here = lax.all_gather(last, 'zl', axis=0)  16.6 us
    all_to_all x1, blocking collectives, body(): grads = lax.all_to_all(copies, PLANE, 0, 0, tiled=True)  15.4 us
    all_to_all x1, waiting for transfers between devices, body(): quarter = lax.all_to_all(sending, 'zl', 0, 0, tiled=True)  15.1 us
    all_to_all x1, waiting for transfers between devices, body(): lax.all_to_all(partial_value.reshape(BLOCKS, small, wide), PLANE, 0, 0, t...  11.4 us
    all_to_all x1, starting transfers between devices, body(): lax.all_to_all(partial_value.reshape(BLOCKS, small, wide), PLANE, 0, 0, t...  7.53 us
  transfers between devices with their start and end apart: 11, of which 8 were waited for; matrix products, arithmetic and copies ran while one was open for 5% of the time, Pallas kernels for 0%

profile of v4, /device:TPU:1, one launch (start us, length us, event | category | flops | bytes accessed | tf_op | source)
XLA Modules:
  0.0 188.6 jit_solution(14222684386584248923)
XLA Ops:
  8.7 8.8 %collective-permute-start = (bf16[8,448]{1,0:T(8,128)(2,1)S(1)}, bf16[8,448]{1,0:T(8,128)(2,1)S(1)}, u32[]{:S(2)}, u32[]{:S(2)}) collective-permute-start(bf16[8,448]{1,0:T(8,128)(2,1)S(1)} %broadcast_select_fusion.6), channel_id=1, source_target_pairs={{0,64},{64,0},{1,65},{65,1},{2,66},{66,2},{3,67},{67,3},{4,68},{68... | collective-permute-start | bytes 21512 | tf_op jit(solution)/shard_map/ppermute | solution.py:52
  19.8 9.4 %all-to-all-start = ((bf16[4,8,896]{2,1,0:T(8,128)(2,1)}), bf16[4,8,896]{2,1,0:T(8,128)(2,1)S(1)}, u32[]{:S(2)}, u32[]{:S(2)}) async-start(bf16[4,8,896]{2,1,0:T(8,128)(2,1)} %broadcast_in_dim.10), calls=%async_computation | async-start | bytes 114688 | tf_op jit(solution)/shard_map/all_to_all | solution.py:48
  29.2 2.5 %collective-permute-start.2 = (f32[448]{0:T(512)}, f32[448]{0:T(512)S(1)}, u32[]{:S(2)}, u32[]{:S(2)}) collective-permute-start(f32[448]{0:T(512)} %param.11), channel_id=1, source_target_pairs={{0,64},{64,0},{1,65},{65,1},{2,66},{66,2},{3,67},{67,3},{4,68},{68... | collective-permute-start | bytes 5384 | tf_op jit(solution)/shard_map/ppermute | solution.py:52
  31.8 1.9 %collective-permute-start.1 = (bf16[448,512]{1,0:T(8,128)(2,1)}, bf16[448,512]{1,0:T(8,128)(2,1)S(1)}, u32[]{:S(2)}, u32[]{:S(2)}) collective-permute-start(bf16[448,512]{1,0:T(8,128)(2,1)} %param.8), channel_id=1, source_target_pairs={{0,64},{64,0},{1,65},{65,1},{2,66},{66,2},{3,67},{67,3},{4,68},{68... | collective-permute-start | bytes 1376264 | tf_op jit(solution)/shard_map/ppermute | solution.py:52
  33.7 7.5 %all-to-all-done = bf16[4,8,896]{2,1,0:T(8,128)(2,1)S(1)} async-done(((bf16[4,8,896]{2,1,0:T(8,128)(2,1)}), bf16[4,8,896]{2,1,0:T(8,128)(2,1)S(1)}, u32[]{:S(2)}, u32[]{:S(2)}) %all-to-all-start) | async-done | bytes 57376 | tf_op jit(solution)/shard_map/all_to_all | solution.py:48
  41.3 1.0 broadcast_in_dim.12
  42.3 6.8 %all-to-all-start.1 = ((bf16[16,4,8,896]{3,2,1,0:T(8,128)(2,1)}), bf16[16,4,8,896]{3,2,1,0:T(8,128)(2,1)S(1)}, u32[]{:S(2)}, u32[]{:S(2)}) async-start(bf16[16,4,8,896]{3,2,1,0:T(8,128)(2,1)} %broadcast_in_dim.12), calls=%async_computation.1 | async-start | bytes 1835008 | tf_op jit(solution)/shard_map/all_to_all | solution.py:48
  49.4 13.3 %all-to-all-done.1 = bf16[16,4,8,896]{3,2,1,0:T(8,128)(2,1)S(1)} async-done(((bf16[16,4,8,896]{3,2,1,0:T(8,128)(2,1)}), bf16[16,4,8,896]{3,2,1,0:T(8,128)(2,1)S(1)}, u32[]{:S(2)}, u32[]{:S(2)}) %all-to-all-start.1) | async-done | bytes 917536 | tf_op jit(solution)/shard_map/all_to_all | solution.py:48
  64.5 3.5 %all-to-all-start.2 = ((bf16[4,152,512]{2,1,0:T(8,128)(2,1)}), bf16[4,152,512]{2,1,0:T(8,128)(2,1)S(1)}, u32[]{:S(2)}, u32[]{:S(2)}) async-start(bf16[4,152,512]{2,1,0:T(8,128)(2,1)} %fusion.8), calls=%async_computation.2 | async-start | bytes 1245184 | tf_op jit(solution)/shard_map/all_to_all | solution.py:240
  68.0 15.1 %all-to-all-done.2.quarter_ref = bf16[4,152,512]{2,1,0:T(8,128)(2,1)S(1)} async-done(((bf16[4,152,512]{2,1,0:T(8,128)(2,1)}), bf16[4,152,512]{2,1,0:T(8,128)(2,1)S(1)}, u32[]{:S(2)}, u32[]{:S(2)}) %all-to-all-start.2) | async-done | bytes 622624 | tf_op jit(solution)/shard_map/all_to_all | solution.py:240
  83.1 4.0 %decode.1 = (bf16[128,3584]{1,0:T(8,128)(2,1)}, bf16[128,512]{1,0:T(8,128)(2,1)S(1)}, f32[128,512]{1,0:T(8,128)S(1)}) custom-call(bf16[4,152,512]{2,1,0:T(8,128)(2,1)S(1)} %all-to-all-done.2.quarter_ref, f32[1,512]{1,0:T(1,128)S(1)} %bitcast.30, bf16[3584,512]{1,0:T(8,128)(2,1)} %all-gather.3.cloned.1.call-done.dec_ref), custom_call_target="tpu_custom_call" | custom-call | flops 469762048 | bytes 4587520 | tf_op jit(solution)/shard_map/decode/pallas_call | solution.py:96
  87.0 7.5 %all-to-all-start.3 = ((bf16[16,8,3584]{2,1,0:T(8,128)(2,1)}), bf16[16,8,3584]{2,1,0:T(8,128)(2,1)S(1)}, u32[]{:S(2)}, u32[]{:S(2)}) async-start(bf16[16,8,3584]{2,1,0:T(8,128)(2,1)} %bitcast.11), calls=%async_computation.3 | async-start | bytes 1835008 | tf_op jit(solution)/shard_map/all_to_all | solution.py:253
  94.6 2.8 %multiply_reduce_fusion.1 = (f32[512]{0:T(512)S(1)}, f32[512]{0:T(512)S(1)}) fusion(bf16[3584,512]{1,0:T(8,128)(2,1)} %all-gather.3.cloned.1.call-done.dec_ref), kind=kLoop, calls=%fused_computation.1 | loop fusion | flops 5504000 | bytes 3674112 | tf_op jit(solution)/shard_map/reduce_sum | solution.py:246
  97.5 11.4 %all-to-all-done.3 = bf16[16,8,3584]{2,1,0:T(8,128)(2,1)S(1)} async-done(((bf16[16,8,3584]{2,1,0:T(8,128)(2,1)}), bf16[16,8,3584]{2,1,0:T(8,128)(2,1)S(1)}, u32[]{:S(2)}, u32[]{:S(2)}) %all-to-all-start.3) | async-done | bytes 917536 | tf_op jit(solution)/shard_map/all_to_all | solution.py:253
  109.7 9.3 %all-to-all-start.4 = ((bf16[4,8,3840]{2,1,0:T(8,128)(2,1)}), bf16[4,8,3840]{2,1,0:T(8,128)(2,1)S(1)}, u32[]{:S(2)}, u32[]{:S(2)}) async-start(bf16[4,8,3840]{2,1,0:T(8,128)(2,1)} %broadcast_in_dim.14), calls=%async_computation.4 | async-start | bytes 491520 | tf_op jit(solution)/shard_map/all_to_all | solution.py:48
  119.3 4.6 %collective-permute-start.3 = (bf16[512,448]{1,0:T(8,128)(2,1)S(1)}, bf16[512,448]{1,0:T(8,128)(2,1)S(1)}, u32[]{:S(2)}, u32[]{:S(2)}) collective-permute-start(bf16[512,448]{1,0:T(8,128)(2,1)S(1)} %get-tuple-element.22), channel_id=1, source_target_pairs={{0,64},{64,0},{1,65},{65,1},{2,66},{66,2},{3,67},{67,3},{4,68},{68... | collective-permute-start | bytes 1376264 | tf_op jit(solution)/shard_map/ppermute | solution.py:52
  124.0 1.4 collective-permute-done.3
  125.4 9.1 %all-to-all-done.4.got_ref = bf16[4,8,3840]{2,1,0:T(8,128)(2,1)S(1)} async-done(((bf16[4,8,3840]{2,1,0:T(8,128)(2,1)}), bf16[4,8,3840]{2,1,0:T(8,128)(2,1)S(1)}, u32[]{:S(2)}, u32[]{:S(2)}) %all-to-all-start.4) | async-done | bytes 245792 | tf_op jit(solution)/shard_map/all_to_all | solution.py:48
  134.7 15.4 %all_to_all.30 = bf16[16,8,3840]{2,1,0:T(8,128)(2,1)S(1)} all-to-all(bf16[16,8,3840]{2,1,0:T(8,128)(2,1)S(1)} %error.1), channel_id=1, replica_groups=mesh['zl'=4,'core'=2,'y'=4,'x'=4,'zh'=4] {'y','x'}, dimensions={0} | all-to-all | bytes 1966080 | tf_op jit(solution)/shard_map/all_to_all | solution.py:260
  150.0 2.4 %back.1 = bf16[136,512]{1,0:T(8,128)(2,1)S(1)} custom-call(bf16[128,3840]{1,0:T(8,128)(2,1)S(1)} %bitcast.28, bf16[3584,512]{1,0:T(8,128)(2,1)} %all-gather.3.cloned.1.call-done.dec_ref, f32[128,512]{1,0:T(8,128)S(1)} %get-tuple-element.12.slopes_ref, f32[1,512]{1,0:T(1,128)S(1)} %bitcast.29), custom_call_target="tpu_custom_call" | custom-call | flops 469762048 | bytes 4587520 | tf_op jit(solution)/shard_map/back/pallas_call | solution.py:179
  152.4 16.6 %all-gather = bf16[544,512]{1,0:T(8,128)(2,1)S(1)} all-gather(bf16[136,512]{1,0:T(8,128)(2,1)S(1)} %back.1), channel_id=2, replica_groups=mesh['zl'=4,'core'=2,'y'=4,'x'=4,'zh'=4] {'zl'}, dimensions={0}, use_global_device_ids=true | all-gather | bytes 696320 | tf_op jit(solution)/shard_map/all_gather | solution.py:262
  169.0 8.0 %collective-permute-start.4 = (bf16[4,136,512]{2,1,0:T(8,128)(2,1)S(1)}, bf16[4,136,512]{2,1,0:T(8,128)(2,1)S(1)}, u32[]{:S(2)}, u32[]{:S(2)}) collective-permute-start(bf16[4,136,512]{2,1,0:T(8,128)(2,1)S(1)} %bitcast.33), channel_id=1, source_target_pairs={{0,64},{64,0},{1,65},{65,1},{2,66},{66,2},{3,67},{67,3},{4,68},{68... | collective-permute-start | bytes 1671176 | tf_op jit(solution)/shard_map/ppermute | solution.py:52
  177.6 1.0 collective-permute-done.4
  179.2 2.5 %subtract_convert_fusion = (bf16[448,512]{1,0:T(8,128)(2,1)}, f32[448,512]{1,0:T(8,128)}, f32[448,512]{1,0:T(8,128)}) fusion(bf16[448,512]{1,0:T(8,128)(2,1)S(1)} %copy-done.2, f32[448,512]{1,0:T(8,128)S(1)} %copy-done.4, f32[448,512]{1,0:T(8,128)S(1)} %copy-done.5, f32[448,512]{1,0:T(8,128)S(1)} %convolution_bitcast_fusion.1, ...), kind=kOutput, calls=%fused_computation.15 | convolution fusion | flops 253231104 | bytes 6520832 | tf_op jit(solution)/shard_map/dot_general | solution.py:267
  (54 shorter events, 8.5 us)
Async XLA Ops:
  7.2 75.9 %all-gather.3.cloned.1.call-start = ((), (), s32[]{:S(2)}) async-start(), calls=%async_computation.6 | async-start | bytes 4128768 | tf_op jit(solution)/shard_map/all_gather | solution.py:207
  7.9 41.1 %copy-start.3 = (f32[448]{0:T(512)S(1)}, f32[448]{0:T(512)}, u32[]{:S(2)}) copy-start(f32[448]{0:T(512)} %param.11) | copy-start | bytes 5380
  7.9 41.4 %copy-start.2 = (bf16[448,512]{1,0:T(8,128)(2,1)S(1)}, bf16[448,512]{1,0:T(8,128)(2,1)}, u32[]{:S(2)}) copy-start(bf16[448,512]{1,0:T(8,128)(2,1)} %param.8) | copy-start | bytes 1376260
  8.7 9.6 %collective-permute-start = (bf16[8,448]{1,0:T(8,128)(2,1)S(1)}, bf16[8,448]{1,0:T(8,128)(2,1)S(1)}, u32[]{:S(2)}, u32[]{:S(2)}) collective-permute-start(bf16[8,448]{1,0:T(8,128)(2,1)S(1)} %broadcast_select_fusion.6), channel_id=1, source_target_pairs={{0,64},{64,0},{1,65},{65,1},{2,66},{66,2},{3,67},{67,3},{4,68},{68... | collective-permute-start | bytes 21512 | tf_op jit(solution)/shard_map/ppermute | solution.py:52
  19.8 21.3 %all-to-all-start = ((bf16[4,8,896]{2,1,0:T(8,128)(2,1)}), bf16[4,8,896]{2,1,0:T(8,128)(2,1)S(1)}, u32[]{:S(2)}, u32[]{:S(2)}) async-start(bf16[4,8,896]{2,1,0:T(8,128)(2,1)} %broadcast_in_dim.10), calls=%async_computation | async-start | bytes 114688 | tf_op jit(solution)/shard_map/all_to_all | solution.py:48
  29.2 19.8 %collective-permute-start.2 = (f32[448]{0:T(512)}, f32[448]{0:T(512)S(1)}, u32[]{:S(2)}, u32[]{:S(2)}) collective-permute-start(f32[448]{0:T(512)} %param.11), channel_id=1, source_target_pairs={{0,64},{64,0},{1,65},{65,1},{2,66},{66,2},{3,67},{67,3},{4,68},{68... | collective-permute-start | bytes 5384 | tf_op jit(solution)/shard_map/ppermute | solution.py:52
  31.8 17.5 %collective-permute-start.1 = (bf16[448,512]{1,0:T(8,128)(2,1)}, bf16[448,512]{1,0:T(8,128)(2,1)S(1)}, u32[]{:S(2)}, u32[]{:S(2)}) collective-permute-start(bf16[448,512]{1,0:T(8,128)(2,1)} %param.8), channel_id=1, source_target_pairs={{0,64},{64,0},{1,65},{65,1},{2,66},{66,2},{3,67},{67,3},{4,68},{68... | collective-permute-start | bytes 1376264 | tf_op jit(solution)/shard_map/ppermute | solution.py:52
  41.3 8.2 %copy-start.1 = (bf16[4,8,896]{2,1,0:T(8,128)(2,1)}, bf16[4,8,896]{2,1,0:T(8,128)(2,1)S(1)}, u32[]{:S(2)}) copy-start(bf16[4,8,896]{2,1,0:T(8,128)(2,1)S(1)} %broadcast_in_dim.11) | copy-start | bytes 172036
  42.3 20.5 %all-to-all-start.1 = ((bf16[16,4,8,896]{3,2,1,0:T(8,128)(2,1)}), bf16[16,4,8,896]{3,2,1,0:T(8,128)(2,1)S(1)}, u32[]{:S(2)}, u32[]{:S(2)}) async-start(bf16[16,4,8,896]{3,2,1,0:T(8,128)(2,1)} %broadcast_in_dim.12), calls=%async_computation.1 | async-start | bytes 1835008 | tf_op jit(solution)/shard_map/all_to_all | solution.py:48
  62.8 0.8 slice-start
  62.8 0.8 slice-start.1
  63.6 19.5 %copy-start = (f32[512]{0:T(512)S(1)}, f32[512]{0:T(512)}, u32[]{:S(2)}) copy-start(f32[512]{0:T(512)} %param.9) | copy-start | bytes 6148
  64.5 18.6 %all-to-all-start.2 = ((bf16[4,152,512]{2,1,0:T(8,128)(2,1)}), bf16[4,152,512]{2,1,0:T(8,128)(2,1)S(1)}, u32[]{:S(2)}, u32[]{:S(2)}) async-start(bf16[4,152,512]{2,1,0:T(8,128)(2,1)} %fusion.8), calls=%async_computation.2 | async-start | bytes 1245184 | tf_op jit(solution)/shard_map/all_to_all | solution.py:240
  87.0 21.9 %all-to-all-start.3 = ((bf16[16,8,3584]{2,1,0:T(8,128)(2,1)}), bf16[16,8,3584]{2,1,0:T(8,128)(2,1)S(1)}, u32[]{:S(2)}, u32[]{:S(2)}) async-start(bf16[16,8,3584]{2,1,0:T(8,128)(2,1)} %bitcast.11), calls=%async_computation.3 | async-start | bytes 1835008 | tf_op jit(solution)/shard_map/all_to_all | solution.py:253
  109.7 24.8 %all-to-all-start.4 = ((bf16[4,8,3840]{2,1,0:T(8,128)(2,1)}), bf16[4,8,3840]{2,1,0:T(8,128)(2,1)S(1)}, u32[]{:S(2)}, u32[]{:S(2)}) async-start(bf16[4,8,3840]{2,1,0:T(8,128)(2,1)} %broadcast_in_dim.14), calls=%async_computation.4 | async-start | bytes 491520 | tf_op jit(solution)/shard_map/all_to_all | solution.py:48
  119.3 6.1 %collective-permute-start.3 = (bf16[512,448]{1,0:T(8,128)(2,1)S(1)}, bf16[512,448]{1,0:T(8,128)(2,1)S(1)}, u32[]{:S(2)}, u32[]{:S(2)}) collective-permute-start(bf16[512,448]{1,0:T(8,128)(2,1)S(1)} %get-tuple-element.22), channel_id=1, source_target_pairs={{0,64},{64,0},{1,65},{65,1},{2,66},{66,2},{3,67},{67,3},{4,68},{68... | collective-permute-start | bytes 1376264 | tf_op jit(solution)/shard_map/ppermute | solution.py:52
  152.4 26.8 %copy-start.4 = (f32[448,512]{1,0:T(8,128)S(1)}, f32[448,512]{1,0:T(8,128)}, u32[]{:S(2)}) copy-start(f32[448,512]{1,0:T(8,128)} %param.12) | copy-start | bytes 2752516
  152.4 26.8 %copy-start.5 = (f32[448,512]{1,0:T(8,128)S(1)}, f32[448,512]{1,0:T(8,128)}, u32[]{:S(2)}) copy-start(f32[448,512]{1,0:T(8,128)} %param.13) | copy-start | bytes 2752516
  169.0 9.5 %collective-permute-start.4 = (bf16[4,136,512]{2,1,0:T(8,128)(2,1)S(1)}, bf16[4,136,512]{2,1,0:T(8,128)(2,1)S(1)}, u32[]{:S(2)}, u32[]{:S(2)}) collective-permute-start(bf16[4,136,512]{2,1,0:T(8,128)(2,1)S(1)} %bitcast.33), channel_id=1, source_target_pairs={{0,64},{64,0},{1,65},{65,1},{2,66},{66,2},{3,67},{67,3},{4,68},{68... | collective-permute-start | bytes 1671176 | tf_op jit(solution)/shard_map/ppermute | solution.py:52
Sparse Core Ops, SparseCore 0:
  10.1 59.0 all-gather.2

commit v5 on v4

--- a/solution.py
+++ b/solution.py
@@ -68,10 +68,9 @@
 
 
 def decode_kernel(quarter_ref, bias_ref, dec_ref, out_ref, codes_ref, slopes_ref, held, sems):
-    tokens = codes_ref.shape[0]
     step = held.shape[0] // CHIPS
     blocks = start_blocks(dec_ref, held, sems, CHIPS)
-    sums = jnp.sum(quarter_ref[...].astype(F32), axis=0)[:tokens]
+    sums = jnp.sum(quarter_ref[...].astype(F32), axis=0)
     scaled = sharpness * (sums + bias_ref[...])
     small = jnp.exp(-jnp.abs(scaled))
     soft = jnp.maximum(scaled, 0.0) + jnp.log1p(small)
@@ -118,11 +117,11 @@
     return jnp.sum(jnp.where((row >= first) & (row < last), rows, 0.0), axis=0, keepdims=True)
 
 
-def error_kernel(scale, got_ref, quarter_ref, mask_ref, out_ref):
+def error_kernel(scale, got_ref, extra_ref, mask_ref, out_ref):
     small, longer = got_ref.shape[1:]
-    wide = longer - 2 * LANES
-    left = wide // CHIPS - quarter_ref.shape[2]
-    extra = quarter_ref[...][:, -3 * small :].astype(F32)
+    wide = longer - LANES
+    left = wide // CHIPS - extra_ref.shape[2]
+    extra = extra_ref[...].astype(F32)
     target = []
     for chip in range(CHIPS):
         biases = extra[chip, 2 * small :]
@@ -134,13 +133,12 @@
     for start in range(0, wide, LANES):
         part = error[:, start : start + LANES]
         squares = squares + part * part
-    sparse = total[:, wide : wide + LANES] + total[:, wide + LANES :]
-    lanes = scale * (mask_ref[...] * squares + sparsity * sparse)
-    row = jnp.concatenate([(error * (2.0 * scale)).astype(BF), *pieces(lanes, 2)], axis=1)
+    lanes = scale * (mask_ref[...] * squares + sparsity * total[:, wide:])
+    row = jnp.concatenate([error * (2.0 * scale), lanes], axis=1).astype(BF)
     out_ref[...] = jnp.broadcast_to(row[None], out_ref.shape)
 
 
-def error_copies(got, quarter, mask, scale):
+def error_copies(got, extra, mask, scale):
     rows, longer = got.shape[1:]
     return pl.pallas_call(
         functools.partial(error_kernel, scale),
@@ -150,7 +148,7 @@
             flops=10 * rows * longer, bytes_accessed=60 * rows * longer, transcendentals=0
         ),
         name="error",
-    )(got, quarter, mask)
+    )(got, extra, mask)
 
 
 def back_kernel(scale, grad_ref, dec_ref, slopes_ref, norms_ref, out_ref, held, sems):
@@ -158,7 +156,7 @@
     step = wide // CHIPS
     blocks = start_blocks(dec_ref, held, sems, CHIPS)
     sums = jnp.sum(grad_ref[:, wide:].astype(F32), axis=0, keepdims=True)
-    high, low = pieces(sums[:, :LANES] + sums[:, LANES:], 2)
+    high, low = pieces(sums, 2)
     row = lax.broadcasted_iota(jnp.int32, (8, LANES), 0)
     both = jnp.where(row == 0, high.astype(F32), jnp.where(row == 1, low.astype(F32), 0.0))
     block = jnp.concatenate([both, jnp.zeros((8, latents - LANES), F32)], axis=1)
@@ -213,19 +211,13 @@
         return jnp.concatenate([first, second], axis=axis)
 
     padded = jnp.concatenate([acts, jnp.zeros((1, chans), BF)], axis=0)
-    low, high = padded[:half], padded[half:]
-    taken = swap(jnp.where(core == 0, high, low))
-    pair = ordered(jnp.where(core == 0, low, high), taken, 1)
-    column = spread(pair, "zh", HIGH).reshape(HIGH, CHIPS, share, 2 * chans)
-    column = column.transpose(1, 0, 2, 3).reshape(CHIPS, small, 2 * chans)
+    halves = jnp.broadcast_to(padded.reshape(CORES, 1, half, chans), (CORES, HIGH, half, chans))
+    halves = halves.reshape(CORES * HIGH, half, chans)
+    column = lax.all_to_all(halves, ("core", "zh"), 0, 0, tiled=True)
+    column = column.reshape(CORES, HIGH, CHIPS, share, chans).transpose(2, 1, 3, 0, 4)
+    column = column.reshape(CHIPS, small, 2 * chans)
     gathered = spread(column, PLANE, BLOCKS).transpose(1, 0, 2, 3)
     gathered = gathered.reshape(CHIPS * tokens, 2 * chans)
-    first_half, second_half = gathered[:, :chans], gathered[:, chans:]
-    acts_here = jnp.where(core == 0, first_half, second_half)
-    acts_there = swap(jnp.where(core == 0, second_half, first_half))
-
-    enc_pair = ordered(enc_weight, enc_there, 0)
-    sums = jnp.dot(gathered, enc_pair, preferred_element_type=F32).astype(BF)
 
     def folded(rows_of):
         fill = [(0, 0)] * (rows_of.ndim - 1) + [(0, 2 * latents - 2 * chans)]
@@ -236,8 +228,22 @@
     bias_rows = jnp.pad(bias_rows, ((0, small - 6), (0, 0)))
     bias_rows = jnp.broadcast_to(bias_rows[None], (CHIPS, small, latents))
     extra = jnp.concatenate([folded(column), bias_rows], axis=1)
-    sending = jnp.concatenate([sums.reshape(CHIPS, tokens, latents), extra], axis=1)
-    quarter = lax.all_to_all(sending, "zl", 0, 0, tiled=True)
+    came = []
+    for away in range(CHIPS):
+        block = lax.dynamic_index_in_dim(extra, (chip + away) & (CHIPS - 1), 0)
+        ways = [(i, (i + away) % CHIPS) for i in range(CHIPS)]
+        came.append(lax.ppermute(block, "zl", ways) if away else block)
+    gathered, *came = lax.optimization_barrier((gathered, *came))
+    turned = jnp.concatenate([came[-k % CHIPS] for k in range(2 * CHIPS - 1)], axis=0)
+    mine = lax.dynamic_slice_in_dim(turned, (CHIPS - chip) & (CHIPS - 1), CHIPS, axis=0)
+
+    first_half, second_half = gathered[:, :chans], gathered[:, chans:]
+    acts_here = jnp.where(core == 0, first_half, second_half)
+    acts_there = swap(jnp.where(core == 0, second_half, first_half))
+
+    enc_pair = ordered(enc_weight, enc_there, 0)
+    sums = jnp.dot(gathered, enc_pair, preferred_element_type=F32).astype(BF)
+    quarter = lax.all_to_all(sums.reshape(CHIPS, tokens, latents), "zl", 0, 0, tiled=True)
     partial_value, codes, slopes = decode(quarter, enc_bias, dec_all, tokens)
 
     dec_norms = jnp.zeros((latents,), F32)
@@ -245,7 +251,7 @@
         block = dec_all[layer * (wide // LAYERS) : (layer + 1) * (wide // LAYERS)].astype(F32)
         dec_norms = dec_norms + jnp.sqrt(jnp.sum(block * block, axis=0))
 
-    place = lax.broadcasted_iota(jnp.int32, (small, LANES), 0) % share
+    place = lax.broadcasted_iota(jnp.int32, (small, LANES), 0) & (share - 1)
     real = (core * half + chip * share + place < rows).astype(F32)
     weighed = jnp.sum((codes.astype(F32) * dec_norms).reshape(BLOCKS, small, latents), axis=0)
     sparse = real * sum(weighed[:, k : k + LANES] for k in range(0, latents, LANES))
@@ -254,11 +260,11 @@
         partial_value.reshape(BLOCKS, small, wide), PLANE, 0, 0, tiled=True
     )
     summed = jnp.sum(got.astype(F32), axis=0).astype(BF)
-    again = spread(jnp.concatenate([summed, *pieces(sparse, 2)], axis=1), "zh", HIGH)
+    again = spread(jnp.concatenate([summed, sparse.astype(BF)], axis=1), "zh", HIGH)
     again, acts_there = lax.optimization_barrier((again, acts_there))
-    copies = error_copies(again, quarter, real, inv_batch)
+    copies = error_copies(again, mine, real, inv_batch)
     grads = lax.all_to_all(copies, PLANE, 0, 0, tiled=True)
-    last = back(grads.reshape(tokens, wide + 2 * LANES), dec_all, slopes, dec_norms, inv_batch)
+    last = back(grads.reshape(tokens, wide + LANES), dec_all, slopes, dec_norms, inv_batch)
     pre_here = lax.all_gather(last, "zl", axis=0)
     pre_there = swap(pre_here)
 

time: 189 us -> 187 us (0.989)
  waiting for transfers between devices: 60.3 us -> 46.3 us
  starting transfers between devices: 62.4 us -> 67.3 us
  matrix products: 3.8 us -> 6.83 us
  blocking collectives: 32 us -> 34.8 us
    all_to_all x1 -> x2, starting transfers between devices: 3.48 us -> 21.4 us  [the longest x1 16.6 us: body(): column = lax.all_to_all(halves, ('core', 'zh'), 0, 0, tiled=True)]
    all_to_all x3 -> x2, waiting for transfers between devices: 29.9 us -> 15.9 us  [spread(): return lax.all_to_all(copies, axes, 0, 0, tiled=True)]
    all_to_all x3 -> x2, starting transfers between devices: 25.5 us -> 13.6 us  [spread(): return lax.all_to_all(copies, axes, 0, 0, tiled=True)]
    ppermute x5 -> x4, starting transfers between devices: 25.8 us -> 15.1 us  [swap(): return lax.ppermute(value, 'core', [(0, 1), (1, 0)])]
    ppermute x0 -> x3, starting transfers between devices: none -> 10.4 us  [body(): came.append(lax.ppermute(block, 'zl', ways) if away else block)]
    all_to_all x1, blocking collectives: 15.4 us -> 19.4 us  [body(): grads = lax.all_to_all(copies, PLANE, 0, 0, tiled=True)]
    all_to_all x1 -> x2, waiting for transfers between devices: 15.1 us -> 17.4 us  [the longest x1 9.95 us: body(): lax.all_to_all(sums.reshape(CHIPS, tokens, latents), 'zl', 0, 0, tiled=True)]
    ppermute x5 -> x4, waiting for transfers between devices: 3.25 us -> 1.01 us  [swap(): return lax.ppermute(value, 'core', [(0, 1), (1, 0)])]
  transfers between devices with their start and end apart: 11 -> 13, of which waited for: 8 -> 6; matrix products, arithmetic and copies ran while one was open for 5% -> 7% of each run, Pallas kernels for 0% -> 2%
where the time goes in v5:
time: 187 us; the launch traced here: 186 us
  starting transfers between devices  67.3 us (36%)
  waiting for transfers between devices  46.3 us (25%)
  blocking collectives  34.8 us (19%)
  between operations  14.4 us (8%)
  matrix products  6.83 us (4%)
  Pallas kernels  6.54 us (3%)
  other arithmetic  5.85 us (3%)
  local copies, waits for them, and re-layouts  4.14 us (2%)
    all_to_all x1, blocking collectives, body(): grads = lax.all_to_all(copies, PLANE, 0, 0, tiled=True)  19.4 us
    all_to_all x1, starting transfers between devices, body(): column = lax.all_to_all(halves, ('core', 'zh'), 0, 0, tiled=True)  16.6 us
    all_to_all x2, waiting for transfers between devices, spread(): return lax.all_to_all(copies, axes, 0, 0, tiled=True)  15.9 us
    all_gather x1, blocking collectives, body(): pre_here = lax.all_gather(last, 'zl', axis=0)  15.4 us
    ppermute x4, starting transfers between devices, swap(): return lax.ppermute(value, 'core', [(0, 1), (1, 0)])  15.1 us
    all_to_all x2, starting transfers between devices, spread(): return lax.all_to_all(copies, axes, 0, 0, tiled=True)  13.6 us
    all_to_all x1, waiting for transfers between devices, body(): lax.all_to_all(partial_value.reshape(BLOCKS, small, wide), PLANE, 0, 0, t...  11.3 us
    ppermute x3, starting transfers between devices, body(): came.append(lax.ppermute(block, 'zl', ways) if away else block)  10.4 us
  transfers between devices with their start and end apart: 13, of which 6 were waited for; matrix products, arithmetic and copies ran while one was open for 7% of the time, Pallas kernels for 2%

profile of v5, /device:TPU:1, one launch (start us, length us, event | category | flops | bytes accessed | tf_op | source)
XLA Modules:
  0.0 186.2 jit_solution(10171620891785922599)
XLA Ops:
  9.3 16.6 %all-to-all-start = ((bf16[8,8,448]{2,1,0:T(8,128)(2,1)}), bf16[8,8,448]{2,1,0:T(8,128)(2,1)S(1)}, u32[]{:S(2)}, u32[]{:S(2)}) async-start(bf16[8,8,448]{2,1,0:T(8,128)(2,1)} %bitcast.1), calls=%async_computation | async-start | bytes 131072 | tf_op jit(solution)/shard_map/all_to_all | solution.py:216
  25.9 1.9 %collective-permute-start = (f32[448]{0:T(512)}, f32[448]{0:T(512)S(1)}, u32[]{:S(2)}, u32[]{:S(2)}) collective-permute-start(f32[448]{0:T(512)} %param.11), channel_id=1, source_target_pairs={{0,64},{64,0},{1,65},{65,1},{2,66},{66,2},{3,67},{67,3},{4,68},{68... | collective-permute-start | bytes 5384 | tf_op jit(solution)/shard_map/ppermute | solution.py:52
  27.8 2.4 %collective-permute-start.4 = (bf16[448,512]{1,0:T(8,128)(2,1)}, bf16[448,512]{1,0:T(8,128)(2,1)S(1)}, u32[]{:S(2)}, u32[]{:S(2)}) collective-permute-start(bf16[448,512]{1,0:T(8,128)(2,1)} %param.8), channel_id=1, source_target_pairs={{0,64},{64,0},{1,65},{65,1},{2,66},{66,2},{3,67},{67,3},{4,68},{68... | collective-permute-start | bytes 1376264 | tf_op jit(solution)/shard_map/ppermute | solution.py:52
  31.0 7.5 %all-to-all-done = bf16[8,8,448]{2,1,0:T(8,128)(2,1)S(1)} async-done(((bf16[8,8,448]{2,1,0:T(8,128)(2,1)}), bf16[8,8,448]{2,1,0:T(8,128)(2,1)S(1)}, u32[]{:S(2)}, u32[]{:S(2)}) %all-to-all-start) | async-done | bytes 57376 | tf_op jit(solution)/shard_map/all_to_all | solution.py:216
  39.7 6.8 %all-to-all-start.1 = ((bf16[16,4,8,896]{3,2,1,0:T(8,128)(2,1)}), bf16[16,4,8,896]{3,2,1,0:T(8,128)(2,1)S(1)}, u32[]{:S(2)}, u32[]{:S(2)}) async-start(bf16[16,4,8,896]{3,2,1,0:T(8,128)(2,1)} %broadcast_in_dim.15), calls=%async_computation.1 | async-start | bytes 1835008 | tf_op jit(solution)/shard_map/all_to_all | solution.py:48
  46.7 4.0 %collective-permute-start.1 = (bf16[1,24,512]{2,1,0:T(8,128)(2,1)S(1)}, bf16[1,24,512]{2,1,0:T(8,128)(2,1)S(1)}, u32[]{:S(2)}, u32[]{:S(2)}) collective-permute-start(bf16[1,24,512]{2,1,0:T(8,128)(2,1)S(1)} %get-tuple-element.35), channel_id=1, source_target_pairs={{0,128},{128,256},{256,384},{384,0},{1,129},{129,257},{257,385},{3... | collective-permute-start | bytes 73736 | tf_op jit(solution)/shard_map/ppermute | solution.py:235
  50.6 2.2 %collective-permute-start.2 = (bf16[1,24,512]{2,1,0:T(8,128)(2,1)S(1)}, bf16[1,24,512]{2,1,0:T(8,128)(2,1)S(1)}, u32[]{:S(2)}, u32[]{:S(2)}) collective-permute-start(bf16[1,24,512]{2,1,0:T(8,128)(2,1)S(1)} %get-tuple-element.34), channel_id=1, source_target_pairs={{0,256},{128,384},{256,0},{384,128},{1,257},{129,385},{257,1},{385... | collective-permute-start | bytes 73736 | tf_op jit(solution)/shard_map/ppermute | solution.py:235
  52.9 4.3 %collective-permute-start.3 = (bf16[1,24,512]{2,1,0:T(8,128)(2,1)S(1)}, bf16[1,24,512]{2,1,0:T(8,128)(2,1)S(1)}, u32[]{:S(2)}, u32[]{:S(2)}) collective-permute-start(bf16[1,24,512]{2,1,0:T(8,128)(2,1)S(1)} %get-tuple-element.33), channel_id=1, source_target_pairs={{0,384},{128,0},{256,128},{384,256},{1,385},{129,1},{257,129},{385... | collective-permute-start | bytes 73736 | tf_op jit(solution)/shard_map/ppermute | solution.py:235
  58.2 3.2 %all-to-all-done.1 = bf16[16,4,8,896]{3,2,1,0:T(8,128)(2,1)S(1)} async-done(((bf16[16,4,8,896]{3,2,1,0:T(8,128)(2,1)}), bf16[16,4,8,896]{3,2,1,0:T(8,128)(2,1)S(1)}, u32[]{:S(2)}, u32[]{:S(2)}) %all-to-all-start.1) | async-done | bytes 917536 | tf_op jit(solution)/shard_map/all_to_all | solution.py:48
  61.5 2.7 %convolution_convert_fusion = bf16[512,512]{1,0:T(8,128)(2,1)} fusion(bf16[512,896]{1,0:T(8,128)(2,1)S(1)} %bitcast.32, bf16[448,512]{1,0:T(8,128)(2,1)} %get-tuple-element.32, bf16[448,512]{1,0:T(8,128)(2,1)} %get-tuple-element.31), kind=kOutput, calls=%fused_computation.5 | convolution fusion | flops 471859200 | bytes 2359296 | tf_op jit(solution)/shard_map/dot_general | solution.py:245
  64.2 4.8 %all-to-all-start.2 = ((bf16[4,128,512]{2,1,0:T(8,128)(2,1)}), bf16[4,128,512]{2,1,0:T(8,128)(2,1)S(1)}, u32[]{:S(2)}, u32[]{:S(2)}) async-start(bf16[4,128,512]{2,1,0:T(8,128)(2,1)} %bitcast.8), calls=%async_computation.2 | async-start | bytes 1048576 | tf_op jit(solution)/shard_map/all_to_all | solution.py:246
  69.2 3.2 %collective-permute-start.5 = (bf16[512,448]{1,0:T(8,128)(2,1)S(1)}, bf16[512,448]{1,0:T(8,128)(2,1)}, u32[]{:S(2)}, u32[]{:S(2)}) collective-permute-start(bf16[512,448]{1,0:T(8,128)(2,1)S(1)} %get-tuple-element.30), channel_id=1, source_target_pairs={{0,64},{64,0},{1,65},{65,1},{2,66},{66,2},{3,67},{67,3},{4,68},{68... | collective-permute-start | bytes 1376264 | tf_op jit(solution)/shard_map/ppermute | solution.py:52
  73.0 9.9 %all-to-all-done.2.quarter_ref = bf16[4,128,512]{2,1,0:T(8,128)(2,1)S(1)} async-done(((bf16[4,128,512]{2,1,0:T(8,128)(2,1)}), bf16[4,128,512]{2,1,0:T(8,128)(2,1)S(1)}, u32[]{:S(2)}, u32[]{:S(2)}) %all-to-all-start.2) | async-done | bytes 524320 | tf_op jit(solution)/shard_map/all_to_all | solution.py:246
  83.0 4.0 %decode.1 = (bf16[128,3584]{1,0:T(8,128)(2,1)}, bf16[128,512]{1,0:T(8,128)(2,1)S(1)}, f32[128,512]{1,0:T(8,128)S(1)}) custom-call(bf16[4,128,512]{2,1,0:T(8,128)(2,1)S(1)} %all-to-all-done.2.quarter_ref, f32[1,512]{1,0:T(1,128)S(1)} %bitcast.31, bf16[3584,512]{1,0:T(8,128)(2,1)} %all-gather.3.cloned.1.call-done.dec_ref), custom_call_target="tpu_custom_call" | custom-call | flops 469762048 | bytes 4587520 | tf_op jit(solution)/shard_map/decode/pallas_call | solution.py:95
  86.9 6.6 %all-to-all-start.3 = ((bf16[16,8,3584]{2,1,0:T(8,128)(2,1)}), bf16[16,8,3584]{2,1,0:T(8,128)(2,1)S(1)}, u32[]{:S(2)}, u32[]{:S(2)}) async-start(bf16[16,8,3584]{2,1,0:T(8,128)(2,1)} %bitcast.11), calls=%async_computation.3 | async-start | bytes 1835008 | tf_op jit(solution)/shard_map/all_to_all | solution.py:259
  93.5 2.8 %multiply_reduce_fusion.1 = (f32[512]{0:T(512)S(1)}, f32[512]{0:T(512)S(1)}) fusion(bf16[3584,512]{1,0:T(8,128)(2,1)} %all-gather.3.cloned.1.call-done.dec_ref), kind=kLoop, calls=%fused_computation.1 | loop fusion | flops 5504000 | bytes 3674112 | tf_op jit(solution)/shard_map/reduce_sum | solution.py:252
  96.5 11.3 %all-to-all-done.3 = bf16[16,8,3584]{2,1,0:T(8,128)(2,1)S(1)} async-done(((bf16[16,8,3584]{2,1,0:T(8,128)(2,1)}), bf16[16,8,3584]{2,1,0:T(8,128)(2,1)S(1)}, u32[]{:S(2)}, u32[]{:S(2)}) %all-to-all-start.3) | async-done | bytes 917536 | tf_op jit(solution)/shard_map/all_to_all | solution.py:259
  108.7 6.9 %all-to-all-start.4 = ((bf16[4,8,3712]{2,1,0:T(8,128)(2,1)}), bf16[4,8,3712]{2,1,0:T(8,128)(2,1)S(1)}, u32[]{:S(2)}, u32[]{:S(2)}) async-start(bf16[4,8,3712]{2,1,0:T(8,128)(2,1)} %broadcast_in_dim.33), calls=%async_computation.4 | async-start | bytes 475136 | tf_op jit(solution)/shard_map/all_to_all | solution.py:48
  115.7 12.7 %all-to-all-done.4.got_ref = bf16[4,8,3712]{2,1,0:T(8,128)(2,1)S(1)} async-done(((bf16[4,8,3712]{2,1,0:T(8,128)(2,1)}), bf16[4,8,3712]{2,1,0:T(8,128)(2,1)S(1)}, u32[]{:S(2)}, u32[]{:S(2)}) %all-to-all-start.4) | async-done | bytes 237600 | tf_op jit(solution)/shard_map/all_to_all | solution.py:48
  128.5 19.4 %all_to_all.30 = bf16[16,8,3712]{2,1,0:T(8,128)(2,1)S(1)} all-to-all(bf16[16,8,3712]{2,1,0:T(8,128)(2,1)S(1)} %error.1), channel_id=1, replica_groups=mesh['zl'=4,'core'=2,'y'=4,'x'=4,'zh'=4] {'y','x'}, dimensions={0} | all-to-all | bytes 1900544 | tf_op jit(solution)/shard_map/all_to_all | solution.py:266
  148.0 2.5 %back.1 = bf16[136,512]{1,0:T(8,128)(2,1)S(1)} custom-call(bf16[128,3712]{1,0:T(8,128)(2,1)S(1)} %bitcast.29, bf16[3584,512]{1,0:T(8,128)(2,1)} %all-gather.3.cloned.1.call-done.dec_ref, f32[128,512]{1,0:T(8,128)S(1)} %get-tuple-element.22.slopes_ref, f32[1,512]{1,0:T(1,128)S(1)} %bitcast.30), custom_call_target="tpu_custom_call" | custom-call | flops 469762048 | bytes 4587520 | tf_op jit(solution)/shard_map/back/pallas_call | solution.py:177
  150.5 15.4 %all-gather = bf16[544,512]{1,0:T(8,128)(2,1)S(1)} all-gather(bf16[136,512]{1,0:T(8,128)(2,1)S(1)} %back.1), channel_id=2, replica_groups=mesh['zl'=4,'core'=2,'y'=4,'x'=4,'zh'=4] {'zl'}, dimensions={0}, use_global_device_ids=true | all-gather | bytes 696320 | tf_op jit(solution)/shard_map/all_gather | solution.py:268
  165.9 7.6 %collective-permute-start.6 = (bf16[4,136,512]{2,1,0:T(8,128)(2,1)S(1)}, bf16[4,136,512]{2,1,0:T(8,128)(2,1)S(1)}, u32[]{:S(2)}, u32[]{:S(2)}) collective-permute-start(bf16[4,136,512]{2,1,0:T(8,128)(2,1)S(1)} %bitcast.34), channel_id=1, source_target_pairs={{0,64},{64,0},{1,65},{65,1},{2,66},{66,2},{3,67},{67,3},{4,68},{68... | collective-permute-start | bytes 1671176 | tf_op jit(solution)/shard_map/ppermute | solution.py:52
  175.7 3.6 %subtract_convert_fusion = (bf16[448,512]{1,0:T(8,128)(2,1)}, f32[448,512]{1,0:T(8,128)}, f32[448,512]{1,0:T(8,128)}) fusion(bf16[448,512]{1,0:T(8,128)(2,1)S(1)} %copy-done.1, f32[448,512]{1,0:T(8,128)S(1)} %copy-done.3, f32[448,512]{1,0:T(8,128)S(1)} %copy-done.4, f32[448,512]{1,0:T(8,128)S(1)} %convolution_bitcast_fusion.1, ...), kind=kOutput, calls=%fused_computation.11 | convolution fusion | flops 253231104 | bytes 6520832 | tf_op jit(solution)/shard_map/dot_general | solution.py:273
  (61 shorter events, 9.6 us)
Async XLA Ops:
  7.2 50.0 %copy-start.1 = (bf16[448,512]{1,0:T(8,128)(2,1)S(1)}, bf16[448,512]{1,0:T(8,128)(2,1)}, u32[]{:S(2)}) copy-start(bf16[448,512]{1,0:T(8,128)(2,1)} %param.8) | copy-start | bytes 1376260
  7.2 75.8 %all-gather.3.cloned.1.call-start = ((), (), s32[]{:S(2)}) async-start(), calls=%async_computation.6 | async-start | bytes 4128768 | tf_op jit(solution)/shard_map/all_gather | solution.py:205
  9.3 29.2 %all-to-all-start = ((bf16[8,8,448]{2,1,0:T(8,128)(2,1)}), bf16[8,8,448]{2,1,0:T(8,128)(2,1)S(1)}, u32[]{:S(2)}, u32[]{:S(2)}) async-start(bf16[8,8,448]{2,1,0:T(8,128)(2,1)} %bitcast.1), calls=%async_computation | async-start | bytes 131072 | tf_op jit(solution)/shard_map/all_to_all | solution.py:216
  25.9 4.4 %collective-permute-start = (f32[448]{0:T(512)}, f32[448]{0:T(512)S(1)}, u32[]{:S(2)}, u32[]{:S(2)}) collective-permute-start(f32[448]{0:T(512)} %param.11), channel_id=1, source_target_pairs={{0,64},{64,0},{1,65},{65,1},{2,66},{66,2},{3,67},{67,3},{4,68},{68... | collective-permute-start | bytes 5384 | tf_op jit(solution)/shard_map/ppermute | solution.py:52
  27.8 29.3 %collective-permute-start.4 = (bf16[448,512]{1,0:T(8,128)(2,1)}, bf16[448,512]{1,0:T(8,128)(2,1)S(1)}, u32[]{:S(2)}, u32[]{:S(2)}) collective-permute-start(bf16[448,512]{1,0:T(8,128)(2,1)} %param.8), channel_id=1, source_target_pairs={{0,64},{64,0},{1,65},{65,1},{2,66},{66,2},{3,67},{67,3},{4,68},{68... | collective-permute-start | bytes 1376264 | tf_op jit(solution)/shard_map/ppermute | solution.py:52
  39.7 21.7 %all-to-all-start.1 = ((bf16[16,4,8,896]{3,2,1,0:T(8,128)(2,1)}), bf16[16,4,8,896]{3,2,1,0:T(8,128)(2,1)S(1)}, u32[]{:S(2)}, u32[]{:S(2)}) async-start(bf16[16,4,8,896]{3,2,1,0:T(8,128)(2,1)} %broadcast_in_dim.15), calls=%async_computation.1 | async-start | bytes 1835008 | tf_op jit(solution)/shard_map/all_to_all | solution.py:48
  46.7 14.8 %collective-permute-start.1 = (bf16[1,24,512]{2,1,0:T(8,128)(2,1)S(1)}, bf16[1,24,512]{2,1,0:T(8,128)(2,1)S(1)}, u32[]{:S(2)}, u32[]{:S(2)}) collective-permute-start(bf16[1,24,512]{2,1,0:T(8,128)(2,1)S(1)} %get-tuple-element.35), channel_id=1, source_target_pairs={{0,128},{128,256},{256,384},{384,0},{1,129},{129,257},{257,385},{3... | collective-permute-start | bytes 73736 | tf_op jit(solution)/shard_map/ppermute | solution.py:235
  50.6 10.8 %collective-permute-start.2 = (bf16[1,24,512]{2,1,0:T(8,128)(2,1)S(1)}, bf16[1,24,512]{2,1,0:T(8,128)(2,1)S(1)}, u32[]{:S(2)}, u32[]{:S(2)}) collective-permute-start(bf16[1,24,512]{2,1,0:T(8,128)(2,1)S(1)} %get-tuple-element.34), channel_id=1, source_target_pairs={{0,256},{128,384},{256,0},{384,128},{1,257},{129,385},{257,1},{385... | collective-permute-start | bytes 73736 | tf_op jit(solution)/shard_map/ppermute | solution.py:235
  52.9 8.6 %collective-permute-start.3 = (bf16[1,24,512]{2,1,0:T(8,128)(2,1)S(1)}, bf16[1,24,512]{2,1,0:T(8,128)(2,1)S(1)}, u32[]{:S(2)}, u32[]{:S(2)}) collective-permute-start(bf16[1,24,512]{2,1,0:T(8,128)(2,1)S(1)} %get-tuple-element.33), channel_id=1, source_target_pairs={{0,384},{128,0},{256,128},{384,256},{1,385},{129,1},{257,129},{385... | collective-permute-start | bytes 73736 | tf_op jit(solution)/shard_map/ppermute | solution.py:235
  61.4 21.5 %copy-start = (f32[512]{0:T(512)S(1)}, f32[512]{0:T(512)}, u32[]{:S(2)}) copy-start(f32[512]{0:T(512)} %param.9) | copy-start | bytes 6148
  64.2 18.8 %all-to-all-start.2 = ((bf16[4,128,512]{2,1,0:T(8,128)(2,1)}), bf16[4,128,512]{2,1,0:T(8,128)(2,1)S(1)}, u32[]{:S(2)}, u32[]{:S(2)}) async-start(bf16[4,128,512]{2,1,0:T(8,128)(2,1)} %bitcast.8), calls=%async_computation.2 | async-start | bytes 1048576 | tf_op jit(solution)/shard_map/all_to_all | solution.py:246
  69.2 46.4 %collective-permute-start.5 = (bf16[512,448]{1,0:T(8,128)(2,1)S(1)}, bf16[512,448]{1,0:T(8,128)(2,1)}, u32[]{:S(2)}, u32[]{:S(2)}) collective-permute-start(bf16[512,448]{1,0:T(8,128)(2,1)S(1)} %get-tuple-element.30), channel_id=1, source_target_pairs={{0,64},{64,0},{1,65},{65,1},{2,66},{66,2},{3,67},{67,3},{4,68},{68... | collective-permute-start | bytes 1376264 | tf_op jit(solution)/shard_map/ppermute | solution.py:52
  86.9 28.6 %copy-start.2 = (bf16[7,24,512]{2,1,0:T(8,128)(2,1)S(1)}, bf16[7,24,512]{2,1,0:T(8,128)(2,1)}, u32[]{:S(2)}) copy-start(bf16[7,24,512]{2,1,0:T(8,128)(2,1)} %constant_dynamic-update-slice_fusion.6) | copy-start | bytes 516100
  86.9 20.9 %all-to-all-start.3 = ((bf16[16,8,3584]{2,1,0:T(8,128)(2,1)}), bf16[16,8,3584]{2,1,0:T(8,128)(2,1)S(1)}, u32[]{:S(2)}, u32[]{:S(2)}) async-start(bf16[16,8,3584]{2,1,0:T(8,128)(2,1)} %bitcast.11), calls=%async_computation.3 | async-start | bytes 1835008 | tf_op jit(solution)/shard_map/all_to_all | solution.py:259
  108.7 19.7 %all-to-all-start.4 = ((bf16[4,8,3712]{2,1,0:T(8,128)(2,1)}), bf16[4,8,3712]{2,1,0:T(8,128)(2,1)S(1)}, u32[]{:S(2)}, u32[]{:S(2)}) async-start(bf16[4,8,3712]{2,1,0:T(8,128)(2,1)} %broadcast_in_dim.33), calls=%async_computation.4 | async-start | bytes 475136 | tf_op jit(solution)/shard_map/all_to_all | solution.py:48
  148.0 27.7 %copy-start.3 = (f32[448,512]{1,0:T(8,128)S(1)}, f32[448,512]{1,0:T(8,128)}, u32[]{:S(2)}) copy-start(f32[448,512]{1,0:T(8,128)} %param.12) | copy-start | bytes 2752516
  148.0 27.7 %copy-start.4 = (f32[448,512]{1,0:T(8,128)S(1)}, f32[448,512]{1,0:T(8,128)}, u32[]{:S(2)}) copy-start(f32[448,512]{1,0:T(8,128)} %param.13) | copy-start | bytes 2752516
  165.9 9.2 %collective-permute-start.6 = (bf16[4,136,512]{2,1,0:T(8,128)(2,1)S(1)}, bf16[4,136,512]{2,1,0:T(8,128)(2,1)S(1)}, u32[]{:S(2)}, u32[]{:S(2)}) collective-permute-start(bf16[4,136,512]{2,1,0:T(8,128)(2,1)S(1)} %bitcast.34), channel_id=1, source_target_pairs={{0,64},{64,0},{1,65},{65,1},{2,66},{66,2},{3,67},{67,3},{4,68},{68... | collective-permute-start | bytes 1671176 | tf_op jit(solution)/shard_map/ppermute | solution.py:52
Sparse Core Ops, SparseCore 0:
  10.1 59.7 all-gather.2

commit v6 on v5

--- a/solution.py
+++ b/solution.py
@@ -56,20 +56,29 @@
     return pltpu.CompilerParams(vmem_limit_bytes=mebibytes * 1024 * 1024)
 
 
-def start_blocks(source, held, sems, count):
-    step = source.shape[0] // count
+def start_blocks(sources, held, sems):
+    step = sources[0].shape[0] // CHIPS
     found = []
-    for k in range(count):
-        rows = pl.ds(k * step, step)
-        found.append(pltpu.make_async_copy(source.at[rows], held.at[rows], sems.at[k]))
+    for chip in range(CHIPS):
+        for k, source in enumerate(sources):
+            place = chip * len(sources) + k
+            rows, there = pl.ds(chip * step, step), pl.ds(place * step, step)
+            found.append(pltpu.make_async_copy(source.at[rows], held.at[there], sems.at[place]))
     for copy in found:
         copy.start()
     return found
 
 
-def decode_kernel(quarter_ref, bias_ref, dec_ref, out_ref, codes_ref, slopes_ref, held, sems):
+def await_chip(blocks, chip):
+    for copy in blocks[chip * CORES : (chip + 1) * CORES]:
+        copy.wait()
+
+
+def decode_kernel(
+    quarter_ref, bias_ref, here_ref, there_ref, out_ref, codes_ref, slopes_ref, held, sems
+):
     step = held.shape[0] // CHIPS
-    blocks = start_blocks(dec_ref, held, sems, CHIPS)
+    blocks = start_blocks((here_ref, there_ref), held, sems)
     sums = jnp.sum(quarter_ref[...].astype(F32), axis=0)
     scaled = sharpness * (sums + bias_ref[...])
     small = jnp.exp(-jnp.abs(scaled))
@@ -77,7 +86,7 @@
     codes_ref[...] = (soft / sharpness).astype(BF)
     slopes_ref[...] = jnp.where(scaled >= 0.0, 1.0, small) / (1.0 + small)
     for k in range(CHIPS):
-        blocks[k].wait()
+        await_chip(blocks, k)
         out_ref[:, k * step : (k + 1) * step] = lax.dot_general(
             codes_ref[...],
             held[k * step : (k + 1) * step],
@@ -86,22 +95,26 @@
         ).astype(BF)
 
 
+def in_hbm():
+    return pl.BlockSpec(memory_space=pltpu.HBM)
+
+
 def whole():
     return pl.BlockSpec(memory_space=pltpu.VMEM)
 
 
-def decode(quarter, enc_bias, dec_all, tokens):
-    wide, latents = dec_all.shape
+def decode(quarter, enc_bias, dec_here, dec_there, tokens):
+    wide, latents = CORES * dec_here.shape[0], dec_here.shape[1]
     return pl.pallas_call(
         decode_kernel,
-        in_specs=[whole(), whole(), pl.BlockSpec(memory_space=pltpu.HBM)],
+        in_specs=[whole(), whole(), in_hbm(), in_hbm()],
         out_specs=[whole(), whole(), whole()],
         out_shape=[
             jax.ShapeDtypeStruct((tokens, wide), BF),
             jax.ShapeDtypeStruct((tokens, latents), BF),
             jax.ShapeDtypeStruct((tokens, latents), F32),
         ],
-        scratch_shapes=[pltpu.VMEM((wide, latents), BF), pltpu.SemaphoreType.DMA((CHIPS,))],
+        scratch_shapes=[pltpu.VMEM((wide, latents), BF), pltpu.SemaphoreType.DMA((PARTS,))],
         compiler_params=params(50),
         cost_estimate=pl.CostEstimate(
             flops=2 * tokens * latents * wide,
@@ -109,7 +122,7 @@
             transcendentals=3 * tokens * latents,
         ),
         name="decode",
-    )(quarter, enc_bias.reshape(1, latents), dec_all)
+    )(quarter, enc_bias.reshape(1, latents), dec_here, dec_there)
 
 
 def row_sum(rows, first, last):
@@ -151,10 +164,12 @@
     )(got, extra, mask)
 
 
-def back_kernel(scale, grad_ref, dec_ref, slopes_ref, norms_ref, out_ref, held, sems):
+def back_kernel(
+    scale, grad_ref, here_ref, there_ref, slopes_ref, norms_ref, out_ref, held, sems
+):
     wide, latents = held.shape
     step = wide // CHIPS
-    blocks = start_blocks(dec_ref, held, sems, CHIPS)
+    blocks = start_blocks((here_ref, there_ref), held, sems)
     sums = jnp.sum(grad_ref[:, wide:].astype(F32), axis=0, keepdims=True)
     high, low = pieces(sums, 2)
     row = lax.broadcasted_iota(jnp.int32, (8, LANES), 0)
@@ -162,7 +177,7 @@
     block = jnp.concatenate([both, jnp.zeros((8, latents - LANES), F32)], axis=1)
     code_grad = sparsity * scale * norms_ref[...]
     for k in range(CHIPS):
-        blocks[k].wait()
+        await_chip(blocks, k)
         code_grad = code_grad + jnp.dot(
             grad_ref[:, k * step : (k + 1) * step],
             held[k * step : (k + 1) * step],
@@ -171,15 +186,15 @@
     out_ref[...] = jnp.concatenate([code_grad * slopes_ref[...], block], axis=0).astype(BF)
 
 
-def back(grads, dec_all, slopes, norms, scale):
+def back(grads, dec_here, dec_there, slopes, norms, scale):
     tokens = grads.shape[0]
-    wide, latents = dec_all.shape
+    wide, latents = CORES * dec_here.shape[0], dec_here.shape[1]
     return pl.pallas_call(
         functools.partial(back_kernel, scale),
-        in_specs=[whole(), pl.BlockSpec(memory_space=pltpu.HBM), whole(), whole()],
+        in_specs=[whole(), in_hbm(), in_hbm(), whole(), whole()],
         out_specs=whole(),
         out_shape=jax.ShapeDtypeStruct((tokens + 8, latents), BF),
-        scratch_shapes=[pltpu.VMEM((wide, latents), BF), pltpu.SemaphoreType.DMA((CHIPS,))],
+        scratch_shapes=[pltpu.VMEM((wide, latents), BF), pltpu.SemaphoreType.DMA((PARTS,))],
         compiler_params=params(50),
         cost_estimate=pl.CostEstimate(
             flops=2 * tokens * latents * wide,
@@ -187,7 +202,7 @@
             transcendentals=0,
         ),
         name="back",
-    )(grads, dec_all, slopes, norms.reshape(1, latents))
+    )(grads, dec_here, dec_there, slopes, norms.reshape(1, latents))
 
 
 def body(acts, enc_weight, enc_bias, dec_weight, dec_bias, enc_moment, enc_second):
@@ -202,19 +217,18 @@
     small = HIGH * share
     tokens = BLOCKS * small
 
-    dec_all = lax.all_gather(dec_weight.T, LAYER, axis=0, tiled=True)
+    dec_here = lax.all_gather(dec_weight.T, "zl", axis=0, tiled=True)
+    dec_there = swap(dec_here)
     enc_there = swap(enc_weight)
     bias_there = swap(dec_bias)
-
-    def ordered(near, far, axis):
-        first, second = jnp.where(core == 0, near, far), jnp.where(core == 0, far, near)
-        return jnp.concatenate([first, second], axis=axis)
 
     padded = jnp.concatenate([acts, jnp.zeros((1, chans), BF)], axis=0)
     halves = jnp.broadcast_to(padded.reshape(CORES, 1, half, chans), (CORES, HIGH, half, chans))
     halves = halves.reshape(CORES * HIGH, half, chans)
     column = lax.all_to_all(halves, ("core", "zh"), 0, 0, tiled=True)
-    column = column.reshape(CORES, HIGH, CHIPS, share, chans).transpose(2, 1, 3, 0, 4)
+    column = column.reshape(CORES, HIGH, CHIPS, share, chans)
+    column = jnp.where(core == 0, column, column[::-1])
+    column = column.transpose(2, 1, 3, 0, 4)
     column = column.reshape(CHIPS, small, 2 * chans)
     gathered = spread(column, PLANE, BLOCKS).transpose(1, 0, 2, 3)
     gathered = gathered.reshape(CHIPS * tokens, 2 * chans)
@@ -224,7 +238,7 @@
         rest = jnp.pad(rows_of[..., latents:], fill)
         return jnp.concatenate([rows_of[..., :latents], rest], axis=-2)
 
-    bias_rows = folded(jnp.stack(pieces(ordered(dec_bias, bias_there, 0), 3)))
+    bias_rows = folded(jnp.stack(pieces(jnp.concatenate([dec_bias, bias_there]), 3)))
     bias_rows = jnp.pad(bias_rows, ((0, small - 6), (0, 0)))
     bias_rows = jnp.broadcast_to(bias_rows[None], (CHIPS, small, latents))
     extra = jnp.concatenate([folded(column), bias_rows], axis=1)
@@ -237,19 +251,18 @@
     turned = jnp.concatenate([came[-k % CHIPS] for k in range(2 * CHIPS - 1)], axis=0)
     mine = lax.dynamic_slice_in_dim(turned, (CHIPS - chip) & (CHIPS - 1), CHIPS, axis=0)
 
-    first_half, second_half = gathered[:, :chans], gathered[:, chans:]
-    acts_here = jnp.where(core == 0, first_half, second_half)
-    acts_there = swap(jnp.where(core == 0, second_half, first_half))
-
-    enc_pair = ordered(enc_weight, enc_there, 0)
+    acts_here = gathered[:, :chans]
+    acts_there = swap(gathered[:, chans:])
+    enc_pair = jnp.concatenate([enc_weight, enc_there], axis=0)
     sums = jnp.dot(gathered, enc_pair, preferred_element_type=F32).astype(BF)
     quarter = lax.all_to_all(sums.reshape(CHIPS, tokens, latents), "zl", 0, 0, tiled=True)
-    partial_value, codes, slopes = decode(quarter, enc_bias, dec_all, tokens)
+    partial_value, codes, slopes = decode(quarter, enc_bias, dec_here, dec_there, tokens)
 
     dec_norms = jnp.zeros((latents,), F32)
     for layer in range(LAYERS):
-        block = dec_all[layer * (wide // LAYERS) : (layer + 1) * (wide // LAYERS)].astype(F32)
-        dec_norms = dec_norms + jnp.sqrt(jnp.sum(block * block, axis=0))
+        rows_of = slice(layer * CHIPS // LAYERS * chans, (layer + 1) * CHIPS // LAYERS * chans)
+        near, far = dec_here[rows_of].astype(F32), dec_there[rows_of].astype(F32)
+        dec_norms = dec_norms + jnp.sqrt(jnp.sum(near * near + far * far, axis=0))
 
     place = lax.broadcasted_iota(jnp.int32, (small, LANES), 0) & (share - 1)
     real = (core * half + chip * share + place < rows).astype(F32)
@@ -260,11 +273,11 @@
         partial_value.reshape(BLOCKS, small, wide), PLANE, 0, 0, tiled=True
     )
     summed = jnp.sum(got.astype(F32), axis=0).astype(BF)
-    again = spread(jnp.concatenate([summed, sparse.astype(BF)], axis=1), "zh", HIGH)
+    again = lax.all_gather(jnp.concatenate([summed, sparse.astype(BF)], axis=1), "zh", axis=0)
     again, acts_there = lax.optimization_barrier((again, acts_there))
     copies = error_copies(again, mine, real, inv_batch)
     grads = lax.all_to_all(copies, PLANE, 0, 0, tiled=True)
-    last = back(grads.reshape(tokens, wide + LANES), dec_all, slopes, dec_norms, inv_batch)
+    last = back(grads.reshape(tokens, wide + LANES), dec_here, dec_there, slopes, dec_norms, inv_batch)
     pre_here = lax.all_gather(last, "zl", axis=0)
     pre_there = swap(pre_here)
 

time: 187 us -> 193 us (1.032)
  blocking collectives: 34.8 us -> 48.7 us
  starting transfers between devices: 67.3 us -> 62.8 us
    all_gather x0 -> x1, blocking collectives: none -> 20 us  [body(): lax.all_gather(jnp.concatenate([summed, sparse.astype(BF)], axis=1), 'zh'...]
    all_to_all x2 -> x1, waiting for transfers between devices: 15.9 us -> 0.01 us  [spread(): return lax.all_to_all(copies, axes, 0, 0, tiled=True)]
    all_to_all x2 -> x1, starting transfers between devices: 13.6 us -> 6.75 us  [spread(): return lax.all_to_all(copies, axes, 0, 0, tiled=True)]
    all_gather x1, waiting for transfers between devices: 0.01 us -> 6.37 us  [body(): dec_here = lax.all_gather(dec_weight.T, 'zl', axis=0, tiled=True)]
    all_to_all x1, waiting for transfers between devices: 7.48 us -> 12.6 us  [body(): column = lax.all_to_all(halves, ('core', 'zh'), 0, 0, tiled=True)]
    all_to_all x1, blocking collectives: 19.4 us -> 15.4 us  [body(): grads = lax.all_to_all(copies, PLANE, 0, 0, tiled=True)]
    ppermute x4 -> x5, starting transfers between devices: 15.1 us -> 19 us  [swap(): return lax.ppermute(value, 'core', [(0, 1), (1, 0)])]
    all_gather x1, blocking collectives: 15.4 us -> 13.3 us  [body(): pre_here = lax.all_gather(last, 'zl', axis=0)]
  transfers between devices with their start and end apart: 13 -> 13, of which waited for: 6 -> 5; matrix products, arithmetic and copies ran while one was open for 7% -> 5% of each run, Pallas kernels for 2% -> 2%
where the time goes in v6:
time: 193 us; the launch traced here: 192 us
  starting transfers between devices  62.8 us (33%)
  blocking collectives  48.7 us (25%)
  waiting for transfers between devices  44.8 us (23%)
  between operations  14.5 us (8%)
  Pallas kernels  6.86 us (4%)
  matrix products  5.65 us (3%)
  other arithmetic  4.5 us (2%)
  local copies, waits for them, and re-layouts  4.11 us (2%)
    all_gather x1, blocking collectives, body(): lax.all_gather(jnp.concatenate([summed, sparse.astype(BF)], axis=1), 'zh'...  20 us
    ppermute x5, starting transfers between devices, swap(): return lax.ppermute(value, 'core', [(0, 1), (1, 0)])  19 us
    all_to_all x1, starting transfers between devices, body(): column = lax.all_to_all(halves, ('core', 'zh'), 0, 0, tiled=True)  16.6 us
    all_to_all x1, blocking collectives, body(): grads = lax.all_to_all(copies, PLANE, 0, 0, tiled=True)  15.4 us
    all_gather x1, blocking collectives, body(): pre_here = lax.all_gather(last, 'zl', axis=0)  13.3 us
    all_to_all x1, waiting for transfers between devices, body(): column = lax.all_to_all(halves, ('core', 'zh'), 0, 0, tiled=True)  12.6 us
    all_to_all x1, waiting for transfers between devices, body(): lax.all_to_all(partial_value.reshape(BLOCKS, small, wide), PLANE, 0, 0, t...  12.2 us
    all_to_all x1, waiting for transfers between devices, body(): lax.all_to_all(sums.reshape(CHIPS, tokens, latents), 'zl', 0, 0, tiled=True)  11.3 us
  transfers between devices with their start and end apart: 13, of which 5 were waited for; matrix products, arithmetic and copies ran while one was open for 5% of the time, Pallas kernels for 2%

profile of v6, /device:TPU:1, one launch (start us, length us, event | category | flops | bytes accessed | tf_op | source)
XLA Modules:
  0.0 191.9 jit_solution(11509270414568147504)
XLA Ops:
  9.3 16.6 %all-to-all-start = ((bf16[8,8,448]{2,1,0:T(8,128)(2,1)}), bf16[8,8,448]{2,1,0:T(8,128)(2,1)S(1)}, u32[]{:S(2)}, u32[]{:S(2)}) async-start(bf16[8,8,448]{2,1,0:T(8,128)(2,1)} %bitcast.1), calls=%async_computation | async-start | bytes 131072 | tf_op jit(solution)/shard_map/all_to_all | solution.py:228
  25.9 12.6 %all-to-all-done = bf16[8,8,448]{2,1,0:T(8,128)(2,1)S(1)} async-done(((bf16[8,8,448]{2,1,0:T(8,128)(2,1)}), bf16[8,8,448]{2,1,0:T(8,128)(2,1)S(1)}, u32[]{:S(2)}, u32[]{:S(2)}) %all-to-all-start) | async-done | bytes 57376 | tf_op jit(solution)/shard_map/all_to_all | solution.py:228
  39.8 6.8 %all-to-all-start.1 = ((bf16[16,4,8,896]{3,2,1,0:T(8,128)(2,1)}), bf16[16,4,8,896]{3,2,1,0:T(8,128)(2,1)S(1)}, u32[]{:S(2)}, u32[]{:S(2)}) async-start(bf16[16,4,8,896]{3,2,1,0:T(8,128)(2,1)} %broadcast_in_dim.25), calls=%async_computation.1 | async-start | bytes 1835008 | tf_op jit(solution)/shard_map/all_to_all | solution.py:48
  46.6 2.6 %collective-permute-start = (f32[448]{0:T(512)S(1)}, f32[448]{0:T(512)S(1)}, u32[]{:S(2)}, u32[]{:S(2)}) collective-permute-start(f32[448]{0:T(512)S(1)} %copy-done.3), channel_id=1, source_target_pairs={{0,64},{64,0},{1,65},{65,1},{2,66},{66,2},{3,67},{67,3},{4,68},{68... | collective-permute-start | bytes 5384 | tf_op jit(solution)/shard_map/ppermute | solution.py:52
  49.2 1.9 %collective-permute-start.4 = (bf16[448,512]{1,0:T(8,128)(2,1)S(1)}, bf16[448,512]{1,0:T(8,128)(2,1)S(1)}, u32[]{:S(2)}, u32[]{:S(2)}) collective-permute-start(bf16[448,512]{1,0:T(8,128)(2,1)S(1)} %copy-done.6), channel_id=1, source_target_pairs={{0,64},{64,0},{1,65},{65,1},{2,66},{66,2},{3,67},{67,3},{4,68},{68... | collective-permute-start | bytes 1376264 | tf_op jit(solution)/shard_map/ppermute | solution.py:52
  51.5 3.8 %collective-permute-start.1 = (bf16[1,24,512]{2,1,0:T(8,128)(2,1)S(1)}, bf16[1,24,512]{2,1,0:T(8,128)(2,1)S(1)}, u32[]{:S(2)}, u32[]{:S(2)}) collective-permute-start(bf16[1,24,512]{2,1,0:T(8,128)(2,1)S(1)} %get-tuple-element.33), channel_id=1, source_target_pairs={{0,128},{128,256},{256,384},{384,0},{1,129},{129,257},{257,385},{3... | collective-permute-start | bytes 73736 | tf_op jit(solution)/shard_map/ppermute | solution.py:249
  55.2 2.2 %collective-permute-start.2 = (bf16[1,24,512]{2,1,0:T(8,128)(2,1)S(1)}, bf16[1,24,512]{2,1,0:T(8,128)(2,1)S(1)}, u32[]{:S(2)}, u32[]{:S(2)}) collective-permute-start(bf16[1,24,512]{2,1,0:T(8,128)(2,1)S(1)} %get-tuple-element.32), channel_id=1, source_target_pairs={{0,256},{128,384},{256,0},{384,128},{1,257},{129,385},{257,1},{385... | collective-permute-start | bytes 73736 | tf_op jit(solution)/shard_map/ppermute | solution.py:249
  57.4 4.3 %collective-permute-start.3 = (bf16[1,24,512]{2,1,0:T(8,128)(2,1)S(1)}, bf16[1,24,512]{2,1,0:T(8,128)(2,1)S(1)}, u32[]{:S(2)}, u32[]{:S(2)}) collective-permute-start(bf16[1,24,512]{2,1,0:T(8,128)(2,1)S(1)} %get-tuple-element.31), channel_id=1, source_target_pairs={{0,384},{128,0},{256,128},{384,256},{1,385},{129,1},{257,129},{385... | collective-permute-start | bytes 73736 | tf_op jit(solution)/shard_map/ppermute | solution.py:249
  61.7 6.4 %all-gather.4.cloned.1.call-done.here_ref = bf16[1792,512]{1,0:T(8,128)(2,1)} async-done(((bf16[448,512]{1,0:T(8,128)(2,1)}), bf16[1792,512]{1,0:T(8,128)(2,1)}) %all-gather.4.cloned.1.call-update) | async-done | bytes 1835024 | tf_op jit(solution)/shard_map/all_gather | solution.py:220
  68.1 2.8 %collective-permute-start.5 = (bf16[1792,512]{1,0:T(8,128)(2,1)}, bf16[1792,512]{1,0:T(8,128)(2,1)}, u32[]{:S(2)}, u32[]{:S(2)}) collective-permute-start(bf16[1792,512]{1,0:T(8,128)(2,1)} %all-gather.4.cloned.1.call-done.here_ref), channel_id=1, source_target_pairs={{0,64},{64,0},{1,65},{65,1},{2,66},{66,2},{3,67},{67,3},{4,68},{68... | collective-permute-start | bytes 5505032 | tf_op jit(solution)/shard_map/ppermute | solution.py:52
  72.6 3.6 %all-to-all-start.2 = ((bf16[4,128,512]{2,1,0:T(8,128)(2,1)}), bf16[4,128,512]{2,1,0:T(8,128)(2,1)S(1)}, u32[]{:S(2)}, u32[]{:S(2)}) async-start(bf16[4,128,512]{2,1,0:T(8,128)(2,1)} %bitcast.40), calls=%async_computation.2 | async-start | bytes 1048576 | tf_op jit(solution)/shard_map/all_to_all | solution.py:258
  77.4 1.9 collective-permute-start.6
  79.4 11.3 %all-to-all-done.2.quarter_ref = bf16[4,128,512]{2,1,0:T(8,128)(2,1)S(1)} async-done(((bf16[4,128,512]{2,1,0:T(8,128)(2,1)}), bf16[4,128,512]{2,1,0:T(8,128)(2,1)S(1)}, u32[]{:S(2)}, u32[]{:S(2)}) %all-to-all-start.2) | async-done | bytes 524320 | tf_op jit(solution)/shard_map/all_to_all | solution.py:258
  90.8 4.2 %decode.1 = (bf16[128,3584]{1,0:T(8,128)(2,1)}, bf16[128,512]{1,0:T(8,128)(2,1)S(1)}, f32[128,512]{1,0:T(8,128)S(1)}) custom-call(bf16[4,128,512]{2,1,0:T(8,128)(2,1)S(1)} %all-to-all-done.2.quarter_ref, f32[1,512]{1,0:T(1,128)S(1)} %bitcast.34, bf16[1792,512]{1,0:T(8,128)(2,1)S(1)} %copy-done, bf16[1792,512]{1,0:T(8,128)(2,1)} %collective-permute-done.5.there_ref), custom_call_target="tpu_custom_call" | custom-call | flops 469762048 | bytes 4587520 | tf_op jit(solution)/shard_map/decode/pallas_call | solution.py:108
  95.0 6.6 %all-to-all-start.3 = ((bf16[16,8,3584]{2,1,0:T(8,128)(2,1)}), bf16[16,8,3584]{2,1,0:T(8,128)(2,1)}, u32[]{:S(2)}, u32[]{:S(2)}) async-start(bf16[16,8,3584]{2,1,0:T(8,128)(2,1)} %bitcast.11), calls=%async_computation.3 | async-start | bytes 1835008 | tf_op jit(solution)/shard_map/all_to_all | solution.py:272
  101.6 2.2 %add_reduce_fusion.1 = (f32[512]{0:T(512)S(1)}, f32[512]{0:T(512)S(1)}) fusion(bf16[1792,512]{1,0:T(8,128)(2,1)} %collective-permute-done.5.there_ref, bf16[1792,512]{1,0:T(8,128)(2,1)S(1)} %copy-done), kind=kLoop, calls=%fused_computation.1 | loop fusion | flops 5504000 | bytes 3674112 | tf_op jit(solution)/shard_map/reduce_sum | solution.py:265
  103.9 12.2 %all-to-all-done.3 = bf16[16,8,3584]{2,1,0:T(8,128)(2,1)} async-done(((bf16[16,8,3584]{2,1,0:T(8,128)(2,1)}), bf16[16,8,3584]{2,1,0:T(8,128)(2,1)}, u32[]{:S(2)}, u32[]{:S(2)}) %all-to-all-start.3) | async-done | bytes 917536 | tf_op jit(solution)/shard_map/all_to_all | solution.py:272
  117.5 20.0 %all-gather = bf16[32,3712]{1,0:T(8,128)(2,1)S(1)} all-gather(bf16[8,3712]{1,0:T(8,128)(2,1)S(1)} %pad_maximum_fusion), channel_id=2, replica_groups=mesh['zl'=4,'core'=2,'y'=4,'x'=4,'zh'=4] {'zh'}, dimensions={0}, use_global_device_ids=true | all-gather | bytes 296960 | tf_op jit(solution)/shard_map/all_gather | solution.py:276
  137.6 15.4 %all_to_all.25 = bf16[16,8,3712]{2,1,0:T(8,128)(2,1)S(1)} all-to-all(bf16[16,8,3712]{2,1,0:T(8,128)(2,1)S(1)} %error.1), channel_id=1, replica_groups=mesh['zl'=4,'core'=2,'y'=4,'x'=4,'zh'=4] {'y','x'}, dimensions={0} | all-to-all | bytes 1900544 | tf_op jit(solution)/shard_map/all_to_all | solution.py:279
  153.0 2.6 %back.1 = bf16[136,512]{1,0:T(8,128)(2,1)S(1)} custom-call(bf16[128,3712]{1,0:T(8,128)(2,1)S(1)} %bitcast.31, bf16[1792,512]{1,0:T(8,128)(2,1)S(1)} %copy-done, bf16[1792,512]{1,0:T(8,128)(2,1)} %collective-permute-done.5.there_ref, f32[128,512]{1,0:T(8,128)S(1)} %get-tuple-element.22.slopes_ref, f32[1,512]{1,0:T(1,128)S(1)} %bitcast.33), custom_call_target="tpu_custom_call" | custom-call | flops 469762048 | bytes 4587520 | tf_op jit(solution)/shard_map/back/pallas_call | solution.py:192
  155.7 13.3 %all-gather.1 = bf16[544,512]{1,0:T(8,128)(2,1)S(1)} all-gather(bf16[136,512]{1,0:T(8,128)(2,1)S(1)} %back.1), channel_id=3, replica_groups=mesh['zl'=4,'core'=2,'y'=4,'x'=4,'zh'=4] {'zl'}, dimensions={0}, use_global_device_ids=true | all-gather | bytes 696320 | tf_op jit(solution)/shard_map/all_gather | solution.py:281
  169.0 9.7 %collective-permute-start.7 = (bf16[4,136,512]{2,1,0:T(8,128)(2,1)S(1)}, bf16[4,136,512]{2,1,0:T(8,128)(2,1)S(1)}, u32[]{:S(2)}, u32[]{:S(2)}) collective-permute-start(bf16[4,136,512]{2,1,0:T(8,128)(2,1)S(1)} %bitcast.37), channel_id=1, source_target_pairs={{0,64},{64,0},{1,65},{65,1},{2,66},{66,2},{3,67},{67,3},{4,68},{68... | collective-permute-start | bytes 1671176 | tf_op jit(solution)/shard_map/ppermute | solution.py:52
  180.3 1.6 convolution_bitcast_fusion
  181.9 2.5 %subtract_convert_fusion = (bf16[448,512]{1,0:T(8,128)(2,1)}, f32[448,512]{1,0:T(8,128)}, f32[448,512]{1,0:T(8,128)}) fusion(bf16[448,512]{1,0:T(8,128)(2,1)S(1)} %copy-done.7, f32[448,512]{1,0:T(8,128)S(1)} %copy-done.4, f32[448,512]{1,0:T(8,128)S(1)} %copy-done.5, f32[448,512]{1,0:T(8,128)S(1)} %convolution_bitcast_fusion, ...), kind=kOutput, calls=%fused_computation.11 | convolution fusion | flops 253231104 | bytes 6520832 | tf_op jit(solution)/shard_map/dot_general | solution.py:286
  (66 shorter events, 10.3 us)
Async XLA Ops:
  7.2 60.9 %all-gather.4.cloned.1.call-start = ((), (), s32[]{:S(2)}) async-start(), calls=%async_computation.5 | async-start | bytes 2293760 | tf_op jit(solution)/shard_map/all_gather | solution.py:220
  7.9 38.7 %copy-start.3 = (f32[448]{0:T(512)S(1)}, f32[448]{0:T(512)}, u32[]{:S(2)}) copy-start(f32[448]{0:T(512)} %param.11) | copy-start | bytes 5380
  7.9 41.3 %copy-start.6 = (bf16[448,512]{1,0:T(8,128)(2,1)S(1)}, bf16[448,512]{1,0:T(8,128)(2,1)}, u32[]{:S(2)}) copy-start(bf16[448,512]{1,0:T(8,128)(2,1)} %param.8) | copy-start | bytes 1376260
  9.3 29.2 %all-to-all-start = ((bf16[8,8,448]{2,1,0:T(8,128)(2,1)}), bf16[8,8,448]{2,1,0:T(8,128)(2,1)S(1)}, u32[]{:S(2)}, u32[]{:S(2)}) async-start(bf16[8,8,448]{2,1,0:T(8,128)(2,1)} %bitcast.1), calls=%async_computation | async-start | bytes 131072 | tf_op jit(solution)/shard_map/all_to_all | solution.py:228
  39.8 31.1 %all-to-all-start.1 = ((bf16[16,4,8,896]{3,2,1,0:T(8,128)(2,1)}), bf16[16,4,8,896]{3,2,1,0:T(8,128)(2,1)S(1)}, u32[]{:S(2)}, u32[]{:S(2)}) async-start(bf16[16,4,8,896]{3,2,1,0:T(8,128)(2,1)} %broadcast_in_dim.25), calls=%async_computation.1 | async-start | bytes 1835008 | tf_op jit(solution)/shard_map/all_to_all | solution.py:48
  46.6 4.5 %collective-permute-start = (f32[448]{0:T(512)S(1)}, f32[448]{0:T(512)S(1)}, u32[]{:S(2)}, u32[]{:S(2)}) collective-permute-start(f32[448]{0:T(512)S(1)} %copy-done.3), channel_id=1, source_target_pairs={{0,64},{64,0},{1,65},{65,1},{2,66},{66,2},{3,67},{67,3},{4,68},{68... | collective-permute-start | bytes 5384 | tf_op jit(solution)/shard_map/ppermute | solution.py:52
  49.2 21.8 %collective-permute-start.4 = (bf16[448,512]{1,0:T(8,128)(2,1)S(1)}, bf16[448,512]{1,0:T(8,128)(2,1)S(1)}, u32[]{:S(2)}, u32[]{:S(2)}) collective-permute-start(bf16[448,512]{1,0:T(8,128)(2,1)S(1)} %copy-done.6), channel_id=1, source_target_pairs={{0,64},{64,0},{1,65},{65,1},{2,66},{66,2},{3,67},{67,3},{4,68},{68... | collective-permute-start | bytes 1376264 | tf_op jit(solution)/shard_map/ppermute | solution.py:52
  51.5 19.5 %collective-permute-start.1 = (bf16[1,24,512]{2,1,0:T(8,128)(2,1)S(1)}, bf16[1,24,512]{2,1,0:T(8,128)(2,1)S(1)}, u32[]{:S(2)}, u32[]{:S(2)}) collective-permute-start(bf16[1,24,512]{2,1,0:T(8,128)(2,1)S(1)} %get-tuple-element.33), channel_id=1, source_target_pairs={{0,128},{128,256},{256,384},{384,0},{1,129},{129,257},{257,385},{3... | collective-permute-start | bytes 73736 | tf_op jit(solution)/shard_map/ppermute | solution.py:249
  55.2 15.8 %collective-permute-start.2 = (bf16[1,24,512]{2,1,0:T(8,128)(2,1)S(1)}, bf16[1,24,512]{2,1,0:T(8,128)(2,1)S(1)}, u32[]{:S(2)}, u32[]{:S(2)}) collective-permute-start(bf16[1,24,512]{2,1,0:T(8,128)(2,1)S(1)} %get-tuple-element.32), channel_id=1, source_target_pairs={{0,256},{128,384},{256,0},{384,128},{1,257},{129,385},{257,1},{385... | collective-permute-start | bytes 73736 | tf_op jit(solution)/shard_map/ppermute | solution.py:249
  57.4 13.6 %collective-permute-start.3 = (bf16[1,24,512]{2,1,0:T(8,128)(2,1)S(1)}, bf16[1,24,512]{2,1,0:T(8,128)(2,1)S(1)}, u32[]{:S(2)}, u32[]{:S(2)}) collective-permute-start(bf16[1,24,512]{2,1,0:T(8,128)(2,1)S(1)} %get-tuple-element.31), channel_id=1, source_target_pairs={{0,384},{128,0},{256,128},{384,256},{1,385},{129,1},{257,129},{385... | collective-permute-start | bytes 73736 | tf_op jit(solution)/shard_map/ppermute | solution.py:249
  68.1 22.7 %collective-permute-start.5 = (bf16[1792,512]{1,0:T(8,128)(2,1)}, bf16[1792,512]{1,0:T(8,128)(2,1)}, u32[]{:S(2)}, u32[]{:S(2)}) collective-permute-start(bf16[1792,512]{1,0:T(8,128)(2,1)} %all-gather.4.cloned.1.call-done.here_ref), channel_id=1, source_target_pairs={{0,64},{64,0},{1,65},{65,1},{2,66},{66,2},{3,67},{67,3},{4,68},{68... | collective-permute-start | bytes 5505032 | tf_op jit(solution)/shard_map/ppermute | solution.py:52
  72.5 18.2 %copy-start = (bf16[1792,512]{1,0:T(8,128)(2,1)S(1)}, bf16[1792,512]{1,0:T(8,128)(2,1)}, u32[]{:S(2)}) copy-start(bf16[1792,512]{1,0:T(8,128)(2,1)} %all-gather.4.cloned.1.call-done.here_ref) | copy-start | bytes 5505028
  72.5 18.2 %copy-start.1 = (f32[512]{0:T(512)S(1)}, f32[512]{0:T(512)}, u32[]{:S(2)}) copy-start(f32[512]{0:T(512)} %param.9) | copy-start | bytes 6148
  72.6 18.2 %all-to-all-start.2 = ((bf16[4,128,512]{2,1,0:T(8,128)(2,1)}), bf16[4,128,512]{2,1,0:T(8,128)(2,1)S(1)}, u32[]{:S(2)}, u32[]{:S(2)}) async-start(bf16[4,128,512]{2,1,0:T(8,128)(2,1)} %bitcast.40), calls=%async_computation.2 | async-start | bytes 1048576 | tf_op jit(solution)/shard_map/all_to_all | solution.py:258
  77.4 60.1 %collective-permute-start.6 = (bf16[512,448]{1,0:T(8,128)(2,1)}, bf16[512,448]{1,0:T(8,128)(2,1)}, u32[]{:S(2)}, u32[]{:S(2)}) collective-permute-start(bf16[512,448]{1,0:T(8,128)(2,1)} %get-tuple-element.30), channel_id=1, source_target_pairs={{0,64},{64,0},{1,65},{65,1},{2,66},{66,2},{3,67},{67,3},{4,68},{68... | collective-permute-start | bytes 1376264 | tf_op jit(solution)/shard_map/ppermute | solution.py:52
  95.0 21.2 %all-to-all-start.3 = ((bf16[16,8,3584]{2,1,0:T(8,128)(2,1)}), bf16[16,8,3584]{2,1,0:T(8,128)(2,1)}, u32[]{:S(2)}, u32[]{:S(2)}) async-start(bf16[16,8,3584]{2,1,0:T(8,128)(2,1)} %bitcast.11), calls=%async_computation.3 | async-start | bytes 1835008 | tf_op jit(solution)/shard_map/all_to_all | solution.py:272
  155.6 26.3 %copy-start.2 = (bf16[512,448]{1,0:T(8,128)(2,1)S(1)}, bf16[512,448]{1,0:T(8,128)(2,1)}, u32[]{:S(2)}) copy-start(bf16[512,448]{1,0:T(8,128)(2,1)} %get-tuple-element.29) | copy-start | bytes 1376260
  155.6 26.3 %copy-start.4 = (f32[448,512]{1,0:T(8,128)S(1)}, f32[448,512]{1,0:T(8,128)}, u32[]{:S(2)}) copy-start(f32[448,512]{1,0:T(8,128)} %param.12) | copy-start | bytes 2752516
  155.6 26.3 %copy-start.5 = (f32[448,512]{1,0:T(8,128)S(1)}, f32[448,512]{1,0:T(8,128)}, u32[]{:S(2)}) copy-start(f32[448,512]{1,0:T(8,128)} %param.13) | copy-start | bytes 2752516
  155.6 26.3 %copy-start.7 = (bf16[448,512]{1,0:T(8,128)(2,1)S(1)}, bf16[448,512]{1,0:T(8,128)(2,1)}, u32[]{:S(2)}) copy-start(bf16[448,512]{1,0:T(8,128)(2,1)} %param.8) | copy-start | bytes 1376260
  169.0 11.3 %collective-permute-start.7 = (bf16[4,136,512]{2,1,0:T(8,128)(2,1)S(1)}, bf16[4,136,512]{2,1,0:T(8,128)(2,1)S(1)}, u32[]{:S(2)}, u32[]{:S(2)}) collective-permute-start(bf16[4,136,512]{2,1,0:T(8,128)(2,1)S(1)} %bitcast.37), channel_id=1, source_target_pairs={{0,64},{64,0},{1,65},{65,1},{2,66},{66,2},{3,67},{67,3},{4,68},{68... | collective-permute-start | bytes 1671176 | tf_op jit(solution)/shard_map/ppermute | solution.py:52
Sparse Core Ops, SparseCore 0:
  10.1 57.9 all-gather.3

commit v7 on v6

--- a/solution.py
+++ b/solution.py
@@ -57,13 +57,14 @@
 
 
 def start_blocks(sources, held, sems):
-    step = sources[0].shape[0] // CHIPS
+    step = sources[0].shape[0]
     found = []
-    for chip in range(CHIPS):
-        for k, source in enumerate(sources):
-            place = chip * len(sources) + k
-            rows, there = pl.ds(chip * step, step), pl.ds(place * step, step)
-            found.append(pltpu.make_async_copy(source.at[rows], held.at[there], sems.at[place]))
+    for place, source in enumerate(sources):
+        first = step if source.shape[0] > step else 0
+        there = pl.ds(place * step, step)
+        found.append(
+            pltpu.make_async_copy(source.at[pl.ds(first, step)], held.at[there], sems.at[place])
+        )
     for copy in found:
         copy.start()
     return found
@@ -74,11 +75,10 @@
         copy.wait()
 
 
-def decode_kernel(
-    quarter_ref, bias_ref, here_ref, there_ref, out_ref, codes_ref, slopes_ref, held, sems
-):
+def decode_kernel(quarter_ref, bias_ref, *refs):
+    *dec_refs, out_ref, codes_ref, slopes_ref, held, sems = refs
     step = held.shape[0] // CHIPS
-    blocks = start_blocks((here_ref, there_ref), held, sems)
+    blocks = start_blocks(dec_refs, held, sems)
     sums = jnp.sum(quarter_ref[...].astype(F32), axis=0)
     scaled = sharpness * (sums + bias_ref[...])
     small = jnp.exp(-jnp.abs(scaled))
@@ -103,11 +103,11 @@
     return pl.BlockSpec(memory_space=pltpu.VMEM)
 
 
-def decode(quarter, enc_bias, dec_here, dec_there, tokens):
-    wide, latents = CORES * dec_here.shape[0], dec_here.shape[1]
+def decode(quarter, enc_bias, dec_blocks, tokens):
+    wide, latents = PARTS * dec_blocks[0].shape[0], dec_blocks[0].shape[1]
     return pl.pallas_call(
         decode_kernel,
-        in_specs=[whole(), whole(), in_hbm(), in_hbm()],
+        in_specs=[whole(), whole(), *[in_hbm()] * PARTS],
         out_specs=[whole(), whole(), whole()],
         out_shape=[
             jax.ShapeDtypeStruct((tokens, wide), BF),
@@ -122,7 +122,7 @@
             transcendentals=3 * tokens * latents,
         ),
         name="decode",
-    )(quarter, enc_bias.reshape(1, latents), dec_here, dec_there)
+    )(quarter, enc_bias.reshape(1, latents), *dec_blocks)
 
 
 def row_sum(rows, first, last):
@@ -130,16 +130,17 @@
     return jnp.sum(jnp.where((row >= first) & (row < last), rows, 0.0), axis=0, keepdims=True)
 
 
-def error_kernel(scale, got_ref, extra_ref, mask_ref, out_ref):
+def error_kernel(scale, got_ref, mask_ref, *refs):
+    *extra_refs, out_ref = refs
     small, longer = got_ref.shape[1:]
     wide = longer - LANES
-    left = wide // CHIPS - extra_ref.shape[2]
-    extra = extra_ref[...].astype(F32)
     target = []
-    for chip in range(CHIPS):
-        biases = extra[chip, 2 * small :]
-        target.append(extra[chip, :small] - row_sum(biases, 0, 3))
-        target.append((extra[chip, small : 2 * small] - row_sum(biases, 3, 6))[:, :left])
+    for extra_ref in extra_refs:
+        extra = extra_ref[...][0].astype(F32)
+        left = wide // CHIPS - extra.shape[1]
+        biases = extra[2 * small :]
+        target.append(extra[:small] - row_sum(biases, 0, 3))
+        target.append((extra[small : 2 * small] - row_sum(biases, 3, 6))[:, :left])
     total = jnp.sum(got_ref[...].astype(F32), axis=0)
     error = total[:, :wide] - jnp.concatenate(target, axis=1)
     squares = jnp.zeros((small, LANES), F32)
@@ -151,7 +152,7 @@
     out_ref[...] = jnp.broadcast_to(row[None], out_ref.shape)
 
 
-def error_copies(got, extra, mask, scale):
+def error_copies(got, extras, mask, scale):
     rows, longer = got.shape[1:]
     return pl.pallas_call(
         functools.partial(error_kernel, scale),
@@ -161,15 +162,14 @@
             flops=10 * rows * longer, bytes_accessed=60 * rows * longer, transcendentals=0
         ),
         name="error",
-    )(got, extra, mask)
-
-
-def back_kernel(
-    scale, grad_ref, here_ref, there_ref, slopes_ref, norms_ref, out_ref, held, sems
-):
+    )(got, mask, *extras)
+
+
+def back_kernel(scale, grad_ref, slopes_ref, norms_ref, *refs):
+    *dec_refs, out_ref, held, sems = refs
     wide, latents = held.shape
     step = wide // CHIPS
-    blocks = start_blocks((here_ref, there_ref), held, sems)
+    blocks = start_blocks(dec_refs, held, sems)
     sums = jnp.sum(grad_ref[:, wide:].astype(F32), axis=0, keepdims=True)
     high, low = pieces(sums, 2)
     row = lax.broadcasted_iota(jnp.int32, (8, LANES), 0)
@@ -186,12 +186,12 @@
     out_ref[...] = jnp.concatenate([code_grad * slopes_ref[...], block], axis=0).astype(BF)
 
 
-def back(grads, dec_here, dec_there, slopes, norms, scale):
+def back(grads, dec_blocks, slopes, norms, scale):
     tokens = grads.shape[0]
-    wide, latents = CORES * dec_here.shape[0], dec_here.shape[1]
+    wide, latents = PARTS * dec_blocks[0].shape[0], dec_blocks[0].shape[1]
     return pl.pallas_call(
         functools.partial(back_kernel, scale),
-        in_specs=[whole(), in_hbm(), in_hbm(), whole(), whole()],
+        in_specs=[whole(), whole(), whole(), *[in_hbm()] * PARTS],
         out_specs=whole(),
         out_shape=jax.ShapeDtypeStruct((tokens + 8, latents), BF),
         scratch_shapes=[pltpu.VMEM((wide, latents), BF), pltpu.SemaphoreType.DMA((PARTS,))],
@@ -202,7 +202,7 @@
             transcendentals=0,
         ),
         name="back",
-    )(grads, dec_here, dec_there, slopes, norms.reshape(1, latents))
+    )(grads, slopes, norms.reshape(1, latents), *dec_blocks)
 
 
 def body(acts, enc_weight, enc_bias, dec_weight, dec_bias, enc_moment, enc_second):
@@ -217,10 +217,15 @@
     small = HIGH * share
     tokens = BLOCKS * small
 
-    dec_here = lax.all_gather(dec_weight.T, "zl", axis=0, tiled=True)
-    dec_there = swap(dec_here)
-    enc_there = swap(enc_weight)
-    bias_there = swap(dec_bias)
+    def shifted(value, away):
+        return lax.ppermute(value, "zl", [(i, (i + away) % CHIPS) for i in range(CHIPS)])
+
+    dec_own = dec_weight.T
+    dec_first, dec_last = shifted(dec_own, 1), shifted(dec_own, CHIPS - 1)
+    bias_here = jnp.stack(pieces(dec_bias, 3))
+    bias_block = jnp.pad(bias_here, ((0, 13), (0, latents - chans)))
+    swapped = swap(jnp.concatenate([enc_weight, dec_own, bias_block], axis=0))
+    enc_there, bias_there = swapped[:chans], swapped[2 * chans : 2 * chans + 3, :chans]
 
     padded = jnp.concatenate([acts, jnp.zeros((1, chans), BF)], axis=0)
     halves = jnp.broadcast_to(padded.reshape(CORES, 1, half, chans), (CORES, HIGH, half, chans))
@@ -230,39 +235,49 @@
     column = jnp.where(core == 0, column, column[::-1])
     column = column.transpose(2, 1, 3, 0, 4)
     column = column.reshape(CHIPS, small, 2 * chans)
+    column, dec_first = lax.optimization_barrier((column, dec_first))
+    dec_second = shifted(dec_first, 1)
     gathered = spread(column, PLANE, BLOCKS).transpose(1, 0, 2, 3)
     gathered = gathered.reshape(CHIPS * tokens, 2 * chans)
 
+    acts_here = gathered[:, :chans]
+    acts_there = swap(gathered[:, chans:])
+    enc_pair = jnp.concatenate([enc_weight, enc_there], axis=0)
+    sums = jnp.dot(gathered, enc_pair, preferred_element_type=F32).astype(BF)
+    sums, dec_second, dec_last = lax.optimization_barrier((sums, dec_second, dec_last))
+    dec_blocks = [dec_own, swapped]
+    for block in (dec_first, dec_second, dec_last):
+        dec_blocks += [block, swap(block)]
+    quarter = lax.all_to_all(sums.reshape(CHIPS, tokens, latents), "zl", 0, 0, tiled=True)
+    partial_value, codes, slopes = decode(quarter, enc_bias, dec_blocks, tokens)
+
+    column, partial_value = lax.optimization_barrier((column, partial_value))
     def folded(rows_of):
         fill = [(0, 0)] * (rows_of.ndim - 1) + [(0, 2 * latents - 2 * chans)]
         rest = jnp.pad(rows_of[..., latents:], fill)
         return jnp.concatenate([rows_of[..., :latents], rest], axis=-2)
 
-    bias_rows = folded(jnp.stack(pieces(jnp.concatenate([dec_bias, bias_there]), 3)))
+    bias_rows = folded(jnp.concatenate([bias_here, bias_there], axis=1))
     bias_rows = jnp.pad(bias_rows, ((0, small - 6), (0, 0)))
     bias_rows = jnp.broadcast_to(bias_rows[None], (CHIPS, small, latents))
     extra = jnp.concatenate([folded(column), bias_rows], axis=1)
-    came = []
+    mine = []
     for away in range(CHIPS):
         block = lax.dynamic_index_in_dim(extra, (chip + away) & (CHIPS - 1), 0)
-        ways = [(i, (i + away) % CHIPS) for i in range(CHIPS)]
-        came.append(lax.ppermute(block, "zl", ways) if away else block)
-    gathered, *came = lax.optimization_barrier((gathered, *came))
-    turned = jnp.concatenate([came[-k % CHIPS] for k in range(2 * CHIPS - 1)], axis=0)
-    mine = lax.dynamic_slice_in_dim(turned, (CHIPS - chip) & (CHIPS - 1), CHIPS, axis=0)
-
-    acts_here = gathered[:, :chans]
-    acts_there = swap(gathered[:, chans:])
-    enc_pair = jnp.concatenate([enc_weight, enc_there], axis=0)
-    sums = jnp.dot(gathered, enc_pair, preferred_element_type=F32).astype(BF)
-    quarter = lax.all_to_all(sums.reshape(CHIPS, tokens, latents), "zl", 0, 0, tiled=True)
-    partial_value, codes, slopes = decode(quarter, enc_bias, dec_here, dec_there, tokens)
-
-    dec_norms = jnp.zeros((latents,), F32)
-    for layer in range(LAYERS):
-        rows_of = slice(layer * CHIPS // LAYERS * chans, (layer + 1) * CHIPS // LAYERS * chans)
-        near, far = dec_here[rows_of].astype(F32), dec_there[rows_of].astype(F32)
-        dec_norms = dec_norms + jnp.sqrt(jnp.sum(near * near + far * far, axis=0))
+        mine.append(shifted(block, away) if away else block)
+
+    def squares(block):
+        block = block.astype(F32)
+        return jnp.sum(block * block, axis=0)
+
+    per_layer = [jnp.zeros((latents,), F32)] * LAYERS
+    for away in range(CHIPS):
+        near, far = dec_blocks[2 * away], dec_blocks[2 * away + 1]
+        far = far if away else far[chans : 2 * chans]
+        found = squares(near) + squares(far)
+        layer = ((chip - away) & (CHIPS - 1)) // (CHIPS // LAYERS)
+        per_layer = [t + jnp.where(layer == k, found, 0.0) for k, t in enumerate(per_layer)]
+    dec_norms = sum(jnp.sqrt(t) for t in per_layer)
 
     place = lax.broadcasted_iota(jnp.int32, (small, LANES), 0) & (share - 1)
     real = (core * half + chip * share + place < rows).astype(F32)
@@ -273,11 +288,11 @@
         partial_value.reshape(BLOCKS, small, wide), PLANE, 0, 0, tiled=True
     )
     summed = jnp.sum(got.astype(F32), axis=0).astype(BF)
-    again = lax.all_gather(jnp.concatenate([summed, sparse.astype(BF)], axis=1), "zh", axis=0)
+    again = spread(jnp.concatenate([summed, sparse.astype(BF)], axis=1), "zh", HIGH)
     again, acts_there = lax.optimization_barrier((again, acts_there))
     copies = error_copies(again, mine, real, inv_batch)
     grads = lax.all_to_all(copies, PLANE, 0, 0, tiled=True)
-    last = back(grads.reshape(tokens, wide + LANES), dec_here, dec_there, slopes, dec_norms, inv_batch)
+    last = back(grads.reshape(tokens, wide + LANES), dec_blocks, slopes, dec_norms, inv_batch)
     pre_here = lax.all_gather(last, "zl", axis=0)
     pre_there = swap(pre_here)
 

time: 193 us -> 195 us (1.010)
  starting transfers between devices: 62.8 us -> 83.9 us
  blocking collectives: 48.7 us -> 30.9 us
  between operations: 14.5 us -> 1.1 us
  local copies, waits for them, and re-layouts: 4.11 us -> 11 us
  Pallas kernels: 6.86 us -> 10.2 us
  other arithmetic: 4.5 us -> 7.17 us
    all_gather x1 -> x0, blocking collectives: 20 us -> none  [body(): lax.all_gather(jnp.concatenate([summed, sparse.astype(BF)], axis=1), 'zh'...]
    ppermute x3 -> x6, waiting for transfers between devices: 0.01 us -> 10.8 us  [shifted(): lax.ppermute(value, 'zl', [(i, (i + away) % CHIPS) for i in range(CHIPS)])]
    all_to_all x1 -> x2, starting transfers between devices: 6.75 us -> 15.6 us  [spread(): return lax.all_to_all(copies, axes, 0, 0, tiled=True)]
    all_to_all x1 -> x2, waiting for transfers between devices: 0.01 us -> 8.44 us  [spread(): return lax.all_to_all(copies, axes, 0, 0, tiled=True)]
    all_to_all x1, waiting for transfers between devices: 12.6 us -> 4.79 us  [body(): column = lax.all_to_all(halves, ('core', 'zh'), 0, 0, tiled=True)]
    all_to_all x1, waiting for transfers between devices: 11.3 us -> 4.61 us  [body(): lax.all_to_all(sums.reshape(CHIPS, tokens, latents), 'zl', 0, 0, tiled=True)]
    ppermute x3 -> x6, starting transfers between devices: 10.2 us -> 16.9 us  [shifted(): lax.ppermute(value, 'zl', [(i, (i + away) % CHIPS) for i in range(CHIPS)])]
    all_gather x1 -> x0, waiting for transfers between devices: 6.37 us -> none  [body(): dec_here = lax.all_gather(dec_weight.T, 'zl', axis=0, tiled=True)]
  transfers between devices with their start and end apart: 13 -> 17, of which waited for: 5 -> 8; matrix products, arithmetic and copies ran while one was open for 5% -> 8% of each run, Pallas kernels for 2% -> 0%
where the time goes in v7:
time: 195 us; the launch traced here: 194 us
  starting transfers between devices  83.9 us (43%)
  waiting for transfers between devices  43.6 us (22%)
  blocking collectives  30.9 us (16%)
  local copies, waits for them, and re-layouts  11 us (6%)
  Pallas kernels  10.2 us (5%)
  other arithmetic  7.17 us (4%)
  matrix products  5.78 us (3%)
    ppermute x6, starting transfers between devices, swap(): return lax.ppermute(value, 'core', [(0, 1), (1, 0)])  22.2 us
    all_to_all x1, blocking collectives, body(): grads = lax.all_to_all(copies, PLANE, 0, 0, tiled=True)  18.3 us
    ppermute x6, starting transfers between devices, shifted(): lax.ppermute(value, 'zl', [(i, (i + away) % CHIPS) for i in range(CHIPS)])  16.9 us
    all_to_all x1, starting transfers between devices, body(): column = lax.all_to_all(halves, ('core', 'zh'), 0, 0, tiled=True)  16.6 us
    all_to_all x2, starting transfers between devices, spread(): return lax.all_to_all(copies, axes, 0, 0, tiled=True)  15.6 us
    all_to_all x1, waiting for transfers between devices, body(): lax.all_to_all(partial_value.reshape(BLOCKS, small, wide), PLANE, 0, 0, t...  13.4 us
    all_gather x1, blocking collectives, body(): pre_here = lax.all_gather(last, 'zl', axis=0)  12.6 us
    ppermute x6, waiting for transfers between devices, shifted(): lax.ppermute(value, 'zl', [(i, (i + away) % CHIPS) for i in range(CHIPS)])  10.8 us
  transfers between devices with their start and end apart: 17, of which 8 were waited for; matrix products, arithmetic and copies ran while one was open for 8% of the time, Pallas kernels for 0%

profile of v7, /device:TPU:1, one launch (start us, length us, event | category | flops | bytes accessed | tf_op | source)
XLA Modules:
  0.0 193.6 jit_solution(6725043186666228791)
XLA Ops:
  2.0 16.6 %all-to-all-start = ((bf16[8,8,448]{2,1,0:T(8,128)(2,1)}), bf16[8,8,448]{2,1,0:T(8,128)(2,1)S(1)}, u32[]{:S(2)}, u32[]{:S(2)}) async-start(bf16[8,8,448]{2,1,0:T(8,128)(2,1)} %bitcast.1), calls=%async_computation | async-start | bytes 131072 | tf_op jit(solution)/shard_map/all_to_all | solution.py:233
  18.6 2.6 %collective-permute-start = (bf16[448,512]{1,0:T(8,128)(2,1)}, bf16[448,512]{1,0:T(8,128)(2,1)S(1)}, u32[]{:S(2)}, u32[]{:S(2)}) collective-permute-start(bf16[448,512]{1,0:T(8,128)(2,1)} %bitcast.29), channel_id=1, source_target_pairs={{0,128},{128,256},{256,384},{384,0},{1,129},{129,257},{257,385},{3... | collective-permute-start | bytes 1376264 | tf_op jit(solution)/shard_map/ppermute | solution.py:221
  26.4 4.8 %all-to-all-done = bf16[8,8,448]{2,1,0:T(8,128)(2,1)S(1)} async-done(((bf16[8,8,448]{2,1,0:T(8,128)(2,1)}), bf16[8,8,448]{2,1,0:T(8,128)(2,1)S(1)}, u32[]{:S(2)}, u32[]{:S(2)}) %all-to-all-start) | async-done | bytes 57376 | tf_op jit(solution)/shard_map/all_to_all | solution.py:233
  31.5 5.4 %collective-permute-done.refs_2_ = bf16[448,512]{1,0:T(8,128)(2,1)S(1)} collective-permute-done((bf16[448,512]{1,0:T(8,128)(2,1)}, bf16[448,512]{1,0:T(8,128)(2,1)S(1)}, u32[]{:S(2)}, u32[]{:S(2)}) %collective-permute-start) | collective-permute-done | bytes 458784 | tf_op jit(solution)/shard_map/ppermute | solution.py:221
  37.8 6.9 %all-to-all-start.1 = ((bf16[16,4,8,896]{3,2,1,0:T(8,128)(2,1)}), bf16[16,4,8,896]{3,2,1,0:T(8,128)(2,1)}, u32[]{:S(2)}, u32[]{:S(2)}) async-start(bf16[16,4,8,896]{3,2,1,0:T(8,128)(2,1)} %broadcast_in_dim.40), calls=%async_computation.1 | async-start | bytes 1835008 | tf_op jit(solution)/shard_map/all_to_all | solution.py:48
  46.7 3.4 %collective-permute-start.2 = (bf16[448,512]{1,0:T(8,128)(2,1)S(1)}, bf16[448,512]{1,0:T(8,128)(2,1)S(1)}, u32[]{:S(2)}, u32[]{:S(2)}) collective-permute-start(bf16[448,512]{1,0:T(8,128)(2,1)S(1)} %collective-permute-done.refs_2_), channel_id=1, source_target_pairs={{0,128},{128,256},{256,384},{384,0},{1,129},{129,257},{257,385},{3... | collective-permute-start | bytes 1376264 | tf_op jit(solution)/shard_map/ppermute | solution.py:221
  51.0 8.4 %all-to-all-done.1 = bf16[16,4,8,896]{3,2,1,0:T(8,128)(2,1)} async-done(((bf16[16,4,8,896]{3,2,1,0:T(8,128)(2,1)}), bf16[16,4,8,896]{3,2,1,0:T(8,128)(2,1)}, u32[]{:S(2)}, u32[]{:S(2)}) %all-to-all-start.1) | async-done | bytes 917536 | tf_op jit(solution)/shard_map/all_to_all | solution.py:48
  62.3 3.8 %collective-permute-done.2.refs_4_ = bf16[448,512]{1,0:T(8,128)(2,1)S(1)} collective-permute-done((bf16[448,512]{1,0:T(8,128)(2,1)S(1)}, bf16[448,512]{1,0:T(8,128)(2,1)S(1)}, u32[]{:S(2)}, u32[]{:S(2)}) %collective-permute-start.2) | collective-permute-done | bytes 458784 | tf_op jit(solution)/shard_map/ppermute | solution.py:221
  66.1 5.9 %all-to-all-start.2 = ((bf16[4,128,512]{2,1,0:T(8,128)(2,1)}), bf16[4,128,512]{2,1,0:T(8,128)(2,1)}, u32[]{:S(2)}, u32[]{:S(2)}) async-start(bf16[4,128,512]{2,1,0:T(8,128)(2,1)} %bitcast.8), calls=%async_computation.2 | async-start | bytes 1048576 | tf_op jit(solution)/shard_map/all_to_all | solution.py:251
  72.0 3.5 %collective-permute-start.4 = (bf16[448,512]{1,0:T(8,128)(2,1)S(1)}, bf16[448,512]{1,0:T(8,128)(2,1)S(1)}, u32[]{:S(2)}, u32[]{:S(2)}) collective-permute-start(bf16[448,512]{1,0:T(8,128)(2,1)S(1)} %collective-permute-done.refs_2_), channel_id=1, source_target_pairs={{0,64},{64,0},{1,65},{65,1},{2,66},{66,2},{3,67},{67,3},{4,68},{68... | collective-permute-start | bytes 1376264 | tf_op jit(solution)/shard_map/ppermute | solution.py:52
  81.5 4.6 %all-to-all-done.2.quarter_ref = bf16[4,128,512]{2,1,0:T(8,128)(2,1)} async-done(((bf16[4,128,512]{2,1,0:T(8,128)(2,1)}), bf16[4,128,512]{2,1,0:T(8,128)(2,1)}, u32[]{:S(2)}, u32[]{:S(2)}) %all-to-all-start.2) | async-done | bytes 524320 | tf_op jit(solution)/shard_map/all_to_all | solution.py:251
  86.1 6.0 %decode.1 = (bf16[128,3584]{1,0:T(8,128)(2,1)}, bf16[128,512]{1,0:T(8,128)(2,1)S(1)}, f32[128,512]{1,0:T(8,128)S(1)}) custom-call(bf16[4,128,512]{2,1,0:T(8,128)(2,1)} %all-to-all-done.2.quarter_ref, f32[1,512]{1,0:T(1,128)S(1)} %bitcast.35, bf16[448,512]{1,0:T(8,128)(2,1)S(1)} %bitcast.32, bf16[912,512]{1,0:T(8,128)(2,1)} %copy-done.4, ...), custom_call_target="tpu_custom_call" | custom-call | flops 469762048 | bytes 4587520 | tf_op jit(solution)/shard_map/decode/pallas_call | solution.py:108
  92.8 6.7 %all-to-all-start.3 = ((bf16[16,8,3584]{2,1,0:T(8,128)(2,1)}), bf16[16,8,3584]{2,1,0:T(8,128)(2,1)}, u32[]{:S(2)}, u32[]{:S(2)}) async-start(bf16[16,8,3584]{2,1,0:T(8,128)(2,1)} %bitcast.39), calls=%async_computation.3 | async-start | bytes 1835008 | tf_op jit(solution)/shard_map/all_to_all | solution.py:287
  100.1 13.4 %all-to-all-done.3 = bf16[16,8,3584]{2,1,0:T(8,128)(2,1)} async-done(((bf16[16,8,3584]{2,1,0:T(8,128)(2,1)}), bf16[16,8,3584]{2,1,0:T(8,128)(2,1)}, u32[]{:S(2)}, u32[]{:S(2)}) %all-to-all-start.3) | async-done | bytes 917536 | tf_op jit(solution)/shard_map/all_to_all | solution.py:287
  115.5 8.7 %all-to-all-start.4 = ((bf16[4,8,3712]{2,1,0:T(8,128)(2,1)}), bf16[4,8,3712]{2,1,0:T(8,128)(2,1)S(1)}, u32[]{:S(2)}, u32[]{:S(2)}) async-start(bf16[4,8,3712]{2,1,0:T(8,128)(2,1)} %broadcast_in_dim.42), calls=%async_computation.4 | async-start | bytes 475136 | tf_op jit(solution)/shard_map/all_to_all | solution.py:48
  124.3 2.4 %fusion.33 = (bf16[512,448]{1,0:T(8,128)(2,1)}, bf16[512,448]{1,0:T(8,128)(2,1)}) fusion(bf16[512,896]{1,0:T(8,128)(2,1)} %bitcast.37), kind=kLoop, calls=%fused_computation.72 | loop fusion | bytes 1835008 | tf_op jit(solution)/shard_map/slice | solution.py:243
  126.7 5.0 %collective-permute-start.7 = (bf16[512,448]{1,0:T(8,128)(2,1)}, bf16[512,448]{1,0:T(8,128)(2,1)}, u32[]{:S(2)}, u32[]{:S(2)}) collective-permute-start(bf16[512,448]{1,0:T(8,128)(2,1)} %get-tuple-element.32), channel_id=1, source_target_pairs={{0,64},{64,0},{1,65},{65,1},{2,66},{66,2},{3,67},{67,3},{4,68},{68... | collective-permute-start | bytes 1376264 | tf_op jit(solution)/shard_map/ppermute | solution.py:52
  135.9 2.8 %collective-permute-start.9 = (bf16[1,24,512]{2,1,0:T(8,128)(2,1)}, bf16[1,24,512]{2,1,0:T(8,128)(2,1)S(1)}, u32[]{:S(2)}, u32[]{:S(2)}) collective-permute-start(bf16[1,24,512]{2,1,0:T(8,128)(2,1)} %get-tuple-element.34), channel_id=1, source_target_pairs={{0,256},{128,384},{256,0},{384,128},{1,257},{129,385},{257,1},{385... | collective-permute-start | bytes 73736 | tf_op jit(solution)/shard_map/ppermute | solution.py:221
  138.7 4.3 %collective-permute-start.10 = (bf16[1,24,512]{2,1,0:T(8,128)(2,1)}, bf16[1,24,512]{2,1,0:T(8,128)(2,1)S(1)}, u32[]{:S(2)}, u32[]{:S(2)}) collective-permute-start(bf16[1,24,512]{2,1,0:T(8,128)(2,1)} %get-tuple-element.33), channel_id=1, source_target_pairs={{0,384},{128,0},{256,128},{384,256},{1,385},{129,1},{257,129},{385... | collective-permute-start | bytes 73736 | tf_op jit(solution)/shard_map/ppermute | solution.py:221
  144.8 18.3 %all_to_all.30 = bf16[16,8,3712]{2,1,0:T(8,128)(2,1)} all-to-all(bf16[16,8,3712]{2,1,0:T(8,128)(2,1)S(1)} %error.1), channel_id=1, replica_groups=mesh['zl'=4,'core'=2,'y'=4,'x'=4,'zh'=4] {'y','x'}, dimensions={0} | all-to-all | bytes 1900544 | tf_op jit(solution)/shard_map/all_to_all | solution.py:294
  163.1 4.1 %back.1 = bf16[136,512]{1,0:T(8,128)(2,1)S(1)} custom-call(bf16[128,3712]{1,0:T(8,128)(2,1)} %bitcast.38, f32[128,512]{1,0:T(8,128)S(1)} %copy-done.2, f32[1,512]{1,0:T(1,128)S(1)} %bitcast.34, bf16[448,512]{1,0:T(8,128)(2,1)S(1)} %bitcast.33, bf16[912,512]{1,0:T(8,128)(2,1)} %copy-done.4, bf16[448,512]{1,0:T(8,128)(2,1)S(1)} %collective-permute-done.refs_2_, ...), custom_call_target="tpu_custom_call" | custom-call | flops 469762048 | bytes 4587520 | tf_op jit(solution)/shard_map/back/pallas_call | solution.py:192
  167.2 12.6 %all-gather = bf16[544,512]{1,0:T(8,128)(2,1)S(1)} all-gather(bf16[136,512]{1,0:T(8,128)(2,1)S(1)} %back.1), channel_id=2, replica_groups=mesh['zl'=4,'core'=2,'y'=4,'x'=4,'zh'=4] {'zl'}, dimensions={0}, use_global_device_ids=true | all-gather | bytes 696320 | tf_op jit(solution)/shard_map/all_gather | solution.py:296
  179.8 7.2 %collective-permute-start.11 = (bf16[4,136,512]{2,1,0:T(8,128)(2,1)S(1)}, bf16[4,136,512]{2,1,0:T(8,128)(2,1)S(1)}, u32[]{:S(2)}, u32[]{:S(2)}) collective-permute-start(bf16[4,136,512]{2,1,0:T(8,128)(2,1)S(1)} %bitcast.40), channel_id=1, source_target_pairs={{0,64},{64,0},{1,65},{65,1},{2,66},{66,2},{3,67},{67,3},{4,68},{68... | collective-permute-start | bytes 1671176 | tf_op jit(solution)/shard_map/ppermute | solution.py:52
  190.5 2.5 %subtract_convert_fusion = (bf16[448,512]{1,0:T(8,128)(2,1)}, f32[448,512]{1,0:T(8,128)}, f32[448,512]{1,0:T(8,128)}) fusion(bf16[448,512]{1,0:T(8,128)(2,1)S(1)} %copy-done.8, f32[448,512]{1,0:T(8,128)S(1)} %copy-done.10, f32[448,512]{1,0:T(8,128)S(1)} %copy-done.11, f32[448,512]{1,0:T(8,128)S(1)} %convolution_bitcast_fusion, ...), kind=kOutput, calls=%fused_computation.10 | convolution fusion | flops 253231104 | bytes 6520832 | tf_op jit(solution)/shard_map/dot_general | solution.py:301
  (84 shorter events, 32.7 us)
Async XLA Ops:
  2.0 29.2 %all-to-all-start = ((bf16[8,8,448]{2,1,0:T(8,128)(2,1)}), bf16[8,8,448]{2,1,0:T(8,128)(2,1)S(1)}, u32[]{:S(2)}, u32[]{:S(2)}) async-start(bf16[8,8,448]{2,1,0:T(8,128)(2,1)} %bitcast.1), calls=%async_computation | async-start | bytes 131072 | tf_op jit(solution)/shard_map/all_to_all | solution.py:233
  18.6 18.2 %collective-permute-start = (bf16[448,512]{1,0:T(8,128)(2,1)}, bf16[448,512]{1,0:T(8,128)(2,1)S(1)}, u32[]{:S(2)}, u32[]{:S(2)}) collective-permute-start(bf16[448,512]{1,0:T(8,128)(2,1)} %bitcast.29), channel_id=1, source_target_pairs={{0,128},{128,256},{256,384},{384,0},{1,129},{129,257},{257,385},{3... | collective-permute-start | bytes 1376264 | tf_op jit(solution)/shard_map/ppermute | solution.py:221
  24.2 25.9 %collective-permute-start.1 = (bf16[912,512]{1,0:T(8,128)(2,1)}, bf16[912,512]{1,0:T(8,128)(2,1)S(1)}, u32[]{:S(2)}, u32[]{:S(2)}) collective-permute-start(bf16[912,512]{1,0:T(8,128)(2,1)} %pad_maximum_fusion), channel_id=1, source_target_pairs={{0,64},{64,0},{1,65},{65,1},{2,66},{66,2},{3,67},{67,3},{4,68},{68... | collective-permute-start | bytes 2801672 | tf_op jit(solution)/shard_map/ppermute | solution.py:52
  37.8 6.9 %copy-start = (bf16[512,448]{0,1:T(8,128)(2,1)S(1)}, bf16[512,448]{0,1:T(8,128)(2,1)}, u32[]{:S(2)}) copy-start(bf16[512,448]{0,1:T(8,128)(2,1)} %param.10) | copy-start | bytes 1376260
  37.8 21.6 %all-to-all-start.1 = ((bf16[16,4,8,896]{3,2,1,0:T(8,128)(2,1)}), bf16[16,4,8,896]{3,2,1,0:T(8,128)(2,1)}, u32[]{:S(2)}, u32[]{:S(2)}) async-start(bf16[16,4,8,896]{3,2,1,0:T(8,128)(2,1)} %broadcast_in_dim.40), calls=%async_computation.1 | async-start | bytes 1835008 | tf_op jit(solution)/shard_map/all_to_all | solution.py:48
  44.8 17.6 %collective-permute-start.3 = (bf16[448,512]{1,0:T(8,128)(2,1)S(1)}, bf16[448,512]{1,0:T(8,128)(2,1)S(1)}, u32[]{:S(2)}, u32[]{:S(2)}) collective-permute-start(bf16[448,512]{1,0:T(8,128)(2,1)S(1)} %bitcast.31), channel_id=1, source_target_pairs={{0,384},{128,0},{256,128},{384,256},{1,385},{129,1},{257,129},{385... | collective-permute-start | bytes 1376264 | tf_op jit(solution)/shard_map/ppermute | solution.py:221
  46.7 19.4 %collective-permute-start.2 = (bf16[448,512]{1,0:T(8,128)(2,1)S(1)}, bf16[448,512]{1,0:T(8,128)(2,1)S(1)}, u32[]{:S(2)}, u32[]{:S(2)}) collective-permute-start(bf16[448,512]{1,0:T(8,128)(2,1)S(1)} %collective-permute-done.refs_2_), channel_id=1, source_target_pairs={{0,128},{128,256},{256,384},{384,0},{1,129},{129,257},{257,385},{3... | collective-permute-start | bytes 1376264 | tf_op jit(solution)/shard_map/ppermute | solution.py:221
  50.1 10.7 %copy-start.4 = (bf16[912,512]{1,0:T(8,128)(2,1)}, bf16[912,512]{1,0:T(8,128)(2,1)S(1)}, u32[]{:S(2)}) copy-start(bf16[912,512]{1,0:T(8,128)(2,1)S(1)} %collective-permute-done.1.refs_1_) | copy-start | bytes 2801668
  66.1 20.0 %all-to-all-start.2 = ((bf16[4,128,512]{2,1,0:T(8,128)(2,1)}), bf16[4,128,512]{2,1,0:T(8,128)(2,1)}, u32[]{:S(2)}, u32[]{:S(2)}) async-start(bf16[4,128,512]{2,1,0:T(8,128)(2,1)} %bitcast.8), calls=%async_computation.2 | async-start | bytes 1048576 | tf_op jit(solution)/shard_map/all_to_all | solution.py:251
  72.0 8.2 %collective-permute-start.4 = (bf16[448,512]{1,0:T(8,128)(2,1)S(1)}, bf16[448,512]{1,0:T(8,128)(2,1)S(1)}, u32[]{:S(2)}, u32[]{:S(2)}) collective-permute-start(bf16[448,512]{1,0:T(8,128)(2,1)S(1)} %collective-permute-done.refs_2_), channel_id=1, source_target_pairs={{0,64},{64,0},{1,65},{65,1},{2,66},{66,2},{3,67},{67,3},{4,68},{68... | collective-permute-start | bytes 1376264 | tf_op jit(solution)/shard_map/ppermute | solution.py:52
  75.5 10.6 %copy-start.3 = (f32[512]{0:T(512)S(1)}, f32[512]{0:T(512)}, u32[]{:S(2)}) copy-start(f32[512]{0:T(512)} %param.9) | copy-start | bytes 6148
  75.7 5.8 %collective-permute-start.5 = (bf16[448,512]{1,0:T(8,128)(2,1)S(1)}, bf16[448,512]{1,0:T(8,128)(2,1)S(1)}, u32[]{:S(2)}, u32[]{:S(2)}) collective-permute-start(bf16[448,512]{1,0:T(8,128)(2,1)S(1)} %collective-permute-done.2.refs_4_), channel_id=1, source_target_pairs={{0,64},{64,0},{1,65},{65,1},{2,66},{66,2},{3,67},{67,3},{4,68},{68... | collective-permute-start | bytes 1376264 | tf_op jit(solution)/shard_map/ppermute | solution.py:52
  77.6 3.9 %collective-permute-start.6 = (bf16[448,512]{1,0:T(8,128)(2,1)S(1)}, bf16[448,512]{1,0:T(8,128)(2,1)S(1)}, u32[]{:S(2)}, u32[]{:S(2)}) collective-permute-start(bf16[448,512]{1,0:T(8,128)(2,1)S(1)} %collective-permute-done.3.refs_6_), channel_id=1, source_target_pairs={{0,64},{64,0},{1,65},{65,1},{2,66},{66,2},{3,67},{67,3},{4,68},{68... | collective-permute-start | bytes 1376264 | tf_op jit(solution)/shard_map/ppermute | solution.py:52
  92.8 20.7 %all-to-all-start.3 = ((bf16[16,8,3584]{2,1,0:T(8,128)(2,1)}), bf16[16,8,3584]{2,1,0:T(8,128)(2,1)}, u32[]{:S(2)}, u32[]{:S(2)}) async-start(bf16[16,8,3584]{2,1,0:T(8,128)(2,1)} %bitcast.39), calls=%async_computation.3 | async-start | bytes 1835008 | tf_op jit(solution)/shard_map/all_to_all | solution.py:287
  115.5 27.5 %all-to-all-start.4 = ((bf16[4,8,3712]{2,1,0:T(8,128)(2,1)}), bf16[4,8,3712]{2,1,0:T(8,128)(2,1)S(1)}, u32[]{:S(2)}, u32[]{:S(2)}) async-start(bf16[4,8,3712]{2,1,0:T(8,128)(2,1)} %broadcast_in_dim.42), calls=%async_computation.4 | async-start | bytes 475136 | tf_op jit(solution)/shard_map/all_to_all | solution.py:48
  126.7 16.3 %collective-permute-start.7 = (bf16[512,448]{1,0:T(8,128)(2,1)}, bf16[512,448]{1,0:T(8,128)(2,1)}, u32[]{:S(2)}, u32[]{:S(2)}) collective-permute-start(bf16[512,448]{1,0:T(8,128)(2,1)} %get-tuple-element.32), channel_id=1, source_target_pairs={{0,64},{64,0},{1,65},{65,1},{2,66},{66,2},{3,67},{67,3},{4,68},{68... | collective-permute-start | bytes 1376264 | tf_op jit(solution)/shard_map/ppermute | solution.py:52
  134.0 9.0 %collective-permute-start.8 = (bf16[1,24,512]{2,1,0:T(8,128)(2,1)}, bf16[1,24,512]{2,1,0:T(8,128)(2,1)S(1)}, u32[]{:S(2)}, u32[]{:S(2)}) collective-permute-start(bf16[1,24,512]{2,1,0:T(8,128)(2,1)} %get-tuple-element.35), channel_id=1, source_target_pairs={{0,128},{128,256},{256,384},{384,0},{1,129},{129,257},{257,385},{3... | collective-permute-start | bytes 73736 | tf_op jit(solution)/shard_map/ppermute | solution.py:221
  135.9 7.1 %collective-permute-start.9 = (bf16[1,24,512]{2,1,0:T(8,128)(2,1)}, bf16[1,24,512]{2,1,0:T(8,128)(2,1)S(1)}, u32[]{:S(2)}, u32[]{:S(2)}) collective-permute-start(bf16[1,24,512]{2,1,0:T(8,128)(2,1)} %get-tuple-element.34), channel_id=1, source_target_pairs={{0,256},{128,384},{256,0},{384,128},{1,257},{129,385},{257,1},{385... | collective-permute-start | bytes 73736 | tf_op jit(solution)/shard_map/ppermute | solution.py:221
  138.7 6.0 %collective-permute-start.10 = (bf16[1,24,512]{2,1,0:T(8,128)(2,1)}, bf16[1,24,512]{2,1,0:T(8,128)(2,1)S(1)}, u32[]{:S(2)}, u32[]{:S(2)}) collective-permute-start(bf16[1,24,512]{2,1,0:T(8,128)(2,1)} %get-tuple-element.33), channel_id=1, source_target_pairs={{0,384},{128,0},{256,128},{384,256},{1,385},{129,1},{257,129},{385... | collective-permute-start | bytes 73736 | tf_op jit(solution)/shard_map/ppermute | solution.py:221
  144.8 18.3 %copy-start.2 = (f32[128,512]{1,0:T(8,128)S(1)}, f32[128,512]{1,0:T(8,128)}, u32[]{:S(2)}) copy-start(f32[128,512]{1,0:T(8,128)} %copy-done.1) | copy-start | bytes 786436
  179.8 8.7 %collective-permute-start.11 = (bf16[4,136,512]{2,1,0:T(8,128)(2,1)S(1)}, bf16[4,136,512]{2,1,0:T(8,128)(2,1)S(1)}, u32[]{:S(2)}, u32[]{:S(2)}) collective-permute-start(bf16[4,136,512]{2,1,0:T(8,128)(2,1)S(1)} %bitcast.40), channel_id=1, source_target_pairs={{0,64},{64,0},{1,65},{65,1},{2,66},{66,2},{3,67},{67,3},{4,68},{68... | collective-permute-start | bytes 1671176 | tf_op jit(solution)/shard_map/ppermute | solution.py:52
  188.6 1.8 copy-start.8
  188.6 1.8 copy-start.10
  188.6 1.9 copy-start.11
  (5 other events, 6.8 us)

commit v8 on v7

--- a/solution.py
+++ b/solution.py
@@ -115,7 +115,7 @@
             jax.ShapeDtypeStruct((tokens, latents), F32),
         ],
         scratch_shapes=[pltpu.VMEM((wide, latents), BF), pltpu.SemaphoreType.DMA((PARTS,))],
-        compiler_params=params(50),
+        compiler_params=params(52),
         cost_estimate=pl.CostEstimate(
             flops=2 * tokens * latents * wide,
             bytes_accessed=2 * wide * (latents + tokens),
@@ -195,7 +195,7 @@
         out_specs=whole(),
         out_shape=jax.ShapeDtypeStruct((tokens + 8, latents), BF),
         scratch_shapes=[pltpu.VMEM((wide, latents), BF), pltpu.SemaphoreType.DMA((PARTS,))],
-        compiler_params=params(50),
+        compiler_params=params(52),
         cost_estimate=pl.CostEstimate(
             flops=2 * tokens * latents * wide,
             bytes_accessed=2 * wide * (latents + tokens),
@@ -235,7 +235,6 @@
     column = jnp.where(core == 0, column, column[::-1])
     column = column.transpose(2, 1, 3, 0, 4)
     column = column.reshape(CHIPS, small, 2 * chans)
-    column, dec_first = lax.optimization_barrier((column, dec_first))
     dec_second = shifted(dec_first, 1)
     gathered = spread(column, PLANE, BLOCKS).transpose(1, 0, 2, 3)
     gathered = gathered.reshape(CHIPS * tokens, 2 * chans)
@@ -287,6 +286,7 @@
     got = lax.all_to_all(
         partial_value.reshape(BLOCKS, small, wide), PLANE, 0, 0, tiled=True
     )
+    got, *mine = lax.optimization_barrier((got, *mine))
     summed = jnp.sum(got.astype(F32), axis=0).astype(BF)
     again = spread(jnp.concatenate([summed, sparse.astype(BF)], axis=1), "zh", HIGH)
     again, acts_there = lax.optimization_barrier((again, acts_there))

time: 195 us -> 192 us (0.985)
  waiting for transfers between devices: 43.6 us -> 49.8 us
  local copies, waits for them, and re-layouts: 11 us -> 7.06 us
  blocking collectives: 30.9 us -> 28.7 us
    ppermute x6, waiting for transfers between devices: 10.8 us -> 22.9 us  [shifted(): lax.ppermute(value, 'zl', [(i, (i + away) % CHIPS) for i in range(CHIPS)])]
    all_to_all x1, waiting for transfers between devices: 13.4 us -> 1.84 us  [body(): lax.all_to_all(partial_value.reshape(BLOCKS, small, wide), PLANE, 0, 0, t...]
    all_to_all x2, starting transfers between devices: 15.6 us -> 11.3 us  [spread(): return lax.all_to_all(copies, axes, 0, 0, tiled=True)]
    all_to_all x1, waiting for transfers between devices: 4.79 us -> 8.64 us  [body(): column = lax.all_to_all(halves, ('core', 'zh'), 0, 0, tiled=True)]
    all_to_all x1, blocking collectives: 18.3 us -> 14.9 us  [body(): grads = lax.all_to_all(copies, PLANE, 0, 0, tiled=True)]
    ppermute x6, starting transfers between devices: 22.2 us -> 25.1 us  [swap(): return lax.ppermute(value, 'core', [(0, 1), (1, 0)])]
    slice x1, local copies, waits for them, and re-layouts: 2.42 us -> 0.28 us  [body(): acts_here = gathered[:, :chans]]
    ppermute x6, starting transfers between devices: 16.9 us -> 18.9 us  [shifted(): lax.ppermute(value, 'zl', [(i, (i + away) % CHIPS) for i in range(CHIPS)])]
  transfers between devices with their start and end apart: 17 -> 17, of which waited for: 8 -> 11; matrix products, arithmetic and copies ran while one was open for 8% -> 6% of each run, Pallas kernels for 0% -> 0%
where the time goes in v8:
time: 192 us; the launch traced here: 190 us
  starting transfers between devices  82.9 us (43%)
  waiting for transfers between devices  49.8 us (26%)
  blocking collectives  28.7 us (15%)
  Pallas kernels  9.08 us (5%)
  other arithmetic  7.24 us (4%)
  local copies, waits for them, and re-layouts  7.06 us (4%)
  matrix products  4.59 us (2%)
    ppermute x6, starting transfers between devices, swap(): return lax.ppermute(value, 'core', [(0, 1), (1, 0)])  25.1 us
    ppermute x6, waiting for transfers between devices, shifted(): lax.ppermute(value, 'zl', [(i, (i + away) % CHIPS) for i in range(CHIPS)])  22.9 us
    ppermute x6, starting transfers between devices, shifted(): lax.ppermute(value, 'zl', [(i, (i + away) % CHIPS) for i in range(CHIPS)])  18.9 us
    all_to_all x1, starting transfers between devices, body(): column = lax.all_to_all(halves, ('core', 'zh'), 0, 0, tiled=True)  16.6 us
    all_to_all x1, blocking collectives, body(): grads = lax.all_to_all(copies, PLANE, 0, 0, tiled=True)  14.9 us
    all_gather x1, blocking collectives, body(): pre_here = lax.all_gather(last, 'zl', axis=0)  13.8 us
    all_to_all x2, starting transfers between devices, spread(): return lax.all_to_all(copies, axes, 0, 0, tiled=True)  11.3 us
    all_to_all x2, waiting for transfers between devices, spread(): return lax.all_to_all(copies, axes, 0, 0, tiled=True)  9.05 us
  transfers between devices with their start and end apart: 17, of which 11 were waited for; matrix products, arithmetic and copies ran while one was open for 6% of the time, Pallas kernels for 0%

profile of v8, /device:TPU:1, one launch (start us, length us, event | category | flops | bytes accessed | tf_op | source)
XLA Modules:
  0.0 190.4 jit_solution(9392792661016534478)
XLA Ops:
  2.0 16.6 %all-to-all-start = ((bf16[8,8,448]{2,1,0:T(8,128)(2,1)}), bf16[8,8,448]{2,1,0:T(8,128)(2,1)S(1)}, u32[]{:S(2)}, u32[]{:S(2)}) async-start(bf16[8,8,448]{2,1,0:T(8,128)(2,1)} %bitcast.1), calls=%async_computation | async-start | bytes 131072 | tf_op jit(solution)/shard_map/all_to_all | solution.py:233
  22.6 8.6 %all-to-all-done = bf16[8,8,448]{2,1,0:T(8,128)(2,1)S(1)} async-done(((bf16[8,8,448]{2,1,0:T(8,128)(2,1)}), bf16[8,8,448]{2,1,0:T(8,128)(2,1)S(1)}, u32[]{:S(2)}, u32[]{:S(2)}) %all-to-all-start) | async-done | bytes 57376 | tf_op jit(solution)/shard_map/all_to_all | solution.py:233
  32.5 6.9 %all-to-all-start.1 = ((bf16[16,4,8,896]{3,2,1,0:T(8,128)(2,1)}), bf16[16,4,8,896]{3,2,1,0:T(8,128)(2,1)}, u32[]{:S(2)}, u32[]{:S(2)}) async-start(bf16[16,4,8,896]{3,2,1,0:T(8,128)(2,1)} %broadcast_in_dim.42), calls=%async_computation.1 | async-start | bytes 1835008 | tf_op jit(solution)/shard_map/all_to_all | solution.py:48
  39.4 4.0 %collective-permute-start.1 = (bf16[448,512]{1,0:T(8,128)(2,1)S(1)}, bf16[448,512]{1,0:T(8,128)(2,1)S(1)}, u32[]{:S(2)}, u32[]{:S(2)}) collective-permute-start(bf16[448,512]{1,0:T(8,128)(2,1)S(1)} %bitcast.30), channel_id=1, source_target_pairs={{0,128},{128,256},{256,384},{384,0},{1,129},{129,257},{257,385},{3... | collective-permute-start | bytes 1376264 | tf_op jit(solution)/shard_map/ppermute | solution.py:221
  43.4 3.1 %collective-permute-start.3 = (bf16[448,512]{1,0:T(8,128)(2,1)S(1)}, bf16[448,512]{1,0:T(8,128)(2,1)S(1)}, u32[]{:S(2)}, u32[]{:S(2)}) collective-permute-start(bf16[448,512]{1,0:T(8,128)(2,1)S(1)} %bitcast.31), channel_id=1, source_target_pairs={{0,384},{128,0},{256,128},{384,256},{1,385},{129,1},{257,129},{385... | collective-permute-start | bytes 1376264 | tf_op jit(solution)/shard_map/ppermute | solution.py:221
  46.5 8.0 %collective-permute-done.1.refs_2_ = bf16[448,512]{1,0:T(8,128)(2,1)S(1)} collective-permute-done((bf16[448,512]{1,0:T(8,128)(2,1)S(1)}, bf16[448,512]{1,0:T(8,128)(2,1)S(1)}, u32[]{:S(2)}, u32[]{:S(2)}) %collective-permute-start.1) | collective-permute-done | bytes 458784 | tf_op jit(solution)/shard_map/ppermute | solution.py:221
  54.5 2.8 %collective-permute-start.2 = (bf16[448,512]{1,0:T(8,128)(2,1)S(1)}, bf16[448,512]{1,0:T(8,128)(2,1)}, u32[]{:S(2)}, u32[]{:S(2)}) collective-permute-start(bf16[448,512]{1,0:T(8,128)(2,1)S(1)} %collective-permute-done.1.refs_2_), channel_id=1, source_target_pairs={{0,128},{128,256},{256,384},{384,0},{1,129},{129,257},{257,385},{3... | collective-permute-start | bytes 1376264 | tf_op jit(solution)/shard_map/ppermute | solution.py:221
  61.1 5.3 %collective-permute-done.3.refs_6_ = bf16[448,512]{1,0:T(8,128)(2,1)S(1)} collective-permute-done((bf16[448,512]{1,0:T(8,128)(2,1)S(1)}, bf16[448,512]{1,0:T(8,128)(2,1)S(1)}, u32[]{:S(2)}, u32[]{:S(2)}) %collective-permute-start.3) | collective-permute-done | bytes 458784 | tf_op jit(solution)/shard_map/ppermute | solution.py:221
  66.4 7.9 %collective-permute-done.2.refs_4_ = bf16[448,512]{1,0:T(8,128)(2,1)} collective-permute-done((bf16[448,512]{1,0:T(8,128)(2,1)S(1)}, bf16[448,512]{1,0:T(8,128)(2,1)}, u32[]{:S(2)}, u32[]{:S(2)}) %collective-permute-start.2) | collective-permute-done | bytes 458784 | tf_op jit(solution)/shard_map/ppermute | solution.py:221
  74.3 4.3 %all-to-all-start.2 = ((bf16[4,128,512]{2,1,0:T(8,128)(2,1)}), bf16[4,128,512]{2,1,0:T(8,128)(2,1)}, u32[]{:S(2)}, u32[]{:S(2)}) async-start(bf16[4,128,512]{2,1,0:T(8,128)(2,1)} %bitcast.43), calls=%async_computation.2 | async-start | bytes 1048576 | tf_op jit(solution)/shard_map/all_to_all | solution.py:250
  78.6 3.3 %collective-permute-start.4 = (bf16[448,512]{1,0:T(8,128)(2,1)S(1)}, bf16[448,512]{1,0:T(8,128)(2,1)S(1)}, u32[]{:S(2)}, u32[]{:S(2)}) collective-permute-start(bf16[448,512]{1,0:T(8,128)(2,1)S(1)} %collective-permute-done.1.refs_2_), channel_id=1, source_target_pairs={{0,64},{64,0},{1,65},{65,1},{2,66},{66,2},{3,67},{67,3},{4,68},{68... | collective-permute-start | bytes 1376264 | tf_op jit(solution)/shard_map/ppermute | solution.py:52
  88.6 4.1 %all-to-all-done.2.quarter_ref = bf16[4,128,512]{2,1,0:T(8,128)(2,1)} async-done(((bf16[4,128,512]{2,1,0:T(8,128)(2,1)}), bf16[4,128,512]{2,1,0:T(8,128)(2,1)}, u32[]{:S(2)}, u32[]{:S(2)}) %all-to-all-start.2) | async-done | bytes 524320 | tf_op jit(solution)/shard_map/all_to_all | solution.py:250
  92.7 5.1 %decode.1 = (bf16[128,3584]{1,0:T(8,128)(2,1)}, bf16[128,512]{1,0:T(8,128)(2,1)S(1)}, f32[128,512]{1,0:T(8,128)S(1)}) custom-call(bf16[4,128,512]{2,1,0:T(8,128)(2,1)} %all-to-all-done.2.quarter_ref, f32[1,512]{1,0:T(1,128)S(1)} %bitcast.35, bf16[448,512]{1,0:T(8,128)(2,1)S(1)} %bitcast.32, bf16[912,512]{1,0:T(8,128)(2,1)} %copy-done.2, ...), custom_call_target="tpu_custom_call" | custom-call | flops 469762048 | bytes 4587520 | tf_op jit(solution)/shard_map/decode/pallas_call | solution.py:108
  97.9 6.6 %all-to-all-start.3 = ((bf16[16,8,3584]{2,1,0:T(8,128)(2,1)}), bf16[16,8,3584]{2,1,0:T(8,128)(2,1)}, u32[]{:S(2)}, u32[]{:S(2)}) async-start(bf16[16,8,3584]{2,1,0:T(8,128)(2,1)} %bitcast.39), calls=%async_computation.3 | async-start | bytes 1835008 | tf_op jit(solution)/shard_map/all_to_all | solution.py:286
  107.7 2.7 %collective-permute-start.8 = (bf16[1,24,512]{2,1,0:T(8,128)(2,1)S(1)}, bf16[1,24,512]{2,1,0:T(8,128)(2,1)S(1)}, u32[]{:S(2)}, u32[]{:S(2)}) collective-permute-start(bf16[1,24,512]{2,1,0:T(8,128)(2,1)S(1)} %get-tuple-element.40), channel_id=1, source_target_pairs={{0,256},{128,384},{256,0},{384,128},{1,257},{129,385},{257,1},{385... | collective-permute-start | bytes 73736 | tf_op jit(solution)/shard_map/ppermute | solution.py:221
  110.4 4.4 %collective-permute-start.9 = (bf16[1,24,512]{2,1,0:T(8,128)(2,1)S(1)}, bf16[1,24,512]{2,1,0:T(8,128)(2,1)S(1)}, u32[]{:S(2)}, u32[]{:S(2)}) collective-permute-start(bf16[1,24,512]{2,1,0:T(8,128)(2,1)S(1)} %get-tuple-element.39), channel_id=1, source_target_pairs={{0,384},{128,0},{256,128},{384,256},{1,385},{129,1},{257,129},{385... | collective-permute-start | bytes 73736 | tf_op jit(solution)/shard_map/ppermute | solution.py:221
  120.5 4.4 %all-to-all-start.4 = ((bf16[4,8,3712]{2,1,0:T(8,128)(2,1)}), bf16[4,8,3712]{2,1,0:T(8,128)(2,1)S(1)}, u32[]{:S(2)}, u32[]{:S(2)}) async-start(bf16[4,8,3712]{2,1,0:T(8,128)(2,1)} %broadcast_in_dim.45), calls=%async_computation.4 | async-start | bytes 475136 | tf_op jit(solution)/shard_map/all_to_all | solution.py:48
  125.2 5.0 %collective-permute-start.10 = (bf16[512,448]{1,0:T(8,128)(2,1)S(1)}, bf16[512,448]{1,0:T(8,128)(2,1)S(1)}, u32[]{:S(2)}, u32[]{:S(2)}) collective-permute-start(bf16[512,448]{1,0:T(8,128)(2,1)S(1)} %get-tuple-element.38), channel_id=1, source_target_pairs={{0,64},{64,0},{1,65},{65,1},{2,66},{66,2},{3,67},{67,3},{4,68},{68... | collective-permute-start | bytes 1376264 | tf_op jit(solution)/shard_map/ppermute | solution.py:52
  131.7 9.0 %all-to-all-done.4.got_ref = bf16[4,8,3712]{2,1,0:T(8,128)(2,1)S(1)} async-done(((bf16[4,8,3712]{2,1,0:T(8,128)(2,1)}), bf16[4,8,3712]{2,1,0:T(8,128)(2,1)S(1)}, u32[]{:S(2)}, u32[]{:S(2)}) %all-to-all-start.4) | async-done | bytes 237600 | tf_op jit(solution)/shard_map/all_to_all | solution.py:48
  140.9 14.9 %all_to_all.30 = bf16[16,8,3712]{2,1,0:T(8,128)(2,1)} all-to-all(bf16[16,8,3712]{2,1,0:T(8,128)(2,1)S(1)} %error.1), channel_id=1, replica_groups=mesh['zl'=4,'core'=2,'y'=4,'x'=4,'zh'=4] {'y','x'}, dimensions={0} | all-to-all | bytes 1900544 | tf_op jit(solution)/shard_map/all_to_all | solution.py:294
  155.8 3.8 %back.1 = bf16[136,512]{1,0:T(8,128)(2,1)S(1)} custom-call(bf16[128,3712]{1,0:T(8,128)(2,1)} %bitcast.38, f32[128,512]{1,0:T(8,128)S(1)} %get-tuple-element.32.slopes_ref, f32[1,512]{1,0:T(1,128)S(1)} %bitcast.34, bf16[448,512]{1,0:T(8,128)(2,1)S(1)} %bitcast.33, bf16[912,512]{1,0:T(8,128)(2,1)} %copy-done.2, ...), custom_call_target="tpu_custom_call" | custom-call | flops 469762048 | bytes 4587520 | tf_op jit(solution)/shard_map/back/pallas_call | solution.py:192
  159.6 13.8 %all-gather = bf16[544,512]{1,0:T(8,128)(2,1)S(1)} all-gather(bf16[136,512]{1,0:T(8,128)(2,1)S(1)} %back.1), channel_id=2, replica_groups=mesh['zl'=4,'core'=2,'y'=4,'x'=4,'zh'=4] {'zl'}, dimensions={0}, use_global_device_ids=true | all-gather | bytes 696320 | tf_op jit(solution)/shard_map/all_gather | solution.py:296
  173.5 10.6 %collective-permute-start.11 = (bf16[4,136,512]{2,1,0:T(8,128)(2,1)S(1)}, bf16[4,136,512]{2,1,0:T(8,128)(2,1)S(1)}, u32[]{:S(2)}, u32[]{:S(2)}) collective-permute-start(bf16[4,136,512]{2,1,0:T(8,128)(2,1)S(1)} %bitcast.40), channel_id=1, source_target_pairs={{0,64},{64,0},{1,65},{65,1},{2,66},{66,2},{3,67},{67,3},{4,68},{68... | collective-permute-start | bytes 1671176 | tf_op jit(solution)/shard_map/ppermute | solution.py:52
  187.3 2.5 %subtract_convert_fusion = (bf16[448,512]{1,0:T(8,128)(2,1)}, f32[448,512]{1,0:T(8,128)}, f32[448,512]{1,0:T(8,128)}) fusion(bf16[448,512]{1,0:T(8,128)(2,1)S(1)} %copy-done.8, f32[448,512]{1,0:T(8,128)S(1)} %copy-done.10, f32[448,512]{1,0:T(8,128)S(1)} %copy-done.11, f32[448,512]{1,0:T(8,128)S(1)} %convolution_bitcast_fusion, ...), kind=kOutput, calls=%fused_computation.10 | convolution fusion | flops 253231104 | bytes 6520832 | tf_op jit(solution)/shard_map/dot_general | solution.py:301
  (84 shorter events, 31.4 us)
Async XLA Ops:
  2.0 29.2 %all-to-all-start = ((bf16[8,8,448]{2,1,0:T(8,128)(2,1)}), bf16[8,8,448]{2,1,0:T(8,128)(2,1)S(1)}, u32[]{:S(2)}, u32[]{:S(2)}) async-start(bf16[8,8,448]{2,1,0:T(8,128)(2,1)} %bitcast.1), calls=%async_computation | async-start | bytes 131072 | tf_op jit(solution)/shard_map/all_to_all | solution.py:233
  20.6 36.7 %collective-permute-start = (bf16[912,512]{1,0:T(8,128)(2,1)S(1)}, bf16[912,512]{1,0:T(8,128)(2,1)S(1)}, u32[]{:S(2)}, u32[]{:S(2)}) collective-permute-start(bf16[912,512]{1,0:T(8,128)(2,1)S(1)} %pad_maximum_fusion), channel_id=1, source_target_pairs={{0,64},{64,0},{1,65},{65,1},{2,66},{66,2},{3,67},{67,3},{4,68},{68... | collective-permute-start | bytes 2801672 | tf_op jit(solution)/shard_map/ppermute | solution.py:52
  32.5 6.9 %copy-start = (bf16[512,448]{0,1:T(8,128)(2,1)S(1)}, bf16[512,448]{0,1:T(8,128)(2,1)}, u32[]{:S(2)}) copy-start(bf16[512,448]{0,1:T(8,128)(2,1)} %param.10) | copy-start | bytes 1376260
  32.5 25.7 %all-to-all-start.1 = ((bf16[16,4,8,896]{3,2,1,0:T(8,128)(2,1)}), bf16[16,4,8,896]{3,2,1,0:T(8,128)(2,1)}, u32[]{:S(2)}, u32[]{:S(2)}) async-start(bf16[16,4,8,896]{3,2,1,0:T(8,128)(2,1)} %broadcast_in_dim.42), calls=%async_computation.1 | async-start | bytes 1835008 | tf_op jit(solution)/shard_map/all_to_all | solution.py:48
  39.4 15.1 %collective-permute-start.1 = (bf16[448,512]{1,0:T(8,128)(2,1)S(1)}, bf16[448,512]{1,0:T(8,128)(2,1)S(1)}, u32[]{:S(2)}, u32[]{:S(2)}) collective-permute-start(bf16[448,512]{1,0:T(8,128)(2,1)S(1)} %bitcast.30), channel_id=1, source_target_pairs={{0,128},{128,256},{256,384},{384,0},{1,129},{129,257},{257,385},{3... | collective-permute-start | bytes 1376264 | tf_op jit(solution)/shard_map/ppermute | solution.py:221
  43.4 23.1 %collective-permute-start.3 = (bf16[448,512]{1,0:T(8,128)(2,1)S(1)}, bf16[448,512]{1,0:T(8,128)(2,1)S(1)}, u32[]{:S(2)}, u32[]{:S(2)}) collective-permute-start(bf16[448,512]{1,0:T(8,128)(2,1)S(1)} %bitcast.31), channel_id=1, source_target_pairs={{0,384},{128,0},{256,128},{384,256},{1,385},{129,1},{257,129},{385... | collective-permute-start | bytes 1376264 | tf_op jit(solution)/shard_map/ppermute | solution.py:221
  54.5 19.8 %collective-permute-start.2 = (bf16[448,512]{1,0:T(8,128)(2,1)S(1)}, bf16[448,512]{1,0:T(8,128)(2,1)}, u32[]{:S(2)}, u32[]{:S(2)}) collective-permute-start(bf16[448,512]{1,0:T(8,128)(2,1)S(1)} %collective-permute-done.1.refs_2_), channel_id=1, source_target_pairs={{0,128},{128,256},{256,384},{384,0},{1,129},{129,257},{257,385},{3... | collective-permute-start | bytes 1376264 | tf_op jit(solution)/shard_map/ppermute | solution.py:221
  57.3 29.6 %copy-start.2 = (bf16[912,512]{1,0:T(8,128)(2,1)}, bf16[912,512]{1,0:T(8,128)(2,1)S(1)}, u32[]{:S(2)}) copy-start(bf16[912,512]{1,0:T(8,128)(2,1)S(1)} %collective-permute-done.refs_1_) | copy-start | bytes 2801668
  66.4 20.6 %copy-start.5 = (bf16[448,512]{1,0:T(8,128)(2,1)}, bf16[448,512]{1,0:T(8,128)(2,1)S(1)}, u32[]{:S(2)}) copy-start(bf16[448,512]{1,0:T(8,128)(2,1)S(1)} %collective-permute-done.3.refs_6_) | copy-start | bytes 1376260
  74.3 18.4 %all-to-all-start.2 = ((bf16[4,128,512]{2,1,0:T(8,128)(2,1)}), bf16[4,128,512]{2,1,0:T(8,128)(2,1)}, u32[]{:S(2)}, u32[]{:S(2)}) async-start(bf16[4,128,512]{2,1,0:T(8,128)(2,1)} %bitcast.43), calls=%async_computation.2 | async-start | bytes 1048576 | tf_op jit(solution)/shard_map/all_to_all | solution.py:250
  78.6 5.6 %collective-permute-start.4 = (bf16[448,512]{1,0:T(8,128)(2,1)S(1)}, bf16[448,512]{1,0:T(8,128)(2,1)S(1)}, u32[]{:S(2)}, u32[]{:S(2)}) collective-permute-start(bf16[448,512]{1,0:T(8,128)(2,1)S(1)} %collective-permute-done.1.refs_2_), channel_id=1, source_target_pairs={{0,64},{64,0},{1,65},{65,1},{2,66},{66,2},{3,67},{67,3},{4,68},{68... | collective-permute-start | bytes 1376264 | tf_op jit(solution)/shard_map/ppermute | solution.py:52
  82.3 6.0 %collective-permute-start.6 = (bf16[448,512]{1,0:T(8,128)(2,1)S(1)}, bf16[448,512]{1,0:T(8,128)(2,1)S(1)}, u32[]{:S(2)}, u32[]{:S(2)}) collective-permute-start(bf16[448,512]{1,0:T(8,128)(2,1)S(1)} %collective-permute-done.3.refs_6_), channel_id=1, source_target_pairs={{0,64},{64,0},{1,65},{65,1},{2,66},{66,2},{3,67},{67,3},{4,68},{68... | collective-permute-start | bytes 1376264 | tf_op jit(solution)/shard_map/ppermute | solution.py:52
  84.3 8.4 %copy-start.1 = (f32[512]{0:T(512)S(1)}, f32[512]{0:T(512)}, u32[]{:S(2)}) copy-start(f32[512]{0:T(512)} %param.9) | copy-start | bytes 6148
  84.4 4.2 %collective-permute-start.5 = (bf16[448,512]{1,0:T(8,128)(2,1)}, bf16[448,512]{1,0:T(8,128)(2,1)}, u32[]{:S(2)}, u32[]{:S(2)}) collective-permute-start(bf16[448,512]{1,0:T(8,128)(2,1)} %collective-permute-done.2.refs_4_), channel_id=1, source_target_pairs={{0,64},{64,0},{1,65},{65,1},{2,66},{66,2},{3,67},{67,3},{4,68},{68... | collective-permute-start | bytes 1376264 | tf_op jit(solution)/shard_map/ppermute | solution.py:52
  88.3 4.4 %copy-start.6 = (bf16[448,512]{1,0:T(8,128)(2,1)}, bf16[448,512]{1,0:T(8,128)(2,1)S(1)}, u32[]{:S(2)}) copy-start(bf16[448,512]{1,0:T(8,128)(2,1)S(1)} %collective-permute-done.6.refs_7_) | copy-start | bytes 1376260
  97.9 20.6 %all-to-all-start.3 = ((bf16[16,8,3584]{2,1,0:T(8,128)(2,1)}), bf16[16,8,3584]{2,1,0:T(8,128)(2,1)}, u32[]{:S(2)}, u32[]{:S(2)}) async-start(bf16[16,8,3584]{2,1,0:T(8,128)(2,1)} %bitcast.39), calls=%async_computation.3 | async-start | bytes 1835008 | tf_op jit(solution)/shard_map/all_to_all | solution.py:286
  105.7 9.2 %collective-permute-start.7 = (bf16[1,24,512]{2,1,0:T(8,128)(2,1)S(1)}, bf16[1,24,512]{2,1,0:T(8,128)(2,1)S(1)}, u32[]{:S(2)}, u32[]{:S(2)}) collective-permute-start(bf16[1,24,512]{2,1,0:T(8,128)(2,1)S(1)} %get-tuple-element.41), channel_id=1, source_target_pairs={{0,128},{128,256},{256,384},{384,0},{1,129},{129,257},{257,385},{3... | collective-permute-start | bytes 73736 | tf_op jit(solution)/shard_map/ppermute | solution.py:221
  107.7 7.2 %collective-permute-start.8 = (bf16[1,24,512]{2,1,0:T(8,128)(2,1)S(1)}, bf16[1,24,512]{2,1,0:T(8,128)(2,1)S(1)}, u32[]{:S(2)}, u32[]{:S(2)}) collective-permute-start(bf16[1,24,512]{2,1,0:T(8,128)(2,1)S(1)} %get-tuple-element.40), channel_id=1, source_target_pairs={{0,256},{128,384},{256,0},{384,128},{1,257},{129,385},{257,1},{385... | collective-permute-start | bytes 73736 | tf_op jit(solution)/shard_map/ppermute | solution.py:221
  110.4 6.3 %collective-permute-start.9 = (bf16[1,24,512]{2,1,0:T(8,128)(2,1)S(1)}, bf16[1,24,512]{2,1,0:T(8,128)(2,1)S(1)}, u32[]{:S(2)}, u32[]{:S(2)}) collective-permute-start(bf16[1,24,512]{2,1,0:T(8,128)(2,1)S(1)} %get-tuple-element.39), channel_id=1, source_target_pairs={{0,384},{128,0},{256,128},{384,256},{1,385},{129,1},{257,129},{385... | collective-permute-start | bytes 73736 | tf_op jit(solution)/shard_map/ppermute | solution.py:221
  114.8 10.1 %copy-start.4 = (bf16[16,4,8,896]{3,2,0,1:T(8,128)(2,1)S(1)}, bf16[16,4,8,896]{3,2,0,1:T(8,128)(2,1)}, u32[]{:S(2)}) copy-start(bf16[16,4,8,896]{3,2,0,1:T(8,128)(2,1)} %copy-done.3) | copy-start | bytes 2752516
  120.5 20.2 %all-to-all-start.4 = ((bf16[4,8,3712]{2,1,0:T(8,128)(2,1)}), bf16[4,8,3712]{2,1,0:T(8,128)(2,1)S(1)}, u32[]{:S(2)}, u32[]{:S(2)}) async-start(bf16[4,8,3712]{2,1,0:T(8,128)(2,1)} %broadcast_in_dim.45), calls=%async_computation.4 | async-start | bytes 475136 | tf_op jit(solution)/shard_map/all_to_all | solution.py:48
  125.2 6.5 %collective-permute-start.10 = (bf16[512,448]{1,0:T(8,128)(2,1)S(1)}, bf16[512,448]{1,0:T(8,128)(2,1)S(1)}, u32[]{:S(2)}, u32[]{:S(2)}) collective-permute-start(bf16[512,448]{1,0:T(8,128)(2,1)S(1)} %get-tuple-element.38), channel_id=1, source_target_pairs={{0,64},{64,0},{1,65},{65,1},{2,66},{66,2},{3,67},{67,3},{4,68},{68... | collective-permute-start | bytes 1376264 | tf_op jit(solution)/shard_map/ppermute | solution.py:52
  173.5 12.2 %collective-permute-start.11 = (bf16[4,136,512]{2,1,0:T(8,128)(2,1)S(1)}, bf16[4,136,512]{2,1,0:T(8,128)(2,1)S(1)}, u32[]{:S(2)}, u32[]{:S(2)}) collective-permute-start(bf16[4,136,512]{2,1,0:T(8,128)(2,1)S(1)} %bitcast.40), channel_id=1, source_target_pairs={{0,64},{64,0},{1,65},{65,1},{2,66},{66,2},{3,67},{67,3},{4,68},{68... | collective-permute-start | bytes 1671176 | tf_op jit(solution)/shard_map/ppermute | solution.py:52
  185.7 1.6 copy-start.11
  (5 other events, 6.7 us)

commit v9 on v8

--- a/solution.py
+++ b/solution.py
@@ -115,7 +115,7 @@
             jax.ShapeDtypeStruct((tokens, latents), F32),
         ],
         scratch_shapes=[pltpu.VMEM((wide, latents), BF), pltpu.SemaphoreType.DMA((PARTS,))],
-        compiler_params=params(52),
+        compiler_params=params(56),
         cost_estimate=pl.CostEstimate(
             flops=2 * tokens * latents * wide,
             bytes_accessed=2 * wide * (latents + tokens),
@@ -195,7 +195,7 @@
         out_specs=whole(),
         out_shape=jax.ShapeDtypeStruct((tokens + 8, latents), BF),
         scratch_shapes=[pltpu.VMEM((wide, latents), BF), pltpu.SemaphoreType.DMA((PARTS,))],
-        compiler_params=params(52),
+        compiler_params=params(56),
         cost_estimate=pl.CostEstimate(
             flops=2 * tokens * latents * wide,
             bytes_accessed=2 * wide * (latents + tokens),
@@ -221,7 +221,7 @@
         return lax.ppermute(value, "zl", [(i, (i + away) % CHIPS) for i in range(CHIPS)])
 
     dec_own = dec_weight.T
-    dec_first, dec_last = shifted(dec_own, 1), shifted(dec_own, CHIPS - 1)
+    dec_first = shifted(dec_own, 1)
     bias_here = jnp.stack(pieces(dec_bias, 3))
     bias_block = jnp.pad(bias_here, ((0, 13), (0, latents - chans)))
     swapped = swap(jnp.concatenate([enc_weight, dec_own, bias_block], axis=0))
@@ -236,6 +236,7 @@
     column = column.transpose(2, 1, 3, 0, 4)
     column = column.reshape(CHIPS, small, 2 * chans)
     dec_second = shifted(dec_first, 1)
+    dec_last = shifted(dec_second, 1)
     gathered = spread(column, PLANE, BLOCKS).transpose(1, 0, 2, 3)
     gathered = gathered.reshape(CHIPS * tokens, 2 * chans)
 

time: 192 us -> 188 us (0.979)
  waiting for transfers between devices: 49.8 us -> 37.2 us
  blocking collectives: 28.7 us -> 39.2 us
    all_gather x1, blocking collectives: 13.8 us -> 20.4 us  [body(): pre_here = lax.all_gather(last, 'zl', axis=0)]
    all_to_all x1, blocking collectives: 14.9 us -> 18.8 us  [body(): grads = lax.all_to_all(copies, PLANE, 0, 0, tiled=True)]
    all_to_all x2, waiting for transfers between devices: 9.05 us -> 5.38 us  [spread(): return lax.all_to_all(copies, axes, 0, 0, tiled=True)]
    all_to_all x1, waiting for transfers between devices: 4.11 us -> 1.15 us  [body(): lax.all_to_all(sums.reshape(CHIPS, tokens, latents), 'zl', 0, 0, tiled=True)]
    all_to_all x1, waiting for transfers between devices: 8.64 us -> 5.72 us  [body(): column = lax.all_to_all(halves, ('core', 'zh'), 0, 0, tiled=True)]
    ppermute x6, starting transfers between devices: 25.1 us -> 22.5 us  [swap(): return lax.ppermute(value, 'core', [(0, 1), (1, 0)])]
    all_to_all x2, starting transfers between devices: 11.3 us -> 13.3 us  [spread(): return lax.all_to_all(copies, axes, 0, 0, tiled=True)]
  transfers between devices with their start and end apart: 17 -> 17, of which waited for: 11 -> 9; matrix products, arithmetic and copies ran while one was open for 6% -> 5% of each run, Pallas kernels for 0% -> 0%
where the time goes in v9:
time: 188 us; the launch traced here: 187 us
  starting transfers between devices  82.6 us (44%)
  blocking collectives  39.2 us (21%)
  waiting for transfers between devices  37.2 us (20%)
  Pallas kernels  9.46 us (5%)
  local copies, waits for them, and re-layouts  6.32 us (3%)
  other arithmetic  6.2 us (3%)
  matrix products  4.59 us (2%)
    ppermute x6, starting transfers between devices, swap(): return lax.ppermute(value, 'core', [(0, 1), (1, 0)])  22.5 us
    ppermute x6, waiting for transfers between devices, shifted(): lax.ppermute(value, 'zl', [(i, (i + away) % CHIPS) for i in range(CHIPS)])  21.4 us
    all_gather x1, blocking collectives, body(): pre_here = lax.all_gather(last, 'zl', axis=0)  20.4 us
    ppermute x6, starting transfers between devices, shifted(): lax.ppermute(value, 'zl', [(i, (i + away) % CHIPS) for i in range(CHIPS)])  20 us
    all_to_all x1, blocking collectives, body(): grads = lax.all_to_all(copies, PLANE, 0, 0, tiled=True)  18.8 us
    all_to_all x1, starting transfers between devices, body(): column = lax.all_to_all(halves, ('core', 'zh'), 0, 0, tiled=True)  16.6 us
    all_to_all x2, starting transfers between devices, spread(): return lax.all_to_all(copies, axes, 0, 0, tiled=True)  13.3 us
    all_to_all x1, starting transfers between devices, body(): lax.all_to_all(partial_value.reshape(BLOCKS, small, wide), PLANE, 0, 0, t...  6.03 us
  transfers between devices with their start and end apart: 17, of which 9 were waited for; matrix products, arithmetic and copies ran while one was open for 5% of the time, Pallas kernels for 0%

profile of v9, /device:TPU:1, one launch (start us, length us, event | category | flops | bytes accessed | tf_op | source)
XLA Modules:
  0.0 186.7 jit_solution(15528173911220956042)
XLA Ops:
  2.0 16.6 %all-to-all-start = ((bf16[8,8,448]{2,1,0:T(8,128)(2,1)}), bf16[8,8,448]{2,1,0:T(8,128)(2,1)S(1)}, u32[]{:S(2)}, u32[]{:S(2)}) async-start(bf16[8,8,448]{2,1,0:T(8,128)(2,1)} %bitcast.1), calls=%async_computation | async-start | bytes 131072 | tf_op jit(solution)/shard_map/all_to_all | solution.py:233
  18.6 2.6 %collective-permute-start.1 = (bf16[448,512]{1,0:T(8,128)(2,1)}, bf16[448,512]{1,0:T(8,128)(2,1)S(1)}, u32[]{:S(2)}, u32[]{:S(2)}) collective-permute-start(bf16[448,512]{1,0:T(8,128)(2,1)} %bitcast.29), channel_id=1, source_target_pairs={{0,128},{128,256},{256,384},{384,0},{1,129},{129,257},{257,385},{3... | collective-permute-start | bytes 1376264 | tf_op jit(solution)/shard_map/ppermute | solution.py:221
  25.5 5.7 %all-to-all-done = bf16[8,8,448]{2,1,0:T(8,128)(2,1)S(1)} async-done(((bf16[8,8,448]{2,1,0:T(8,128)(2,1)}), bf16[8,8,448]{2,1,0:T(8,128)(2,1)S(1)}, u32[]{:S(2)}, u32[]{:S(2)}) %all-to-all-start) | async-done | bytes 57376 | tf_op jit(solution)/shard_map/all_to_all | solution.py:233
  32.5 6.8 %all-to-all-start.1 = ((bf16[16,4,8,896]{3,2,1,0:T(8,128)(2,1)}), bf16[16,4,8,896]{3,2,1,0:T(8,128)(2,1)}, u32[]{:S(2)}, u32[]{:S(2)}) async-start(bf16[16,4,8,896]{3,2,1,0:T(8,128)(2,1)} %broadcast_in_dim.42), calls=%async_computation.1 | async-start | bytes 1835008 | tf_op jit(solution)/shard_map/all_to_all | solution.py:48
  39.3 3.9 %collective-permute-start.2 = (bf16[448,512]{1,0:T(8,128)(2,1)S(1)}, bf16[448,512]{1,0:T(8,128)(2,1)}, u32[]{:S(2)}, u32[]{:S(2)}) collective-permute-start(bf16[448,512]{1,0:T(8,128)(2,1)S(1)} %collective-permute-done.1.refs_2_), channel_id=1, source_target_pairs={{0,128},{128,256},{256,384},{384,0},{1,129},{129,257},{257,385},{3... | collective-permute-start | bytes 1376264 | tf_op jit(solution)/shard_map/ppermute | solution.py:221
  43.2 11.2 %collective-permute-done.2.refs_4_ = bf16[448,512]{1,0:T(8,128)(2,1)} collective-permute-done((bf16[448,512]{1,0:T(8,128)(2,1)S(1)}, bf16[448,512]{1,0:T(8,128)(2,1)}, u32[]{:S(2)}, u32[]{:S(2)}) %collective-permute-start.2) | collective-permute-done | bytes 458784 | tf_op jit(solution)/shard_map/ppermute | solution.py:221
  54.5 2.7 %collective-permute-start.3 = (bf16[448,512]{1,0:T(8,128)(2,1)}, bf16[448,512]{1,0:T(8,128)(2,1)}, u32[]{:S(2)}, u32[]{:S(2)}) collective-permute-start(bf16[448,512]{1,0:T(8,128)(2,1)} %collective-permute-done.2.refs_4_), channel_id=1, source_target_pairs={{0,128},{128,256},{256,384},{384,0},{1,129},{129,257},{257,385},{3... | collective-permute-start | bytes 1376264 | tf_op jit(solution)/shard_map/ppermute | solution.py:221
  60.4 8.6 %collective-permute-done.3.refs_6_ = bf16[448,512]{1,0:T(8,128)(2,1)} collective-permute-done((bf16[448,512]{1,0:T(8,128)(2,1)}, bf16[448,512]{1,0:T(8,128)(2,1)}, u32[]{:S(2)}, u32[]{:S(2)}) %collective-permute-start.3) | collective-permute-done | bytes 458784 | tf_op jit(solution)/shard_map/ppermute | solution.py:221
  68.9 4.1 %all-to-all-start.2 = ((bf16[4,128,512]{2,1,0:T(8,128)(2,1)}), bf16[4,128,512]{2,1,0:T(8,128)(2,1)}, u32[]{:S(2)}, u32[]{:S(2)}) async-start(bf16[4,128,512]{2,1,0:T(8,128)(2,1)} %bitcast.8), calls=%async_computation.2 | async-start | bytes 1048576 | tf_op jit(solution)/shard_map/all_to_all | solution.py:251
  73.1 4.4 %collective-permute-start.4 = (bf16[448,512]{1,0:T(8,128)(2,1)S(1)}, bf16[448,512]{1,0:T(8,128)(2,1)}, u32[]{:S(2)}, u32[]{:S(2)}) collective-permute-start(bf16[448,512]{1,0:T(8,128)(2,1)S(1)} %collective-permute-done.1.refs_2_), channel_id=1, source_target_pairs={{0,64},{64,0},{1,65},{65,1},{2,66},{66,2},{3,67},{67,3},{4,68},{68... | collective-permute-start | bytes 1376264 | tf_op jit(solution)/shard_map/ppermute | solution.py:52
  81.0 2.4 %collective-permute-start.5 = (bf16[448,512]{1,0:T(8,128)(2,1)}, bf16[448,512]{1,0:T(8,128)(2,1)S(1)}, u32[]{:S(2)}, u32[]{:S(2)}) collective-permute-start(bf16[448,512]{1,0:T(8,128)(2,1)} %collective-permute-done.2.refs_4_), channel_id=1, source_target_pairs={{0,64},{64,0},{1,65},{65,1},{2,66},{66,2},{3,67},{67,3},{4,68},{68... | collective-permute-start | bytes 1376264 | tf_op jit(solution)/shard_map/ppermute | solution.py:52
  86.3 5.0 %decode.1 = (bf16[128,3584]{1,0:T(8,128)(2,1)}, bf16[128,512]{1,0:T(8,128)(2,1)}, f32[128,512]{1,0:T(8,128)}) custom-call(bf16[4,128,512]{2,1,0:T(8,128)(2,1)} %all-to-all-done.2.quarter_ref, f32[1,512]{1,0:T(1,128)} %bitcast.42, bf16[448,512]{1,0:T(8,128)(2,1)} %bitcast.31, bf16[912,512]{1,0:T(8,128)(2,1)} %copy-done, bf16[448,512]{1,0:T(8,128)(2,1)} %copy-done.2, ...), custom_call_target="tpu_custom_call" | custom-call | flops 469762048 | bytes 4587520 | tf_op jit(solution)/shard_map/decode/pallas_call | solution.py:108
  91.3 6.0 %all-to-all-start.3 = ((bf16[16,8,3584]{2,1,0:T(8,128)(2,1)}), bf16[16,8,3584]{2,1,0:T(8,128)(2,1)S(1)}, u32[]{:S(2)}, u32[]{:S(2)}) async-start(bf16[16,8,3584]{2,1,0:T(8,128)(2,1)} %bitcast.36), calls=%async_computation.3 | async-start | bytes 1835008 | tf_op jit(solution)/shard_map/all_to_all | solution.py:287
  97.6 3.6 %collective-permute-start.7 = (bf16[1,24,512]{2,1,0:T(8,128)(2,1)S(1)}, bf16[1,24,512]{2,1,0:T(8,128)(2,1)S(1)}, u32[]{:S(2)}, u32[]{:S(2)}) collective-permute-start(bf16[1,24,512]{2,1,0:T(8,128)(2,1)S(1)} %get-tuple-element.41), channel_id=1, source_target_pairs={{0,128},{128,256},{256,384},{384,0},{1,129},{129,257},{257,385},{3... | collective-permute-start | bytes 73736 | tf_op jit(solution)/shard_map/ppermute | solution.py:221
  101.2 4.0 %collective-permute-start.8 = (bf16[1,24,512]{2,1,0:T(8,128)(2,1)S(1)}, bf16[1,24,512]{2,1,0:T(8,128)(2,1)S(1)}, u32[]{:S(2)}, u32[]{:S(2)}) collective-permute-start(bf16[1,24,512]{2,1,0:T(8,128)(2,1)S(1)} %get-tuple-element.40), channel_id=1, source_target_pairs={{0,256},{128,384},{256,0},{384,128},{1,257},{129,385},{257,1},{385... | collective-permute-start | bytes 73736 | tf_op jit(solution)/shard_map/ppermute | solution.py:221
  105.2 3.1 %collective-permute-start.9 = (bf16[1,24,512]{2,1,0:T(8,128)(2,1)S(1)}, bf16[1,24,512]{2,1,0:T(8,128)(2,1)S(1)}, u32[]{:S(2)}, u32[]{:S(2)}) collective-permute-start(bf16[1,24,512]{2,1,0:T(8,128)(2,1)S(1)} %get-tuple-element.39), channel_id=1, source_target_pairs={{0,384},{128,0},{256,128},{384,256},{1,385},{129,1},{257,129},{385... | collective-permute-start | bytes 73736 | tf_op jit(solution)/shard_map/ppermute | solution.py:221
  111.5 6.5 %all-to-all-start.4 = ((bf16[4,8,3712]{2,1,0:T(8,128)(2,1)}), bf16[4,8,3712]{2,1,0:T(8,128)(2,1)S(1)}, u32[]{:S(2)}, u32[]{:S(2)}) async-start(bf16[4,8,3712]{2,1,0:T(8,128)(2,1)} %broadcast_in_dim.45), calls=%async_computation.4 | async-start | bytes 475136 | tf_op jit(solution)/shard_map/all_to_all | solution.py:48
  118.3 5.5 %collective-permute-start.10 = (bf16[512,448]{1,0:T(8,128)(2,1)S(1)}, bf16[512,448]{1,0:T(8,128)(2,1)S(1)}, u32[]{:S(2)}, u32[]{:S(2)}) collective-permute-start(bf16[512,448]{1,0:T(8,128)(2,1)S(1)} %get-tuple-element.38), channel_id=1, source_target_pairs={{0,64},{64,0},{1,65},{65,1},{2,66},{66,2},{3,67},{67,3},{4,68},{68... | collective-permute-start | bytes 1376264 | tf_op jit(solution)/shard_map/ppermute | solution.py:52
  125.3 5.4 %all-to-all-done.4.got_ref = bf16[4,8,3712]{2,1,0:T(8,128)(2,1)S(1)} async-done(((bf16[4,8,3712]{2,1,0:T(8,128)(2,1)}), bf16[4,8,3712]{2,1,0:T(8,128)(2,1)S(1)}, u32[]{:S(2)}, u32[]{:S(2)}) %all-to-all-start.4) | async-done | bytes 237600 | tf_op jit(solution)/shard_map/all_to_all | solution.py:48
  130.9 18.8 %all_to_all.30 = bf16[16,8,3712]{2,1,0:T(8,128)(2,1)} all-to-all(bf16[16,8,3712]{2,1,0:T(8,128)(2,1)S(1)} %error.1), channel_id=1, replica_groups=mesh['zl'=4,'core'=2,'y'=4,'x'=4,'zh'=4] {'y','x'}, dimensions={0} | all-to-all | bytes 1900544 | tf_op jit(solution)/shard_map/all_to_all | solution.py:295
  149.7 4.4 %back.1 = bf16[136,512]{1,0:T(8,128)(2,1)} custom-call(bf16[128,3712]{1,0:T(8,128)(2,1)} %bitcast.35, f32[128,512]{1,0:T(8,128)} %get-tuple-element.32.slopes_ref, f32[1,512]{1,0:T(1,128)} %bitcast.41, bf16[448,512]{1,0:T(8,128)(2,1)} %bitcast.32, bf16[912,512]{1,0:T(8,128)(2,1)} %copy-done, bf16[448,512]{1,0:T(8,128)(2,1)} %copy-done.2, ...), custom_call_target="tpu_custom_call" | custom-call | flops 469762048 | bytes 4587520 | tf_op jit(solution)/shard_map/back/pallas_call | solution.py:192
  154.1 20.4 %all-gather = bf16[544,512]{1,0:T(8,128)(2,1)S(1)} all-gather(bf16[136,512]{1,0:T(8,128)(2,1)} %back.1), channel_id=2, replica_groups=mesh['zl'=4,'core'=2,'y'=4,'x'=4,'zh'=4] {'zl'}, dimensions={0}, use_global_device_ids=true | all-gather | bytes 696320 | tf_op jit(solution)/shard_map/all_gather | solution.py:297
  174.5 6.1 %collective-permute-start.11 = (bf16[4,136,512]{2,1,0:T(8,128)(2,1)S(1)}, bf16[4,136,512]{2,1,0:T(8,128)(2,1)S(1)}, u32[]{:S(2)}, u32[]{:S(2)}) collective-permute-start(bf16[4,136,512]{2,1,0:T(8,128)(2,1)S(1)} %bitcast.37), channel_id=1, source_target_pairs={{0,64},{64,0},{1,65},{65,1},{2,66},{66,2},{3,67},{67,3},{4,68},{68... | collective-permute-start | bytes 1671176 | tf_op jit(solution)/shard_map/ppermute | solution.py:52
  183.6 2.5 %subtract_convert_fusion = (bf16[448,512]{1,0:T(8,128)(2,1)}, f32[448,512]{1,0:T(8,128)}, f32[448,512]{1,0:T(8,128)}) fusion(bf16[448,512]{1,0:T(8,128)(2,1)S(1)} %copy-done.6, f32[448,512]{1,0:T(8,128)S(1)} %copy-done.9, f32[448,512]{1,0:T(8,128)S(1)} %copy-done.10, f32[448,512]{1,0:T(8,128)S(1)} %convolution_bitcast_fusion, ...), kind=kOutput, calls=%fused_computation.10 | convolution fusion | flops 253231104 | bytes 6520832 | tf_op jit(solution)/shard_map/dot_general | solution.py:302
  (86 shorter events, 25.1 us)
Async XLA Ops:
  2.0 29.2 %all-to-all-start = ((bf16[8,8,448]{2,1,0:T(8,128)(2,1)}), bf16[8,8,448]{2,1,0:T(8,128)(2,1)S(1)}, u32[]{:S(2)}, u32[]{:S(2)}) async-start(bf16[8,8,448]{2,1,0:T(8,128)(2,1)} %bitcast.1), calls=%async_computation | async-start | bytes 131072 | tf_op jit(solution)/shard_map/all_to_all | solution.py:233
  18.6 20.7 %collective-permute-start.1 = (bf16[448,512]{1,0:T(8,128)(2,1)}, bf16[448,512]{1,0:T(8,128)(2,1)S(1)}, u32[]{:S(2)}, u32[]{:S(2)}) collective-permute-start(bf16[448,512]{1,0:T(8,128)(2,1)} %bitcast.29), channel_id=1, source_target_pairs={{0,128},{128,256},{256,384},{384,0},{1,129},{129,257},{257,385},{3... | collective-permute-start | bytes 1376264 | tf_op jit(solution)/shard_map/ppermute | solution.py:221
  23.3 33.9 %collective-permute-start = (bf16[912,512]{1,0:T(8,128)(2,1)S(1)}, bf16[912,512]{1,0:T(8,128)(2,1)S(1)}, u32[]{:S(2)}, u32[]{:S(2)}) collective-permute-start(bf16[912,512]{1,0:T(8,128)(2,1)S(1)} %pad_maximum_fusion), channel_id=1, source_target_pairs={{0,64},{64,0},{1,65},{65,1},{2,66},{66,2},{3,67},{67,3},{4,68},{68... | collective-permute-start | bytes 2801672 | tf_op jit(solution)/shard_map/ppermute | solution.py:52
  32.5 24.8 %all-to-all-start.1 = ((bf16[16,4,8,896]{3,2,1,0:T(8,128)(2,1)}), bf16[16,4,8,896]{3,2,1,0:T(8,128)(2,1)}, u32[]{:S(2)}, u32[]{:S(2)}) async-start(bf16[16,4,8,896]{3,2,1,0:T(8,128)(2,1)} %broadcast_in_dim.42), calls=%async_computation.1 | async-start | bytes 1835008 | tf_op jit(solution)/shard_map/all_to_all | solution.py:48
  39.3 38.4 %copy-start.2 = (bf16[448,512]{1,0:T(8,128)(2,1)}, bf16[448,512]{1,0:T(8,128)(2,1)S(1)}, u32[]{:S(2)}) copy-start(bf16[448,512]{1,0:T(8,128)(2,1)S(1)} %collective-permute-done.1.refs_2_) | copy-start | bytes 1376260
  39.3 15.2 %collective-permute-start.2 = (bf16[448,512]{1,0:T(8,128)(2,1)S(1)}, bf16[448,512]{1,0:T(8,128)(2,1)}, u32[]{:S(2)}, u32[]{:S(2)}) collective-permute-start(bf16[448,512]{1,0:T(8,128)(2,1)S(1)} %collective-permute-done.1.refs_2_), channel_id=1, source_target_pairs={{0,128},{128,256},{256,384},{384,0},{1,129},{129,257},{257,385},{3... | collective-permute-start | bytes 1376264 | tf_op jit(solution)/shard_map/ppermute | solution.py:221
  54.5 14.5 %collective-permute-start.3 = (bf16[448,512]{1,0:T(8,128)(2,1)}, bf16[448,512]{1,0:T(8,128)(2,1)}, u32[]{:S(2)}, u32[]{:S(2)}) collective-permute-start(bf16[448,512]{1,0:T(8,128)(2,1)} %collective-permute-done.2.refs_4_), channel_id=1, source_target_pairs={{0,128},{128,256},{256,384},{384,0},{1,129},{129,257},{257,385},{3... | collective-permute-start | bytes 1376264 | tf_op jit(solution)/shard_map/ppermute | solution.py:221
  57.2 26.3 %copy-start = (bf16[912,512]{1,0:T(8,128)(2,1)}, bf16[912,512]{1,0:T(8,128)(2,1)S(1)}, u32[]{:S(2)}) copy-start(bf16[912,512]{1,0:T(8,128)(2,1)S(1)} %collective-permute-done.refs_1_) | copy-start | bytes 2801668
  60.4 17.2 %copy-start.1 = (bf16[512,448]{0,1:T(8,128)(2,1)S(1)}, bf16[512,448]{0,1:T(8,128)(2,1)}, u32[]{:S(2)}) copy-start(bf16[512,448]{0,1:T(8,128)(2,1)} %param.10) | copy-start | bytes 1376260
  68.9 17.4 %all-to-all-start.2 = ((bf16[4,128,512]{2,1,0:T(8,128)(2,1)}), bf16[4,128,512]{2,1,0:T(8,128)(2,1)}, u32[]{:S(2)}, u32[]{:S(2)}) async-start(bf16[4,128,512]{2,1,0:T(8,128)(2,1)} %bitcast.8), calls=%async_computation.2 | async-start | bytes 1048576 | tf_op jit(solution)/shard_map/all_to_all | solution.py:251
  73.1 6.7 %collective-permute-start.4 = (bf16[448,512]{1,0:T(8,128)(2,1)S(1)}, bf16[448,512]{1,0:T(8,128)(2,1)}, u32[]{:S(2)}, u32[]{:S(2)}) collective-permute-start(bf16[448,512]{1,0:T(8,128)(2,1)S(1)} %collective-permute-done.1.refs_2_), channel_id=1, source_target_pairs={{0,64},{64,0},{1,65},{65,1},{2,66},{66,2},{3,67},{67,3},{4,68},{68... | collective-permute-start | bytes 1376264 | tf_op jit(solution)/shard_map/ppermute | solution.py:52
  77.8 7.2 %collective-permute-start.6 = (bf16[448,512]{1,0:T(8,128)(2,1)}, bf16[448,512]{1,0:T(8,128)(2,1)S(1)}, u32[]{:S(2)}, u32[]{:S(2)}) collective-permute-start(bf16[448,512]{1,0:T(8,128)(2,1)} %collective-permute-done.3.refs_6_), channel_id=1, source_target_pairs={{0,64},{64,0},{1,65},{65,1},{2,66},{66,2},{3,67},{67,3},{4,68},{68... | collective-permute-start | bytes 1376264 | tf_op jit(solution)/shard_map/ppermute | solution.py:52
  81.0 4.1 %collective-permute-start.5 = (bf16[448,512]{1,0:T(8,128)(2,1)}, bf16[448,512]{1,0:T(8,128)(2,1)S(1)}, u32[]{:S(2)}, u32[]{:S(2)}) collective-permute-start(bf16[448,512]{1,0:T(8,128)(2,1)} %collective-permute-done.2.refs_4_), channel_id=1, source_target_pairs={{0,64},{64,0},{1,65},{65,1},{2,66},{66,2},{3,67},{67,3},{4,68},{68... | collective-permute-start | bytes 1376264 | tf_op jit(solution)/shard_map/ppermute | solution.py:52
  91.3 19.2 %all-to-all-start.3 = ((bf16[16,8,3584]{2,1,0:T(8,128)(2,1)}), bf16[16,8,3584]{2,1,0:T(8,128)(2,1)S(1)}, u32[]{:S(2)}, u32[]{:S(2)}) async-start(bf16[16,8,3584]{2,1,0:T(8,128)(2,1)} %bitcast.36), calls=%async_computation.3 | async-start | bytes 1835008 | tf_op jit(solution)/shard_map/all_to_all | solution.py:287
  97.4 11.0 %copy-start.7 = (bf16[128,512]{1,0:T(8,128)(2,1)S(1)}, bf16[128,512]{1,0:T(8,128)(2,1)}, u32[]{:S(2)}) copy-start(bf16[128,512]{1,0:T(8,128)(2,1)} %get-tuple-element.26) | copy-start | bytes 393220
  97.6 13.9 %copy-start.8 = (f32[512]{0:T(512)}, f32[512]{0:T(512)S(1)}, u32[]{:S(2)}) copy-start(f32[512]{0:T(512)S(1)} %sqrt_add_fusion) | copy-start | bytes 6148
  97.6 10.8 %collective-permute-start.7 = (bf16[1,24,512]{2,1,0:T(8,128)(2,1)S(1)}, bf16[1,24,512]{2,1,0:T(8,128)(2,1)S(1)}, u32[]{:S(2)}, u32[]{:S(2)}) collective-permute-start(bf16[1,24,512]{2,1,0:T(8,128)(2,1)S(1)} %get-tuple-element.41), channel_id=1, source_target_pairs={{0,128},{128,256},{256,384},{384,0},{1,129},{129,257},{257,385},{3... | collective-permute-start | bytes 73736 | tf_op jit(solution)/shard_map/ppermute | solution.py:221
  101.2 7.2 %collective-permute-start.8 = (bf16[1,24,512]{2,1,0:T(8,128)(2,1)S(1)}, bf16[1,24,512]{2,1,0:T(8,128)(2,1)S(1)}, u32[]{:S(2)}, u32[]{:S(2)}) collective-permute-start(bf16[1,24,512]{2,1,0:T(8,128)(2,1)S(1)} %get-tuple-element.40), channel_id=1, source_target_pairs={{0,256},{128,384},{256,0},{384,128},{1,257},{129,385},{257,1},{385... | collective-permute-start | bytes 73736 | tf_op jit(solution)/shard_map/ppermute | solution.py:221
  105.2 4.9 %collective-permute-start.9 = (bf16[1,24,512]{2,1,0:T(8,128)(2,1)S(1)}, bf16[1,24,512]{2,1,0:T(8,128)(2,1)S(1)}, u32[]{:S(2)}, u32[]{:S(2)}) collective-permute-start(bf16[1,24,512]{2,1,0:T(8,128)(2,1)S(1)} %get-tuple-element.39), channel_id=1, source_target_pairs={{0,384},{128,0},{256,128},{384,256},{1,385},{129,1},{257,129},{385... | collective-permute-start | bytes 73736 | tf_op jit(solution)/shard_map/ppermute | solution.py:221
  111.5 19.3 %all-to-all-start.4 = ((bf16[4,8,3712]{2,1,0:T(8,128)(2,1)}), bf16[4,8,3712]{2,1,0:T(8,128)(2,1)S(1)}, u32[]{:S(2)}, u32[]{:S(2)}) async-start(bf16[4,8,3712]{2,1,0:T(8,128)(2,1)} %broadcast_in_dim.45), calls=%async_computation.4 | async-start | bytes 475136 | tf_op jit(solution)/shard_map/all_to_all | solution.py:48
  118.3 7.1 %collective-permute-start.10 = (bf16[512,448]{1,0:T(8,128)(2,1)S(1)}, bf16[512,448]{1,0:T(8,128)(2,1)S(1)}, u32[]{:S(2)}, u32[]{:S(2)}) collective-permute-start(bf16[512,448]{1,0:T(8,128)(2,1)S(1)} %get-tuple-element.38), channel_id=1, source_target_pairs={{0,64},{64,0},{1,65},{65,1},{2,66},{66,2},{3,67},{67,3},{4,68},{68... | collective-permute-start | bytes 1376264 | tf_op jit(solution)/shard_map/ppermute | solution.py:52
  125.3 24.4 %copy-start.11 = (bf16[512,448]{1,0:T(8,128)(2,1)}, bf16[512,448]{1,0:T(8,128)(2,1)S(1)}, u32[]{:S(2)}) copy-start(bf16[512,448]{1,0:T(8,128)(2,1)S(1)} %collective-permute-done.10) | copy-start | bytes 1376260
  149.7 32.4 %copy-start.12 = (bf16[512,448]{1,0:T(8,128)(2,1)S(1)}, bf16[512,448]{1,0:T(8,128)(2,1)}, u32[]{:S(2)}) copy-start(bf16[512,448]{1,0:T(8,128)(2,1)} %copy-done.11) | copy-start | bytes 1376260
  174.5 7.7 %collective-permute-start.11 = (bf16[4,136,512]{2,1,0:T(8,128)(2,1)S(1)}, bf16[4,136,512]{2,1,0:T(8,128)(2,1)S(1)}, u32[]{:S(2)}, u32[]{:S(2)}) collective-permute-start(bf16[4,136,512]{2,1,0:T(8,128)(2,1)S(1)} %bitcast.37), channel_id=1, source_target_pairs={{0,64},{64,0},{1,65},{65,1},{2,66},{66,2},{3,67},{67,3},{4,68},{68... | collective-permute-start | bytes 1671176 | tf_op jit(solution)/shard_map/ppermute | solution.py:52
  (6 other events, 12.8 us)

commit v10 on v5

--- a/solution.py
+++ b/solution.py
@@ -214,10 +214,24 @@
     halves = jnp.broadcast_to(padded.reshape(CORES, 1, half, chans), (CORES, HIGH, half, chans))
     halves = halves.reshape(CORES * HIGH, half, chans)
     column = lax.all_to_all(halves, ("core", "zh"), 0, 0, tiled=True)
-    column = column.reshape(CORES, HIGH, CHIPS, share, chans).transpose(2, 1, 3, 0, 4)
-    column = column.reshape(CHIPS, small, 2 * chans)
-    gathered = spread(column, PLANE, BLOCKS).transpose(1, 0, 2, 3)
+    column = column.reshape(CORES, HIGH, CHIPS, share, chans)
+
+    def lined(blocks):
+        return blocks.transpose(2, 1, 3, 0, 4).reshape(CHIPS, small, 2 * chans)
+
+    own_first = lined(jnp.where(core == 0, column, column[::-1]))
+    column = lined(column)
+    gathered = spread(own_first, PLANE, BLOCKS).transpose(1, 0, 2, 3)
     gathered = gathered.reshape(CHIPS * tokens, 2 * chans)
+
+    acts_here = gathered[:, :chans]
+    acts_there = swap(gathered[:, chans:])
+    enc_pair = jnp.concatenate([enc_weight, enc_there], axis=0)
+    sums = jnp.dot(gathered, enc_pair, preferred_element_type=F32).astype(BF)
+    quarter = lax.all_to_all(sums.reshape(CHIPS, tokens, latents), "zl", 0, 0, tiled=True)
+    partial_value, codes, slopes = decode(quarter, enc_bias, dec_all, tokens)
+
+    column, partial_value = lax.optimization_barrier((column, partial_value))
 
     def folded(rows_of):
         fill = [(0, 0)] * (rows_of.ndim - 1) + [(0, 2 * latents - 2 * chans)]
@@ -233,18 +247,8 @@
         block = lax.dynamic_index_in_dim(extra, (chip + away) & (CHIPS - 1), 0)
         ways = [(i, (i + away) % CHIPS) for i in range(CHIPS)]
         came.append(lax.ppermute(block, "zl", ways) if away else block)
-    gathered, *came = lax.optimization_barrier((gathered, *came))
     turned = jnp.concatenate([came[-k % CHIPS] for k in range(2 * CHIPS - 1)], axis=0)
     mine = lax.dynamic_slice_in_dim(turned, (CHIPS - chip) & (CHIPS - 1), CHIPS, axis=0)
-
-    first_half, second_half = gathered[:, :chans], gathered[:, chans:]
-    acts_here = jnp.where(core == 0, first_half, second_half)
-    acts_there = swap(jnp.where(core == 0, second_half, first_half))
-
-    enc_pair = ordered(enc_weight, enc_there, 0)
-    sums = jnp.dot(gathered, enc_pair, preferred_element_type=F32).astype(BF)
-    quarter = lax.all_to_all(sums.reshape(CHIPS, tokens, latents), "zl", 0, 0, tiled=True)
-    partial_value, codes, slopes = decode(quarter, enc_bias, dec_all, tokens)
 
     dec_norms = jnp.zeros((latents,), F32)
     for layer in range(LAYERS):
@@ -259,6 +263,7 @@
     got = lax.all_to_all(
         partial_value.reshape(BLOCKS, small, wide), PLANE, 0, 0, tiled=True
     )
+    got, mine = lax.optimization_barrier((got, mine))
     summed = jnp.sum(got.astype(F32), axis=0).astype(BF)
     again = spread(jnp.concatenate([summed, sparse.astype(BF)], axis=1), "zh", HIGH)
     again, acts_there = lax.optimization_barrier((again, acts_there))

time: 187 us -> 187 us (level)
  waiting for transfers between devices: 46.3 us -> 50.9 us
  matrix products: 6.83 us -> 4.6 us
  blocking collectives: 34.8 us -> 32.6 us
  other arithmetic: 5.85 us -> 3.97 us
    all_to_all x1, waiting for transfers between devices: 11.3 us -> 2.99 us  [body(): lax.all_to_all(partial_value.reshape(BLOCKS, small, wide), PLANE, 0, 0, t...]
    all_to_all x1, waiting for transfers between devices: 7.48 us -> 12.6 us  [body(): column = lax.all_to_all(halves, ('core', 'zh'), 0, 0, tiled=True)]
    all_to_all x2, waiting for transfers between devices: 15.9 us -> 20.4 us  [spread(): return lax.all_to_all(copies, axes, 0, 0, tiled=True)]
    ppermute x4, starting transfers between devices: 15.1 us -> 19.3 us  [swap(): return lax.ppermute(value, 'core', [(0, 1), (1, 0)])]
    ppermute x3, starting transfers between devices: 10.4 us -> 7.2 us  [body(): came.append(lax.ppermute(block, 'zl', ways) if away else block)]
    all_to_all x1, blocking collectives: 19.4 us -> 17 us  [body(): grads = lax.all_to_all(copies, PLANE, 0, 0, tiled=True)]
    ppermute x4, waiting for transfers between devices: 1.01 us -> 3.27 us  [swap(): return lax.ppermute(value, 'core', [(0, 1), (1, 0)])]
  transfers between devices with their start and end apart: 13 -> 13, of which waited for: 6 -> 9; matrix products, arithmetic and copies ran while one was open for 7% -> 5% of each run, Pallas kernels for 2% -> 0%
where the time goes in v10:
time: 187 us; the launch traced here: 186 us
  starting transfers between devices  69.1 us (37%)
  waiting for transfers between devices  50.9 us (27%)
  blocking collectives  32.6 us (17%)
  between operations  14.4 us (8%)
  Pallas kernels  6.53 us (3%)
  matrix products  4.6 us (2%)
  local copies, waits for them, and re-layouts  3.98 us (2%)
  other arithmetic  3.97 us (2%)
    all_to_all x2, waiting for transfers between devices, spread(): return lax.all_to_all(copies, axes, 0, 0, tiled=True)  20.4 us
    ppermute x4, starting transfers between devices, swap(): return lax.ppermute(value, 'core', [(0, 1), (1, 0)])  19.3 us
    all_to_all x1, blocking collectives, body(): grads = lax.all_to_all(copies, PLANE, 0, 0, tiled=True)  17 us
    all_to_all x1, starting transfers between devices, body(): column = lax.all_to_all(halves, ('core', 'zh'), 0, 0, tiled=True)  16.6 us
    all_gather x1, blocking collectives, body(): pre_here = lax.all_gather(last, 'zl', axis=0)  15.6 us
    all_to_all x2, starting transfers between devices, spread(): return lax.all_to_all(copies, axes, 0, 0, tiled=True)  15.3 us
    all_to_all x1, waiting for transfers between devices, body(): column = lax.all_to_all(halves, ('core', 'zh'), 0, 0, tiled=True)  12.6 us
    all_to_all x1, waiting for transfers between devices, body(): lax.all_to_all(sums.reshape(CHIPS, tokens, latents), 'zl', 0, 0, tiled=True)  9.59 us
  transfers between devices with their start and end apart: 13, of which 9 were waited for; matrix products, arithmetic and copies ran while one was open for 5% of the time, Pallas kernels for 0%

profile of v10, /device:TPU:1, one launch (start us, length us, event | category | flops | bytes accessed | tf_op | source)
XLA Modules:
  0.0 186.0 jit_solution(3462143604832325039)
XLA Ops:
  9.3 16.6 %all-to-all-start = ((bf16[8,8,448]{2,1,0:T(8,128)(2,1)}), bf16[8,8,448]{2,1,0:T(8,128)(2,1)S(1)}, u32[]{:S(2)}, u32[]{:S(2)}) async-start(bf16[8,8,448]{2,1,0:T(8,128)(2,1)} %bitcast.1), calls=%async_computation | async-start | bytes 131072 | tf_op jit(solution)/shard_map/all_to_all | solution.py:216
  25.9 12.6 %all-to-all-done = bf16[8,8,448]{2,1,0:T(8,128)(2,1)S(1)} async-done(((bf16[8,8,448]{2,1,0:T(8,128)(2,1)}), bf16[8,8,448]{2,1,0:T(8,128)(2,1)S(1)}, u32[]{:S(2)}, u32[]{:S(2)}) %all-to-all-start) | async-done | bytes 57376 | tf_op jit(solution)/shard_map/all_to_all | solution.py:216
  39.8 6.8 %all-to-all-start.1 = ((bf16[16,4,8,896]{3,2,1,0:T(8,128)(2,1)}), bf16[16,4,8,896]{3,2,1,0:T(8,128)(2,1)S(1)}, u32[]{:S(2)}, u32[]{:S(2)}) async-start(bf16[16,4,8,896]{3,2,1,0:T(8,128)(2,1)} %broadcast_in_dim.15), calls=%async_computation.1 | async-start | bytes 1835008 | tf_op jit(solution)/shard_map/all_to_all | solution.py:48
  46.5 2.6 %collective-permute-start = (bf16[448,512]{1,0:T(8,128)(2,1)S(1)}, bf16[448,512]{1,0:T(8,128)(2,1)S(1)}, u32[]{:S(2)}, u32[]{:S(2)}) collective-permute-start(bf16[448,512]{1,0:T(8,128)(2,1)S(1)} %copy-done.4), channel_id=1, source_target_pairs={{0,64},{64,0},{1,65},{65,1},{2,66},{66,2},{3,67},{67,3},{4,68},{68... | collective-permute-start | bytes 1376264 | tf_op jit(solution)/shard_map/ppermute | solution.py:52
  49.1 12.3 %all-to-all-done.1 = bf16[16,4,8,896]{3,2,1,0:T(8,128)(2,1)S(1)} async-done(((bf16[16,4,8,896]{3,2,1,0:T(8,128)(2,1)}), bf16[16,4,8,896]{3,2,1,0:T(8,128)(2,1)S(1)}, u32[]{:S(2)}, u32[]{:S(2)}) %all-to-all-start.1) | async-done | bytes 917536 | tf_op jit(solution)/shard_map/all_to_all | solution.py:48
  61.5 1.5 convolution_convert_fusion
  63.0 4.9 %all-to-all-start.2 = ((bf16[4,128,512]{2,1,0:T(8,128)(2,1)}), bf16[4,128,512]{2,1,0:T(8,128)(2,1)S(1)}, u32[]{:S(2)}, u32[]{:S(2)}) async-start(bf16[4,128,512]{2,1,0:T(8,128)(2,1)} %bitcast.8), calls=%async_computation.2 | async-start | bytes 1048576 | tf_op jit(solution)/shard_map/all_to_all | solution.py:231
  67.9 3.2 %collective-permute-start.1 = (f32[448]{0:T(512)S(1)}, f32[448]{0:T(512)S(1)}, u32[]{:S(2)}, u32[]{:S(2)}) collective-permute-start(f32[448]{0:T(512)S(1)} %copy-done.1), channel_id=1, source_target_pairs={{0,64},{64,0},{1,65},{65,1},{2,66},{66,2},{3,67},{67,3},{4,68},{68... | collective-permute-start | bytes 5384 | tf_op jit(solution)/shard_map/ppermute | solution.py:52
  72.3 9.6 %all-to-all-done.2.quarter_ref = bf16[4,128,512]{2,1,0:T(8,128)(2,1)S(1)} async-done(((bf16[4,128,512]{2,1,0:T(8,128)(2,1)}), bf16[4,128,512]{2,1,0:T(8,128)(2,1)S(1)}, u32[]{:S(2)}, u32[]{:S(2)}) %all-to-all-start.2) | async-done | bytes 524320 | tf_op jit(solution)/shard_map/all_to_all | solution.py:231
  81.9 4.0 %decode.1 = (bf16[128,3584]{1,0:T(8,128)(2,1)}, bf16[128,512]{1,0:T(8,128)(2,1)S(1)}, f32[128,512]{1,0:T(8,128)S(1)}) custom-call(bf16[4,128,512]{2,1,0:T(8,128)(2,1)S(1)} %all-to-all-done.2.quarter_ref, f32[1,512]{1,0:T(1,128)S(1)} %bitcast.33, bf16[3584,512]{1,0:T(8,128)(2,1)} %all-gather.3.cloned.1.call-done.dec_ref), custom_call_target="tpu_custom_call" | custom-call | flops 469762048 | bytes 4587520 | tf_op jit(solution)/shard_map/decode/pallas_call | solution.py:95
  85.9 5.7 %all-to-all-start.3 = ((bf16[16,8,3584]{2,1,0:T(8,128)(2,1)}), bf16[16,8,3584]{2,1,0:T(8,128)(2,1)S(1)}, u32[]{:S(2)}, u32[]{:S(2)}) async-start(bf16[16,8,3584]{2,1,0:T(8,128)(2,1)} %bitcast.11), calls=%async_computation.3 | async-start | bytes 1835008 | tf_op jit(solution)/shard_map/all_to_all | solution.py:263
  91.7 2.9 %collective-permute-start.2 = (bf16[1,24,512]{2,1,0:T(8,128)(2,1)S(1)}, bf16[1,24,512]{2,1,0:T(8,128)(2,1)S(1)}, u32[]{:S(2)}, u32[]{:S(2)}) collective-permute-start(bf16[1,24,512]{2,1,0:T(8,128)(2,1)S(1)} %get-tuple-element.32), channel_id=1, source_target_pairs={{0,384},{128,0},{256,128},{384,256},{1,385},{129,1},{257,129},{385... | collective-permute-start | bytes 73736 | tf_op jit(solution)/shard_map/ppermute | solution.py:249
  94.6 1.9 %collective-permute-start.3 = (bf16[1,24,512]{2,1,0:T(8,128)(2,1)S(1)}, bf16[1,24,512]{2,1,0:T(8,128)(2,1)S(1)}, u32[]{:S(2)}, u32[]{:S(2)}) collective-permute-start(bf16[1,24,512]{2,1,0:T(8,128)(2,1)S(1)} %get-tuple-element.31), channel_id=1, source_target_pairs={{0,256},{128,384},{256,0},{384,128},{1,257},{129,385},{257,1},{385... | collective-permute-start | bytes 73736 | tf_op jit(solution)/shard_map/ppermute | solution.py:249
  96.5 2.4 %collective-permute-start.4 = (bf16[1,24,512]{2,1,0:T(8,128)(2,1)S(1)}, bf16[1,24,512]{2,1,0:T(8,128)(2,1)S(1)}, u32[]{:S(2)}, u32[]{:S(2)}) collective-permute-start(bf16[1,24,512]{2,1,0:T(8,128)(2,1)S(1)} %get-tuple-element.29), channel_id=1, source_target_pairs={{0,128},{128,256},{256,384},{384,0},{1,129},{129,257},{257,385},{3... | collective-permute-start | bytes 73736 | tf_op jit(solution)/shard_map/ppermute | solution.py:249
  98.9 2.8 %multiply_reduce_fusion.1 = (f32[512]{0:T(512)S(1)}, f32[512]{0:T(512)S(1)}) fusion(bf16[3584,512]{1,0:T(8,128)(2,1)} %all-gather.3.cloned.1.call-done.dec_ref), kind=kLoop, calls=%fused_computation.1 | loop fusion | flops 5504000 | bytes 3674112 | tf_op jit(solution)/shard_map/reduce_sum | solution.py:256
  103.2 3.0 %all-to-all-done.3 = bf16[16,8,3584]{2,1,0:T(8,128)(2,1)S(1)} async-done(((bf16[16,8,3584]{2,1,0:T(8,128)(2,1)}), bf16[16,8,3584]{2,1,0:T(8,128)(2,1)S(1)}, u32[]{:S(2)}, u32[]{:S(2)}) %all-to-all-start.3) | async-done | bytes 917536 | tf_op jit(solution)/shard_map/all_to_all | solution.py:263
  107.0 8.6 %all-to-all-start.4 = ((bf16[4,8,3712]{2,1,0:T(8,128)(2,1)}), bf16[4,8,3712]{2,1,0:T(8,128)(2,1)S(1)}, u32[]{:S(2)}, u32[]{:S(2)}) async-start(bf16[4,8,3712]{2,1,0:T(8,128)(2,1)} %broadcast_in_dim.33), calls=%async_computation.4 | async-start | bytes 475136 | tf_op jit(solution)/shard_map/all_to_all | solution.py:48
  115.9 4.7 %collective-permute-start.5 = (bf16[512,448]{1,0:T(8,128)(2,1)S(1)}, bf16[512,448]{1,0:T(8,128)(2,1)S(1)}, u32[]{:S(2)}, u32[]{:S(2)}) collective-permute-start(bf16[512,448]{1,0:T(8,128)(2,1)S(1)} %get-tuple-element.28), channel_id=1, source_target_pairs={{0,64},{64,0},{1,65},{65,1},{2,66},{66,2},{3,67},{67,3},{4,68},{68... | collective-permute-start | bytes 1376264 | tf_op jit(solution)/shard_map/ppermute | solution.py:52
  122.1 8.2 %all-to-all-done.4.got_ref = bf16[4,8,3712]{2,1,0:T(8,128)(2,1)S(1)} async-done(((bf16[4,8,3712]{2,1,0:T(8,128)(2,1)}), bf16[4,8,3712]{2,1,0:T(8,128)(2,1)S(1)}, u32[]{:S(2)}, u32[]{:S(2)}) %all-to-all-start.4) | async-done | bytes 237600 | tf_op jit(solution)/shard_map/all_to_all | solution.py:48
  130.5 17.0 %all_to_all.30 = bf16[16,8,3712]{2,1,0:T(8,128)(2,1)S(1)} all-to-all(bf16[16,8,3712]{2,1,0:T(8,128)(2,1)S(1)} %error.1), channel_id=1, replica_groups=mesh['zl'=4,'core'=2,'y'=4,'x'=4,'zh'=4] {'y','x'}, dimensions={0} | all-to-all | bytes 1900544 | tf_op jit(solution)/shard_map/all_to_all | solution.py:271
  147.5 2.5 %back.1 = bf16[136,512]{1,0:T(8,128)(2,1)S(1)} custom-call(bf16[128,3712]{1,0:T(8,128)(2,1)S(1)} %bitcast.31, bf16[3584,512]{1,0:T(8,128)(2,1)} %all-gather.3.cloned.1.call-done.dec_ref, f32[128,512]{1,0:T(8,128)S(1)} %get-tuple-element.20.slopes_ref, f32[1,512]{1,0:T(1,128)S(1)} %bitcast.32), custom_call_target="tpu_custom_call" | custom-call | flops 469762048 | bytes 4587520 | tf_op jit(solution)/shard_map/back/pallas_call | solution.py:177
  150.0 15.6 %all-gather = bf16[544,512]{1,0:T(8,128)(2,1)S(1)} all-gather(bf16[136,512]{1,0:T(8,128)(2,1)S(1)} %back.1), channel_id=2, replica_groups=mesh['zl'=4,'core'=2,'y'=4,'x'=4,'zh'=4] {'zl'}, dimensions={0}, use_global_device_ids=true | all-gather | bytes 696320 | tf_op jit(solution)/shard_map/all_gather | solution.py:273
  165.6 8.9 %collective-permute-start.6 = (bf16[4,136,512]{2,1,0:T(8,128)(2,1)S(1)}, bf16[4,136,512]{2,1,0:T(8,128)(2,1)S(1)}, u32[]{:S(2)}, u32[]{:S(2)}) collective-permute-start(bf16[4,136,512]{2,1,0:T(8,128)(2,1)S(1)} %bitcast.37), channel_id=1, source_target_pairs={{0,64},{64,0},{1,65},{65,1},{2,66},{66,2},{3,67},{67,3},{4,68},{68... | collective-permute-start | bytes 1671176 | tf_op jit(solution)/shard_map/ppermute | solution.py:52
  176.7 2.5 %subtract_convert_fusion = (bf16[448,512]{1,0:T(8,128)(2,1)}, f32[448,512]{1,0:T(8,128)}, f32[448,512]{1,0:T(8,128)}) fusion(bf16[448,512]{1,0:T(8,128)(2,1)S(1)} %copy-done.4, f32[448,512]{1,0:T(8,128)S(1)} %copy-done.2, f32[448,512]{1,0:T(8,128)S(1)} %copy-done.3, f32[448,512]{1,0:T(8,128)S(1)} %convolution_bitcast_fusion.1, ...), kind=kOutput, calls=%fused_computation.11 | convolution fusion | flops 253231104 | bytes 6520832 | tf_op jit(solution)/shard_map/dot_general | solution.py:278
  (62 shorter events, 11.1 us)
Async XLA Ops:
  7.2 39.4 %copy-start.4 = (bf16[448,512]{1,0:T(8,128)(2,1)S(1)}, bf16[448,512]{1,0:T(8,128)(2,1)}, u32[]{:S(2)}) copy-start(bf16[448,512]{1,0:T(8,128)(2,1)} %param.8) | copy-start | bytes 1376260
  7.2 74.7 %all-gather.3.cloned.1.call-start = ((), (), s32[]{:S(2)}) async-start(), calls=%async_computation.6 | async-start | bytes 4128768 | tf_op jit(solution)/shard_map/all_gather | solution.py:205
  9.3 29.2 %all-to-all-start = ((bf16[8,8,448]{2,1,0:T(8,128)(2,1)}), bf16[8,8,448]{2,1,0:T(8,128)(2,1)S(1)}, u32[]{:S(2)}, u32[]{:S(2)}) async-start(bf16[8,8,448]{2,1,0:T(8,128)(2,1)} %bitcast.1), calls=%async_computation | async-start | bytes 131072 | tf_op jit(solution)/shard_map/all_to_all | solution.py:216
  39.8 21.7 %all-to-all-start.1 = ((bf16[16,4,8,896]{3,2,1,0:T(8,128)(2,1)}), bf16[16,4,8,896]{3,2,1,0:T(8,128)(2,1)S(1)}, u32[]{:S(2)}, u32[]{:S(2)}) async-start(bf16[16,4,8,896]{3,2,1,0:T(8,128)(2,1)} %broadcast_in_dim.15), calls=%async_computation.1 | async-start | bytes 1835008 | tf_op jit(solution)/shard_map/all_to_all | solution.py:48
  46.5 21.4 %copy-start.1 = (f32[448]{0:T(512)S(1)}, f32[448]{0:T(512)}, u32[]{:S(2)}) copy-start(f32[448]{0:T(512)} %param.11) | copy-start | bytes 5380
  46.5 35.3 %copy-start = (f32[512]{0:T(512)S(1)}, f32[512]{0:T(512)}, u32[]{:S(2)}) copy-start(f32[512]{0:T(512)} %param.9) | copy-start | bytes 6148
  46.5 14.9 %collective-permute-start = (bf16[448,512]{1,0:T(8,128)(2,1)S(1)}, bf16[448,512]{1,0:T(8,128)(2,1)S(1)}, u32[]{:S(2)}, u32[]{:S(2)}) collective-permute-start(bf16[448,512]{1,0:T(8,128)(2,1)S(1)} %copy-done.4), channel_id=1, source_target_pairs={{0,64},{64,0},{1,65},{65,1},{2,66},{66,2},{3,67},{67,3},{4,68},{68... | collective-permute-start | bytes 1376264 | tf_op jit(solution)/shard_map/ppermute | solution.py:52
  63.0 18.8 %all-to-all-start.2 = ((bf16[4,128,512]{2,1,0:T(8,128)(2,1)}), bf16[4,128,512]{2,1,0:T(8,128)(2,1)S(1)}, u32[]{:S(2)}, u32[]{:S(2)}) async-start(bf16[4,128,512]{2,1,0:T(8,128)(2,1)} %bitcast.8), calls=%async_computation.2 | async-start | bytes 1048576 | tf_op jit(solution)/shard_map/all_to_all | solution.py:231
  67.9 4.0 %collective-permute-start.1 = (f32[448]{0:T(512)S(1)}, f32[448]{0:T(512)S(1)}, u32[]{:S(2)}, u32[]{:S(2)}) collective-permute-start(f32[448]{0:T(512)S(1)} %copy-done.1), channel_id=1, source_target_pairs={{0,64},{64,0},{1,65},{65,1},{2,66},{66,2},{3,67},{67,3},{4,68},{68... | collective-permute-start | bytes 5384 | tf_op jit(solution)/shard_map/ppermute | solution.py:52
  85.9 20.3 %all-to-all-start.3 = ((bf16[16,8,3584]{2,1,0:T(8,128)(2,1)}), bf16[16,8,3584]{2,1,0:T(8,128)(2,1)S(1)}, u32[]{:S(2)}, u32[]{:S(2)}) async-start(bf16[16,8,3584]{2,1,0:T(8,128)(2,1)} %bitcast.11), calls=%async_computation.3 | async-start | bytes 1835008 | tf_op jit(solution)/shard_map/all_to_all | solution.py:263
  91.7 10.2 %collective-permute-start.2 = (bf16[1,24,512]{2,1,0:T(8,128)(2,1)S(1)}, bf16[1,24,512]{2,1,0:T(8,128)(2,1)S(1)}, u32[]{:S(2)}, u32[]{:S(2)}) collective-permute-start(bf16[1,24,512]{2,1,0:T(8,128)(2,1)S(1)} %get-tuple-element.32), channel_id=1, source_target_pairs={{0,384},{128,0},{256,128},{384,256},{1,385},{129,1},{257,129},{385... | collective-permute-start | bytes 73736 | tf_op jit(solution)/shard_map/ppermute | solution.py:249
  94.6 7.3 %collective-permute-start.3 = (bf16[1,24,512]{2,1,0:T(8,128)(2,1)S(1)}, bf16[1,24,512]{2,1,0:T(8,128)(2,1)S(1)}, u32[]{:S(2)}, u32[]{:S(2)}) collective-permute-start(bf16[1,24,512]{2,1,0:T(8,128)(2,1)S(1)} %get-tuple-element.31), channel_id=1, source_target_pairs={{0,256},{128,384},{256,0},{384,128},{1,257},{129,385},{257,1},{385... | collective-permute-start | bytes 73736 | tf_op jit(solution)/shard_map/ppermute | solution.py:249
  96.5 6.7 %collective-permute-start.4 = (bf16[1,24,512]{2,1,0:T(8,128)(2,1)S(1)}, bf16[1,24,512]{2,1,0:T(8,128)(2,1)S(1)}, u32[]{:S(2)}, u32[]{:S(2)}) collective-permute-start(bf16[1,24,512]{2,1,0:T(8,128)(2,1)S(1)} %get-tuple-element.29), channel_id=1, source_target_pairs={{0,128},{128,256},{256,384},{384,0},{1,129},{129,257},{257,385},{3... | collective-permute-start | bytes 73736 | tf_op jit(solution)/shard_map/ppermute | solution.py:249
  107.0 23.3 %all-to-all-start.4 = ((bf16[4,8,3712]{2,1,0:T(8,128)(2,1)}), bf16[4,8,3712]{2,1,0:T(8,128)(2,1)S(1)}, u32[]{:S(2)}, u32[]{:S(2)}) async-start(bf16[4,8,3712]{2,1,0:T(8,128)(2,1)} %broadcast_in_dim.33), calls=%async_computation.4 | async-start | bytes 475136 | tf_op jit(solution)/shard_map/all_to_all | solution.py:48
  115.9 6.2 %collective-permute-start.5 = (bf16[512,448]{1,0:T(8,128)(2,1)S(1)}, bf16[512,448]{1,0:T(8,128)(2,1)S(1)}, u32[]{:S(2)}, u32[]{:S(2)}) collective-permute-start(bf16[512,448]{1,0:T(8,128)(2,1)S(1)} %get-tuple-element.28), channel_id=1, source_target_pairs={{0,64},{64,0},{1,65},{65,1},{2,66},{66,2},{3,67},{67,3},{4,68},{68... | collective-permute-start | bytes 1376264 | tf_op jit(solution)/shard_map/ppermute | solution.py:52
  147.5 29.2 %copy-start.2 = (f32[448,512]{1,0:T(8,128)S(1)}, f32[448,512]{1,0:T(8,128)}, u32[]{:S(2)}) copy-start(f32[448,512]{1,0:T(8,128)} %param.12) | copy-start | bytes 2752516
  147.5 29.2 %copy-start.3 = (f32[448,512]{1,0:T(8,128)S(1)}, f32[448,512]{1,0:T(8,128)}, u32[]{:S(2)}) copy-start(f32[448,512]{1,0:T(8,128)} %param.13) | copy-start | bytes 2752516
  165.6 10.4 %collective-permute-start.6 = (bf16[4,136,512]{2,1,0:T(8,128)(2,1)S(1)}, bf16[4,136,512]{2,1,0:T(8,128)(2,1)S(1)}, u32[]{:S(2)}, u32[]{:S(2)}) collective-permute-start(bf16[4,136,512]{2,1,0:T(8,128)(2,1)S(1)} %bitcast.37), channel_id=1, source_target_pairs={{0,64},{64,0},{1,65},{65,1},{2,66},{66,2},{3,67},{67,3},{4,68},{68... | collective-permute-start | bytes 1671176 | tf_op jit(solution)/shard_map/ppermute | solution.py:52
Sparse Core Ops, SparseCore 0:
  10.1 58.1 all-gather.2

commit v11 on v10

--- a/solution.py
+++ b/solution.py
@@ -265,7 +265,7 @@
     )
     got, mine = lax.optimization_barrier((got, mine))
     summed = jnp.sum(got.astype(F32), axis=0).astype(BF)
-    again = spread(jnp.concatenate([summed, sparse.astype(BF)], axis=1), "zh", HIGH)
+    again = lax.all_gather(jnp.concatenate([summed, sparse.astype(BF)], axis=1), "zh", axis=0)
     again, acts_there = lax.optimization_barrier((again, acts_there))
     copies = error_copies(again, mine, real, inv_batch)
     grads = lax.all_to_all(copies, PLANE, 0, 0, tiled=True)

time: 187 us -> 180 us (0.963)
  blocking collectives: 32.6 us -> 47.4 us
  waiting for transfers between devices: 50.9 us -> 38.6 us
  starting transfers between devices: 69.1 us -> 60.5 us
    all_gather x0 -> x1, blocking collectives: none -> 19 us  [body(): lax.all_gather(jnp.concatenate([summed, sparse.astype(BF)], axis=1), 'zh'...]
    all_to_all x2 -> x1, starting transfers between devices: 15.3 us -> 6.75 us  [spread(): return lax.all_to_all(copies, axes, 0, 0, tiled=True)]
    all_to_all x2 -> x1, waiting for transfers between devices: 20.4 us -> 12.3 us  [spread(): return lax.all_to_all(copies, axes, 0, 0, tiled=True)]
    all_gather x1, blocking collectives: 15.6 us -> 12.2 us  [body(): pre_here = lax.all_gather(last, 'zl', axis=0)]
    all_to_all x1, waiting for transfers between devices: 9.59 us -> 7.04 us  [body(): lax.all_to_all(sums.reshape(CHIPS, tokens, latents), 'zl', 0, 0, tiled=True)]
  transfers between devices with their start and end apart: 13 -> 12, of which waited for: 9 -> 7; matrix products, arithmetic and copies ran while one was open for 5% -> 5% of each run, Pallas kernels for 0% -> 2%
where the time goes in v11:
time: 180 us; the launch traced here: 179 us
  starting transfers between devices  60.5 us (34%)
  blocking collectives  47.4 us (26%)
  waiting for transfers between devices  38.6 us (21%)
  between operations  14.4 us (8%)
  Pallas kernels  6.55 us (4%)
  matrix products  4.59 us (3%)
  other arithmetic  3.97 us (2%)
  local copies, waits for them, and re-layouts  3.28 us (2%)
    ppermute x4, starting transfers between devices, swap(): return lax.ppermute(value, 'core', [(0, 1), (1, 0)])  19.4 us
    all_gather x1, blocking collectives, body(): lax.all_gather(jnp.concatenate([summed, sparse.astype(BF)], axis=1), 'zh'...  19 us
    all_to_all x1, starting transfers between devices, body(): column = lax.all_to_all(halves, ('core', 'zh'), 0, 0, tiled=True)  16.6 us
    all_to_all x1, blocking collectives, body(): grads = lax.all_to_all(copies, PLANE, 0, 0, tiled=True)  16.2 us
    all_to_all x1, waiting for transfers between devices, body(): column = lax.all_to_all(halves, ('core', 'zh'), 0, 0, tiled=True)  12.6 us
    all_to_all x1, waiting for transfers between devices, spread(): return lax.all_to_all(copies, axes, 0, 0, tiled=True)  12.3 us
    all_gather x1, blocking collectives, body(): pre_here = lax.all_gather(last, 'zl', axis=0)  12.2 us
    ppermute x3, starting transfers between devices, body(): came.append(lax.ppermute(block, 'zl', ways) if away else block)  7.2 us
  transfers between devices with their start and end apart: 12, of which 7 were waited for; matrix products, arithmetic and copies ran while one was open for 5% of the time, Pallas kernels for 2%

profile of v11, /device:TPU:1, one launch (start us, length us, event | category | flops | bytes accessed | tf_op | source)
XLA Modules:
  0.0 179.4 jit_solution(5566211028187369844)
XLA Ops:
  9.3 16.6 %all-to-all-start = ((bf16[8,8,448]{2,1,0:T(8,128)(2,1)}), bf16[8,8,448]{2,1,0:T(8,128)(2,1)S(1)}, u32[]{:S(2)}, u32[]{:S(2)}) async-start(bf16[8,8,448]{2,1,0:T(8,128)(2,1)} %bitcast.1), calls=%async_computation | async-start | bytes 131072 | tf_op jit(solution)/shard_map/all_to_all | solution.py:216
  25.9 12.6 %all-to-all-done = bf16[8,8,448]{2,1,0:T(8,128)(2,1)S(1)} async-done(((bf16[8,8,448]{2,1,0:T(8,128)(2,1)}), bf16[8,8,448]{2,1,0:T(8,128)(2,1)S(1)}, u32[]{:S(2)}, u32[]{:S(2)}) %all-to-all-start) | async-done | bytes 57376 | tf_op jit(solution)/shard_map/all_to_all | solution.py:216
  39.8 6.8 %all-to-all-start.1 = ((bf16[16,4,8,896]{3,2,1,0:T(8,128)(2,1)}), bf16[16,4,8,896]{3,2,1,0:T(8,128)(2,1)S(1)}, u32[]{:S(2)}, u32[]{:S(2)}) async-start(bf16[16,4,8,896]{3,2,1,0:T(8,128)(2,1)} %broadcast_in_dim.25), calls=%async_computation.1 | async-start | bytes 1835008 | tf_op jit(solution)/shard_map/all_to_all | solution.py:48
  46.5 2.6 %collective-permute-start = (bf16[448,512]{1,0:T(8,128)(2,1)S(1)}, bf16[448,512]{1,0:T(8,128)(2,1)S(1)}, u32[]{:S(2)}, u32[]{:S(2)}) collective-permute-start(bf16[448,512]{1,0:T(8,128)(2,1)S(1)} %copy-done.4), channel_id=1, source_target_pairs={{0,64},{64,0},{1,65},{65,1},{2,66},{66,2},{3,67},{67,3},{4,68},{68... | collective-permute-start | bytes 1376264 | tf_op jit(solution)/shard_map/ppermute | solution.py:52
  49.1 12.3 %all-to-all-done.1 = bf16[16,4,8,896]{3,2,1,0:T(8,128)(2,1)S(1)} async-done(((bf16[16,4,8,896]{3,2,1,0:T(8,128)(2,1)}), bf16[16,4,8,896]{3,2,1,0:T(8,128)(2,1)S(1)}, u32[]{:S(2)}, u32[]{:S(2)}) %all-to-all-start.1) | async-done | bytes 917536 | tf_op jit(solution)/shard_map/all_to_all | solution.py:48
  61.5 1.5 convolution_convert_fusion
  63.0 4.9 %all-to-all-start.2 = ((bf16[4,128,512]{2,1,0:T(8,128)(2,1)}), bf16[4,128,512]{2,1,0:T(8,128)(2,1)S(1)}, u32[]{:S(2)}, u32[]{:S(2)}) async-start(bf16[4,128,512]{2,1,0:T(8,128)(2,1)} %bitcast.8), calls=%async_computation.2 | async-start | bytes 1048576 | tf_op jit(solution)/shard_map/all_to_all | solution.py:231
  67.9 3.2 %collective-permute-start.1 = (f32[448]{0:T(512)S(1)}, f32[448]{0:T(512)S(1)}, u32[]{:S(2)}, u32[]{:S(2)}) collective-permute-start(f32[448]{0:T(512)S(1)} %copy-done.1), channel_id=1, source_target_pairs={{0,64},{64,0},{1,65},{65,1},{2,66},{66,2},{3,67},{67,3},{4,68},{68... | collective-permute-start | bytes 5384 | tf_op jit(solution)/shard_map/ppermute | solution.py:52
  72.6 2.2 %collective-permute-start.5 = (bf16[512,448]{1,0:T(8,128)(2,1)S(1)}, bf16[512,448]{1,0:T(8,128)(2,1)S(1)}, u32[]{:S(2)}, u32[]{:S(2)}) collective-permute-start(bf16[512,448]{1,0:T(8,128)(2,1)S(1)} %get-tuple-element.28), channel_id=1, source_target_pairs={{0,64},{64,0},{1,65},{65,1},{2,66},{66,2},{3,67},{67,3},{4,68},{68... | collective-permute-start | bytes 1376264 | tf_op jit(solution)/shard_map/ppermute | solution.py:52
  74.8 7.0 %all-to-all-done.2.quarter_ref = bf16[4,128,512]{2,1,0:T(8,128)(2,1)S(1)} async-done(((bf16[4,128,512]{2,1,0:T(8,128)(2,1)}), bf16[4,128,512]{2,1,0:T(8,128)(2,1)S(1)}, u32[]{:S(2)}, u32[]{:S(2)}) %all-to-all-start.2) | async-done | bytes 524320 | tf_op jit(solution)/shard_map/all_to_all | solution.py:231
  81.9 3.9 %decode.1 = (bf16[128,3584]{1,0:T(8,128)(2,1)}, bf16[128,512]{1,0:T(8,128)(2,1)S(1)}, f32[128,512]{1,0:T(8,128)S(1)}) custom-call(bf16[4,128,512]{2,1,0:T(8,128)(2,1)S(1)} %all-to-all-done.2.quarter_ref, f32[1,512]{1,0:T(1,128)S(1)} %bitcast.35, bf16[3584,512]{1,0:T(8,128)(2,1)} %all-gather.4.cloned.1.call-done.dec_ref), custom_call_target="tpu_custom_call" | custom-call | flops 469762048 | bytes 4587520 | tf_op jit(solution)/shard_map/decode/pallas_call | solution.py:95
  85.9 5.7 %all-to-all-start.3 = ((bf16[16,8,3584]{2,1,0:T(8,128)(2,1)}), bf16[16,8,3584]{2,1,0:T(8,128)(2,1)S(1)}, u32[]{:S(2)}, u32[]{:S(2)}) async-start(bf16[16,8,3584]{2,1,0:T(8,128)(2,1)} %bitcast.11), calls=%async_computation.3 | async-start | bytes 1835008 | tf_op jit(solution)/shard_map/all_to_all | solution.py:263
  91.6 2.9 %collective-permute-start.2 = (bf16[1,24,512]{2,1,0:T(8,128)(2,1)S(1)}, bf16[1,24,512]{2,1,0:T(8,128)(2,1)S(1)}, u32[]{:S(2)}, u32[]{:S(2)}) collective-permute-start(bf16[1,24,512]{2,1,0:T(8,128)(2,1)S(1)} %get-tuple-element.32), channel_id=1, source_target_pairs={{0,384},{128,0},{256,128},{384,256},{1,385},{129,1},{257,129},{385... | collective-permute-start | bytes 73736 | tf_op jit(solution)/shard_map/ppermute | solution.py:249
  94.6 1.9 %collective-permute-start.3 = (bf16[1,24,512]{2,1,0:T(8,128)(2,1)S(1)}, bf16[1,24,512]{2,1,0:T(8,128)(2,1)S(1)}, u32[]{:S(2)}, u32[]{:S(2)}) collective-permute-start(bf16[1,24,512]{2,1,0:T(8,128)(2,1)S(1)} %get-tuple-element.31), channel_id=1, source_target_pairs={{0,256},{128,384},{256,0},{384,128},{1,257},{129,385},{257,1},{385... | collective-permute-start | bytes 73736 | tf_op jit(solution)/shard_map/ppermute | solution.py:249
  96.5 2.4 %collective-permute-start.4 = (bf16[1,24,512]{2,1,0:T(8,128)(2,1)S(1)}, bf16[1,24,512]{2,1,0:T(8,128)(2,1)S(1)}, u32[]{:S(2)}, u32[]{:S(2)}) collective-permute-start(bf16[1,24,512]{2,1,0:T(8,128)(2,1)S(1)} %get-tuple-element.29), channel_id=1, source_target_pairs={{0,128},{128,256},{256,384},{384,0},{1,129},{129,257},{257,385},{3... | collective-permute-start | bytes 73736 | tf_op jit(solution)/shard_map/ppermute | solution.py:249
  98.9 2.8 %multiply_reduce_fusion.1 = (f32[512]{0:T(512)S(1)}, f32[512]{0:T(512)S(1)}) fusion(bf16[3584,512]{1,0:T(8,128)(2,1)} %all-gather.4.cloned.1.call-done.dec_ref), kind=kLoop, calls=%fused_computation.1 | loop fusion | flops 5504000 | bytes 3674112 | tf_op jit(solution)/shard_map/reduce_sum | solution.py:256
  101.8 1.3 collective-permute-done.4
  103.2 3.0 %all-to-all-done.3 = bf16[16,8,3584]{2,1,0:T(8,128)(2,1)S(1)} async-done(((bf16[16,8,3584]{2,1,0:T(8,128)(2,1)}), bf16[16,8,3584]{2,1,0:T(8,128)(2,1)S(1)}, u32[]{:S(2)}, u32[]{:S(2)}) %all-to-all-start.3) | async-done | bytes 917536 | tf_op jit(solution)/shard_map/all_to_all | solution.py:263
  106.3 19.0 %all-gather = bf16[32,3712]{1,0:T(8,128)(2,1)S(1)} all-gather(bf16[8,3712]{1,0:T(8,128)(2,1)S(1)} %pad_maximum_fusion), channel_id=2, replica_groups=mesh['zl'=4,'core'=2,'y'=4,'x'=4,'zh'=4] {'zh'}, dimensions={0}, use_global_device_ids=true | all-gather | bytes 296960 | tf_op jit(solution)/shard_map/all_gather | solution.py:268
  125.5 16.2 %all_to_all.25 = bf16[16,8,3712]{2,1,0:T(8,128)(2,1)S(1)} all-to-all(bf16[16,8,3712]{2,1,0:T(8,128)(2,1)S(1)} %error.1), channel_id=1, replica_groups=mesh['zl'=4,'core'=2,'y'=4,'x'=4,'zh'=4] {'y','x'}, dimensions={0} | all-to-all | bytes 1900544 | tf_op jit(solution)/shard_map/all_to_all | solution.py:271
  141.7 2.5 %back.1 = bf16[136,512]{1,0:T(8,128)(2,1)S(1)} custom-call(bf16[128,3712]{1,0:T(8,128)(2,1)S(1)} %bitcast.32, bf16[3584,512]{1,0:T(8,128)(2,1)} %all-gather.4.cloned.1.call-done.dec_ref, f32[128,512]{1,0:T(8,128)S(1)} %get-tuple-element.20.slopes_ref, f32[1,512]{1,0:T(1,128)S(1)} %bitcast.34), custom_call_target="tpu_custom_call" | custom-call | flops 469762048 | bytes 4587520 | tf_op jit(solution)/shard_map/back/pallas_call | solution.py:177
  144.2 12.2 %all-gather.1 = bf16[544,512]{1,0:T(8,128)(2,1)S(1)} all-gather(bf16[136,512]{1,0:T(8,128)(2,1)S(1)} %back.1), channel_id=3, replica_groups=mesh['zl'=4,'core'=2,'y'=4,'x'=4,'zh'=4] {'zl'}, dimensions={0}, use_global_device_ids=true | all-gather | bytes 696320 | tf_op jit(solution)/shard_map/all_gather | solution.py:273
  156.4 11.4 %collective-permute-start.6 = (bf16[4,136,512]{2,1,0:T(8,128)(2,1)S(1)}, bf16[4,136,512]{2,1,0:T(8,128)(2,1)S(1)}, u32[]{:S(2)}, u32[]{:S(2)}) collective-permute-start(bf16[4,136,512]{2,1,0:T(8,128)(2,1)S(1)} %bitcast.39), channel_id=1, source_target_pairs={{0,64},{64,0},{1,65},{65,1},{2,66},{66,2},{3,67},{67,3},{4,68},{68... | collective-permute-start | bytes 1671176 | tf_op jit(solution)/shard_map/ppermute | solution.py:52
  170.0 2.5 %subtract_convert_fusion = (bf16[448,512]{1,0:T(8,128)(2,1)}, f32[448,512]{1,0:T(8,128)}, f32[448,512]{1,0:T(8,128)}) fusion(bf16[448,512]{1,0:T(8,128)(2,1)S(1)} %copy-done.5, f32[448,512]{1,0:T(8,128)S(1)} %copy-done.2, f32[448,512]{1,0:T(8,128)S(1)} %copy-done.3, f32[448,512]{1,0:T(8,128)S(1)} %convolution_bitcast_fusion.1, ...), kind=kOutput, calls=%fused_computation.11 | convolution fusion | flops 253231104 | bytes 6520832 | tf_op jit(solution)/shard_map/dot_general | solution.py:278
  (62 shorter events, 7.6 us)
Async XLA Ops:
  7.2 39.4 %copy-start.4 = (bf16[448,512]{1,0:T(8,128)(2,1)S(1)}, bf16[448,512]{1,0:T(8,128)(2,1)}, u32[]{:S(2)}) copy-start(bf16[448,512]{1,0:T(8,128)(2,1)} %param.8) | copy-start | bytes 1376260
  7.2 74.7 %all-gather.4.cloned.1.call-start = ((), (), s32[]{:S(2)}) async-start(), calls=%async_computation.5 | async-start | bytes 4128768 | tf_op jit(solution)/shard_map/all_gather | solution.py:205
  9.3 29.2 %all-to-all-start = ((bf16[8,8,448]{2,1,0:T(8,128)(2,1)}), bf16[8,8,448]{2,1,0:T(8,128)(2,1)S(1)}, u32[]{:S(2)}, u32[]{:S(2)}) async-start(bf16[8,8,448]{2,1,0:T(8,128)(2,1)} %bitcast.1), calls=%async_computation | async-start | bytes 131072 | tf_op jit(solution)/shard_map/all_to_all | solution.py:216
  39.8 21.7 %all-to-all-start.1 = ((bf16[16,4,8,896]{3,2,1,0:T(8,128)(2,1)}), bf16[16,4,8,896]{3,2,1,0:T(8,128)(2,1)S(1)}, u32[]{:S(2)}, u32[]{:S(2)}) async-start(bf16[16,4,8,896]{3,2,1,0:T(8,128)(2,1)} %broadcast_in_dim.25), calls=%async_computation.1 | async-start | bytes 1835008 | tf_op jit(solution)/shard_map/all_to_all | solution.py:48
  46.5 21.4 %copy-start.1 = (f32[448]{0:T(512)S(1)}, f32[448]{0:T(512)}, u32[]{:S(2)}) copy-start(f32[448]{0:T(512)} %param.11) | copy-start | bytes 5380
  46.5 15.0 %collective-permute-start = (bf16[448,512]{1,0:T(8,128)(2,1)S(1)}, bf16[448,512]{1,0:T(8,128)(2,1)S(1)}, u32[]{:S(2)}, u32[]{:S(2)}) collective-permute-start(bf16[448,512]{1,0:T(8,128)(2,1)S(1)} %copy-done.4), channel_id=1, source_target_pairs={{0,64},{64,0},{1,65},{65,1},{2,66},{66,2},{3,67},{67,3},{4,68},{68... | collective-permute-start | bytes 1376264 | tf_op jit(solution)/shard_map/ppermute | solution.py:52
  61.5 20.4 %copy-start = (f32[512]{0:T(512)S(1)}, f32[512]{0:T(512)}, u32[]{:S(2)}) copy-start(f32[512]{0:T(512)} %param.9) | copy-start | bytes 6148
  63.0 18.8 %all-to-all-start.2 = ((bf16[4,128,512]{2,1,0:T(8,128)(2,1)}), bf16[4,128,512]{2,1,0:T(8,128)(2,1)S(1)}, u32[]{:S(2)}, u32[]{:S(2)}) async-start(bf16[4,128,512]{2,1,0:T(8,128)(2,1)} %bitcast.8), calls=%async_computation.2 | async-start | bytes 1048576 | tf_op jit(solution)/shard_map/all_to_all | solution.py:231
  67.9 4.0 %collective-permute-start.1 = (f32[448]{0:T(512)S(1)}, f32[448]{0:T(512)S(1)}, u32[]{:S(2)}, u32[]{:S(2)}) collective-permute-start(f32[448]{0:T(512)S(1)} %copy-done.1), channel_id=1, source_target_pairs={{0,64},{64,0},{1,65},{65,1},{2,66},{66,2},{3,67},{67,3},{4,68},{68... | collective-permute-start | bytes 5384 | tf_op jit(solution)/shard_map/ppermute | solution.py:52
  72.6 52.7 %collective-permute-start.5 = (bf16[512,448]{1,0:T(8,128)(2,1)S(1)}, bf16[512,448]{1,0:T(8,128)(2,1)S(1)}, u32[]{:S(2)}, u32[]{:S(2)}) collective-permute-start(bf16[512,448]{1,0:T(8,128)(2,1)S(1)} %get-tuple-element.28), channel_id=1, source_target_pairs={{0,64},{64,0},{1,65},{65,1},{2,66},{66,2},{3,67},{67,3},{4,68},{68... | collective-permute-start | bytes 1376264 | tf_op jit(solution)/shard_map/ppermute | solution.py:52
  85.9 20.3 %all-to-all-start.3 = ((bf16[16,8,3584]{2,1,0:T(8,128)(2,1)}), bf16[16,8,3584]{2,1,0:T(8,128)(2,1)S(1)}, u32[]{:S(2)}, u32[]{:S(2)}) async-start(bf16[16,8,3584]{2,1,0:T(8,128)(2,1)} %bitcast.11), calls=%async_computation.3 | async-start | bytes 1835008 | tf_op jit(solution)/shard_map/all_to_all | solution.py:263
  91.6 10.2 %collective-permute-start.2 = (bf16[1,24,512]{2,1,0:T(8,128)(2,1)S(1)}, bf16[1,24,512]{2,1,0:T(8,128)(2,1)S(1)}, u32[]{:S(2)}, u32[]{:S(2)}) collective-permute-start(bf16[1,24,512]{2,1,0:T(8,128)(2,1)S(1)} %get-tuple-element.32), channel_id=1, source_target_pairs={{0,384},{128,0},{256,128},{384,256},{1,385},{129,1},{257,129},{385... | collective-permute-start | bytes 73736 | tf_op jit(solution)/shard_map/ppermute | solution.py:249
  94.6 7.3 %collective-permute-start.3 = (bf16[1,24,512]{2,1,0:T(8,128)(2,1)S(1)}, bf16[1,24,512]{2,1,0:T(8,128)(2,1)S(1)}, u32[]{:S(2)}, u32[]{:S(2)}) collective-permute-start(bf16[1,24,512]{2,1,0:T(8,128)(2,1)S(1)} %get-tuple-element.31), channel_id=1, source_target_pairs={{0,256},{128,384},{256,0},{384,128},{1,257},{129,385},{257,1},{385... | collective-permute-start | bytes 73736 | tf_op jit(solution)/shard_map/ppermute | solution.py:249
  96.5 6.7 %collective-permute-start.4 = (bf16[1,24,512]{2,1,0:T(8,128)(2,1)S(1)}, bf16[1,24,512]{2,1,0:T(8,128)(2,1)S(1)}, u32[]{:S(2)}, u32[]{:S(2)}) collective-permute-start(bf16[1,24,512]{2,1,0:T(8,128)(2,1)S(1)} %get-tuple-element.29), channel_id=1, source_target_pairs={{0,128},{128,256},{256,384},{384,0},{1,129},{129,257},{257,385},{3... | collective-permute-start | bytes 73736 | tf_op jit(solution)/shard_map/ppermute | solution.py:249
  141.7 28.3 %copy-start.2 = (f32[448,512]{1,0:T(8,128)S(1)}, f32[448,512]{1,0:T(8,128)}, u32[]{:S(2)}) copy-start(f32[448,512]{1,0:T(8,128)} %param.12) | copy-start | bytes 2752516
  141.7 28.3 %copy-start.3 = (f32[448,512]{1,0:T(8,128)S(1)}, f32[448,512]{1,0:T(8,128)}, u32[]{:S(2)}) copy-start(f32[448,512]{1,0:T(8,128)} %param.13) | copy-start | bytes 2752516
  141.7 28.3 %copy-start.5 = (bf16[448,512]{1,0:T(8,128)(2,1)S(1)}, bf16[448,512]{1,0:T(8,128)(2,1)}, u32[]{:S(2)}) copy-start(bf16[448,512]{1,0:T(8,128)(2,1)} %param.8) | copy-start | bytes 1376260
  156.4 12.9 %collective-permute-start.6 = (bf16[4,136,512]{2,1,0:T(8,128)(2,1)S(1)}, bf16[4,136,512]{2,1,0:T(8,128)(2,1)S(1)}, u32[]{:S(2)}, u32[]{:S(2)}) collective-permute-start(bf16[4,136,512]{2,1,0:T(8,128)(2,1)S(1)} %bitcast.39), channel_id=1, source_target_pairs={{0,64},{64,0},{1,65},{65,1},{2,66},{66,2},{3,67},{67,3},{4,68},{68... | collective-permute-start | bytes 1671176 | tf_op jit(solution)/shard_map/ppermute | solution.py:52
Sparse Core Ops, SparseCore 0:
  10.1 58.1 all-gather.3
